TPU v7x, 32 devices: a whole 2x2x4 slice. The times are simulated.
32 devices in a mesh: tm: 4 (over z), atom: 2 (over x), chan: 4 (over y, core).
Axes of the slice: x: 2, y: 2, z: 4, core: 2. Of those that a mesh axis runs over, the one named last changes fastest.
Arguments:
- signal: bfloat16 [256, 4096], P('chan', 'tm'), may hold values from -6 to 6
- codes_init: float32 [128, 4096], P('atom', 'tm'), may hold values from -4 to 4
- atom_bank: bfloat16 [128, 256, 512], P('atom', 'chan'), may hold values from -0.015625 to 0.015625
- step_size: float32 [128], P('atom'), may hold values from 0.1 to 0.5
- threshold: float32 [128], P('atom'), may hold values from 0.3 to 3
Outputs:
- final_codes: float32 [128, 4096], P('atom', 'tm')
- residual: float32 [256, 4096], P('chan', 'tm')
All inputs are finite; a program needn't handle non-finite values.
Results may differ from a plain program's by a relative error of at most 0.0025.
Values may be sent and summed in bfloat16 or wider, within the bound.
No kernel may reach another device: no remote copies, remote signals or barrier semaphores. Data moves between devices by JAX's collectives and lax.ppermute only.
A program may use at most 64 MiB of HBM per device.

v0:
```python
import jax
import jax.numpy as jnp
from jax import lax
from jax.sharding import PartitionSpec as P

ITERS = 2


def from_behind(value, axis, steps):
    count = lax.axis_size(axis)
    leading, last = (max(0, -steps), min(count, count - steps))
    return lax.ppermute(value, axis, [(source, source + steps) for source in range(leading, last)])


def synthesize(extended, atom_bank):
    atom_rows, chan_rows, taps = atom_bank.shape
    group = min(32, taps)
    turns = taps // group
    length = extended.shape[1] - taps + 1
    weights = (
        atom_bank.reshape(atom_rows, chan_rows, turns, group)
        .transpose(2, 1, 3, 0)
        .reshape(turns, chan_rows, group * atom_rows)
    )

    def synthesize_accumulate(turn_index, total):
        start = taps - group - turn_index * group
        window = lax.dynamic_slice_in_dim(extended, start, length + group - 1, 1)
        stacked = jnp.concatenate(
            [
                window[:, group - 1 - offset : group - 1 - offset + length]
                for offset in range(group)
            ],
            axis=0,
        )
        return total + jnp.dot(weights[turn_index], stacked, preferred_element_type=jnp.float32)

    return lax.fori_loop(
        0, turns, synthesize_accumulate, jnp.zeros((chan_rows, length), jnp.float32)
    )


def correlate(extended, atom_bank):
    atom_rows, chan_rows, taps = atom_bank.shape
    group = min(32, taps)
    turns = taps // group
    length = extended.shape[1] - taps + 1
    weights = (
        atom_bank.reshape(atom_rows, chan_rows, turns, group)
        .transpose(2, 0, 3, 1)
        .reshape(turns, atom_rows, group * chan_rows)
    )

    def correlate_accumulate(turn_index, total):
        start = turn_index * group
        window = lax.dynamic_slice_in_dim(extended, start, length + group - 1, 1)
        stacked = jnp.concatenate(
            [window[:, offset : offset + length] for offset in range(group)], axis=0
        )
        return total + jnp.dot(weights[turn_index], stacked, preferred_element_type=jnp.float32)

    return lax.fori_loop(
        0, turns, correlate_accumulate, jnp.zeros((atom_rows, length), jnp.float32)
    )


def shrink(current, gradient, step_size, threshold):
    moved = current - step_size[:, None] * gradient
    bound = (step_size * threshold)[:, None]
    return moved - jnp.clip(moved, -bound, bound)


def body(signal, codes_init, atom_bank, step_size, threshold):
    taps = atom_bank.shape[2]
    slab = signal.shape[1]
    current = codes_init
    misfit = None
    for sweep_index in range(ITERS):
        lowered = current.astype(jnp.bfloat16)
        earlier = from_behind(lowered[:, slab - taps + 1 :], "tm", 1)
        partial_recon = synthesize(jnp.concatenate([earlier, lowered], axis=1), atom_bank)
        recon = lax.psum(partial_recon, "atom")
        misfit = recon - signal.astype(jnp.float32)
        rounded = misfit.astype(jnp.bfloat16)
        following = from_behind(rounded[:, : taps - 1], "tm", -1)
        partial_grad = correlate(jnp.concatenate([rounded, following], axis=1), atom_bank)
        gradient = lax.psum(partial_grad, "chan")
        current = shrink(current, gradient, step_size, threshold)
    return (current, misfit)


def solution(mesh):
    placed = (P("chan", "tm"), P("atom", "tm"), P("atom", "chan", None), P("atom"), P("atom"))
    return jax.shard_map(
        body,
        mesh=mesh,
        in_specs=placed,
        out_specs=(P("atom", "tm"), P("chan", "tm")),
        check_vma=False,
    )
```

profile of v0, /device:TPU:0, one launch (start us, length us, event | category | flops | bytes accessed | tf_op | source)
XLA Modules:
  0.0 1967.1 jit_solution(9950875553228892732)
XLA Ops:
  8.3 4.9 collective-permute-start
  13.2 8.4 copy.12
  21.7 16.4 copy.13
  38.0 12.3 reshape.24
  50.5 438.3 %while.60 = (s32[]{:T(128)}, f32[64,1024]{1,0:T(8,128)S(1)}, bf16[16,64,2048]{2,1,0:T(8,128)(2,1)}, bf16[64,1535]{1,0:T(8,128)(2,1)S(1)}, s32[]{:T(128)}, /*inde...) while((s32[]{:T(128)}, f32[64,1024]{1,0:T(8,128)S(1)}, ...), condition=%wide.region_1.0_spmd.clone, body=%wide.region_0.0_spmd.clone.sunk | while | flops 268566560 | bytes 13370765 | solution.py:38
  102.1 3.2 convolution_add_fusion.8
  129.5 3.2 convolution_add_fusion.8
  184.3 3.2 convolution_add_fusion.8
  211.6 3.2 convolution_add_fusion.8
  266.4 3.2 convolution_add_fusion.8
  293.8 3.2 convolution_add_fusion.8
  348.6 3.2 convolution_add_fusion.8
  376.0 3.2 convolution_add_fusion.8
  430.8 3.2 convolution_add_fusion.8
  458.2 3.2 convolution_add_fusion.8
  489.5 23.5 %all-reduce.5.cloned.1.call-done = f32[64,1024]{1,0:T(8,128)} async-done(((f32[64,1024]{1,0:T(8,128)}), f32[64,1024]{1,0:T(8,128)}) %all-reduce.5.cloned.1.call-update) | async-done | bytes 262160 | tf_op jit(solution)/shard_map/psum | solution.py:82
  515.6 12.3 reshape.23
  527.9 6.4 copy.14
  534.4 439.6 %while.61 = (s32[]{:T(128)}, f32[64,1024]{1,0:T(8,128)S(1)}, bf16[16,64,2048]{2,1,0:T(8,128)(2,1)}, bf16[64,1535]{1,0:T(8,128)(2,1)S(1)}, s32[]{:T(128)}, /*inde...) while((s32[]{:T(128)}, f32[64,1024]{1,0:T(8,128)S(1)}, ...), condition=%wide.region_4.0_spmd.clone, body=%wide.region_3.0_spmd.clone.sunk | while | flops 268566560 | bytes 13370745 | solution.py:62
  558.7 3.2 convolution_add_fusion.9
  586.2 3.2 convolution_add_fusion.9
  613.7 3.2 convolution_add_fusion.9
  641.1 3.2 convolution_add_fusion.9
  668.6 3.2 convolution_add_fusion.9
  696.1 3.2 convolution_add_fusion.9
  723.6 3.2 convolution_add_fusion.9
  751.0 3.2 convolution_add_fusion.9
  778.5 3.2 convolution_add_fusion.9
  806.0 3.2 convolution_add_fusion.9
  833.5 3.2 convolution_add_fusion.9
  861.0 3.2 convolution_add_fusion.9
  888.4 3.2 convolution_add_fusion.9
  915.9 3.2 convolution_add_fusion.9
  943.4 3.2 convolution_add_fusion.9
  970.9 3.2 convolution_add_fusion.9
  974.9 33.2 %all-reduce.7.cloned.1.call-done = f32[64,1024]{1,0:T(8,128)} async-done(((f32[64,1024]{1,0:T(8,128)}), f32[64,1024]{1,0:T(8,128)}) %all-reduce.7.cloned.1.call-update) | async-done | bytes 262160 | tf_op jit(solution)/shard_map/psum | solution.py:87
  1009.2 3.4 collective-permute-start.2
  1014.6 439.6 %while.62 = (s32[]{:T(128)}, f32[64,1024]{1,0:T(8,128)S(1)}, bf16[16,64,2048]{2,1,0:T(8,128)(2,1)}, bf16[64,1535]{1,0:T(8,128)(2,1)S(1)}, s32[]{:T(128)}, /*inde...) while((s32[]{:T(128)}, f32[64,1024]{1,0:T(8,128)S(1)}, ...), condition=%wide.region_7.8_spmd.clone, body=%wide.region_6.7_spmd.clone.sunk | while | flops 268566560 | bytes 13370765 | solution.py:38
  1038.9 3.2 convolution_add_fusion.10
  1093.9 3.2 convolution_add_fusion.10
  1455.1 24.2 %all-reduce.9.cloned.1.call-done = f32[64,1024]{1,0:T(8,128)} async-done(((f32[64,1024]{1,0:T(8,128)}), f32[64,1024]{1,0:T(8,128)}) %all-reduce.9.cloned.1.call-update) | async-done | bytes 262160 | tf_op jit(solution)/shard_map/psum | solution.py:82
  1482.5 4.6 collective-permute-done.3
  1487.1 439.6 %while.63 = (s32[]{:T(128)}, f32[64,1024]{1,0:T(8,128)S(1)}, bf16[16,64,2048]{2,1,0:T(8,128)(2,1)}, bf16[64,1535]{1,0:T(8,128)(2,1)S(1)}, s32[]{:T(128)}, /*inde...) while((s32[]{:T(128)}, f32[64,1024]{1,0:T(8,128)S(1)}, ...), condition=%wide.region_10.11_spmd.clone, body=%wide.region_9.10_spmd.clone.sunk | while | flops 268566560 | bytes 13370745 | solution.py:62
  1566.4 3.2 convolution_add_fusion.11
  1648.8 3.2 convolution_add_fusion.11
  1758.7 3.2 convolution_add_fusion.11
  1868.6 3.2 convolution_add_fusion.11
  1927.5 31.2 %all-reduce.11.cloned.1.call-done = f32[64,1024]{1,0:T(8,128)} async-done(((f32[64,1024]{1,0:T(8,128)}), f32[64,1024]{1,0:T(8,128)}) %all-reduce.11.cloned.1.call-update) | async-done | bytes 262160 | tf_op jit(solution)/shard_map/psum | solution.py:87
  (2129 shorter events, 1667.6 us)
Async XLA Ops:
  7.2 505.9 %all-reduce.5.cloned.1.call-start = ((), (), s32[]{:S(2)}) async-start(), calls=%async_computation | async-start | bytes 524288 | tf_op jit(solution)/shard_map/psum | solution.py:82
  8.3 42.1 %collective-permute-start = (bf16[64,511]{1,0:T(8,128)(2,1)S(1)}, bf16[64,511]{1,0:T(8,128)(2,1)S(1)}, u32[]{:S(2)}, u32[]{:S(2)}) collective-permute-start(bf16[64,511]{1,0:T(8,128)(2,1)S(1)} %slice.1232), channel_id=1, source_target_pairs={{0,8},{8,16},{16,24},{1,9},{9,17},{17,25},{2,10},{10,18},{18,26},{... | collective-permute-start | bytes 196232 | tf_op jit(solution)/shard_map/ppermute | solution.py:12
  50.5 462.6 %copy-start.6 = (bf16[64,1024]{1,0:T(8,128)(2,1)S(1)}, bf16[64,1024]{1,0:T(8,128)(2,1)}, u32[]{:S(2)}) copy-start(bf16[64,1024]{1,0:T(8,128)(2,1)} %param.13) | copy-start | bytes 393220
  488.7 0.7 copy-start
  489.5 518.6 %all-reduce.7.cloned.1.call-start = ((), (), s32[]{:S(2)}) async-start(), calls=%async_computation.1 | async-start | bytes 524288 | tf_op jit(solution)/shard_map/psum | solution.py:87
  514.1 20.3 %collective-permute-start.1 = (bf16[64,511]{1,0:T(8,128)(2,1)S(1)}, bf16[64,511]{1,0:T(8,128)(2,1)S(1)}, u32[]{:S(2)}, u32[]{:S(2)}) collective-permute-start(bf16[64,511]{1,0:T(8,128)(2,1)S(1)} %slice.1233), channel_id=1, source_target_pairs={{8,0},{16,8},{24,16},{9,1},{17,9},{25,17},{10,2},{18,10},{26,18},{... | collective-permute-start | bytes 196232 | tf_op jit(solution)/shard_map/ppermute | solution.py:12
  534.4 440.5 %copy-start.7 = (f32[64]{0:T(128)S(1)}, f32[64]{0:T(128)}, u32[]{:S(2)}) copy-start(f32[64]{0:T(128)} %param.16) | copy-start | bytes 772
  534.4 440.5 %copy-start.8 = (f32[64]{0:T(128)S(1)}, f32[64]{0:T(128)}, u32[]{:S(2)}) copy-start(f32[64]{0:T(128)} %param.17) | copy-start | bytes 772
  534.4 473.7 %copy-start.4 = (f32[64,1024]{1,0:T(8,128)S(1)}, f32[64,1024]{1,0:T(8,128)}, u32[]{:S(2)}) copy-start(f32[64,1024]{1,0:T(8,128)} %param.14) | copy-start | bytes 786436
  974.1 0.7 copy-start.1
  974.8 504.5 %all-reduce.9.cloned.1.call-start = ((), (), s32[]{:S(2)}) async-start(), calls=%async_computation.2 | async-start | bytes 524288 | tf_op jit(solution)/shard_map/psum | solution.py:82
  1009.2 5.3 collective-permute-start.2
  1454.3 0.7 copy-start.2
  1455.0 503.7 %all-reduce.11.cloned.1.call-start = ((), (), s32[]{:S(2)}) async-start(), calls=%async_computation.3 | async-start | bytes 524288 | tf_op jit(solution)/shard_map/psum | solution.py:87
  1480.9 6.1 collective-permute-start.3
  1487.1 471.6 %copy-start.5 = (f32[64,1024]{1,0:T(8,128)S(1)}, f32[64,1024]{1,0:T(8,128)}, u32[]{:S(2)}) copy-start(f32[64,1024]{1,0:T(8,128)} %all-reduce.7.cloned.1.call-done) | copy-start | bytes 786436
  1926.8 0.7 copy-start.3
Sparse Core Ops, SparseCore 0:
  489.6 23.4 all-reduce.4
  974.9 33.1 all-reduce.6
  1455.1 24.0 all-reduce.8
  1927.6 31.0 all-reduce.10
where the time goes:
time: 1970 us
  local copies, waits for them, and re-layouts  1610 us (82%)
  matrix products  203 us (10%)
  waiting for transfers between devices  119 us (6%)
    while x1984, local copies, waits for them, and re-layouts  1500 us
    dot_general x32, matrix products, correlate_accumulate(): jnp.dot(weights[turn_index], stacked, preferred_element_type=jnp.float32)  102 us
    dot_general x32, matrix products, synthesize_accumulate(): jnp.dot(weights[turn_index], stacked, preferred_element_type=jnp.float32)  101 us
    psum x2, waiting for transfers between devices, body(): gradient = lax.psum(partial_grad, 'chan')  64.4 us
    psum x2, waiting for transfers between devices, body(): recon = lax.psum(partial_recon, 'atom')  47.7 us
  transfers between devices with their start and end apart: 8, of which 6 were waited for; matrix products, arithmetic and copies ran while one was open for 3% of the time, Pallas kernels for 0%

commit v1 on v0

v1 whole, which is shorter than its diff:
```python
import functools

import jax
import jax.numpy as jnp
from jax import lax
from jax.experimental import pallas as pl
from jax.experimental.pallas import tpu as pltpu
from jax.sharding import PartitionSpec as P

ITERS = 2
PHASES = 4
RUN = 16
GROUP = 8
LANES = 128
VMEM = 56 * 1024 * 1024


def to_blocks(value):
    rows, slab = value.shape
    parts = slab // (RUN * PHASES)
    return (
        value.reshape(rows, parts, RUN, PHASES)
        .transpose(2, 1, 3, 0)
        .reshape(RUN, parts, PHASES * rows)
    )


def from_blocks(value):
    run, parts, width = value.shape
    rows = width // PHASES
    return (
        value.reshape(run, parts, PHASES, rows)
        .transpose(3, 1, 0, 2)
        .reshape(rows, parts * run * PHASES)
    )


def bank_kernel(taps, rows, bank_ref, even_ref, odd_ref, flat):
    atoms, chans, _ = bank_ref.shape
    tiles = even_ref.shape[0]
    margin = 8
    step = min(256, taps)
    eye = (
        lax.broadcasted_iota(jnp.int32, (step, step), 0)
        == lax.broadcasted_iota(jnp.int32, (step, step), 1)
    ).astype(jnp.bfloat16)
    zeros = jnp.zeros((margin, LANES), jnp.float32)

    def turn(pair, carry):
        first = bank_ref[2 * pair]
        second = bank_ref[2 * pair + 1]
        doubled = jnp.concatenate([first, first, second, second], axis=0)
        for which in range(2):
            base = pl.multiple_of((2 * pair + which) * rows, 8)
            flat[pl.ds(base, margin), :] = zeros
            flat[pl.ds(base + margin + taps, margin), :] = zeros
        for part in range(taps // step):
            turned = lax.dot_general(
                eye,
                doubled[:, part * step : (part + 1) * step],
                (((1,), (1,)), ((), ())),
                preferred_element_type=jnp.float32,
            )
            for which in range(2):
                base = pl.multiple_of((2 * pair + which) * rows + margin + part * step, 8)
                flat[pl.ds(base, step), :] = turned[:, which * LANES : (which + 1) * LANES]
        return carry

    lax.fori_loop(0, atoms // 2, turn, 0)

    low = lax.broadcasted_iota(jnp.int32, (atoms, LANES), 1) < chans

    def tap(index):
        return flat[pl.ds(index + margin, atoms, stride=rows), :]

    def merge(turn_index, carry):
        for inner in range(4):
            tile = turn_index * 4 + inner
            middle = tap(2 * tile - 3)
            later = tap(2 * tile - 2)
            even_ref[tile] = jnp.where(low, carry, middle).astype(jnp.bfloat16)
            odd_ref[tile] = jnp.where(low, middle, later).astype(jnp.bfloat16)
            carry = later
        return carry

    lax.fori_loop(0, tiles // 4, merge, tap(-4))


def bank_tiles(atom_bank):
    atoms, chans, taps = atom_bank.shape
    tiles = taps // 2 + 4
    rows = taps + 16
    block = 16
    shape = jax.ShapeDtypeStruct((tiles, atoms, LANES), jnp.bfloat16)
    spec = pl.BlockSpec((tiles, block, LANES), lambda i: (0, i, 0))
    return pl.pallas_call(
        functools.partial(bank_kernel, taps, rows),
        grid=(atoms // block,),
        in_specs=[pl.BlockSpec((block, chans, taps), lambda i: (i, 0, 0))],
        out_specs=[spec, spec],
        out_shape=[shape, shape],
        scratch_shapes=[pltpu.VMEM((block * rows, LANES), jnp.float32)],
        compiler_params=pltpu.CompilerParams(vmem_limit_bytes=VMEM),
        name="bank_tiles",
    )(atom_bank)


def conv_kernel(transposed, steps, own_ref, halo_ref, even_hbm, odd_hbm, out_ref, even, odd, base, spread, total, sems):
    run, parts, width = own_ref.shape
    halo = halo_ref.shape[1]
    chunks = sems.shape[1]
    tiles = even.shape[0]
    size = tiles // chunks

    def copies(chunk):
        span = pl.ds(chunk * size, size)
        return [
            pltpu.make_async_copy(even_hbm.at[span], even.at[span], sems.at[0, chunk]),
            pltpu.make_async_copy(odd_hbm.at[span], odd.at[span], sems.at[1, chunk]),
        ]

    for chunk in range(chunks):
        for copy in copies(chunk):
            copy.start()

    own = own_ref[...].astype(jnp.float32)
    beside = halo_ref[...].astype(jnp.float32)
    if transposed:
        base[:, :parts] = own
        base[:, parts:] = beside
    else:
        base[:, :halo] = beside
        base[:, halo:] = own
    for shift in range(halo + 1):
        spread[shift * run : (shift + 1) * run] = base[:, shift : shift + parts].astype(jnp.bfloat16)

    total[...] = jnp.zeros_like(total)

    def block(step):
        def pair(ref, start):
            return jnp.concatenate([ref[start], ref[start + 1]], axis=1)

        return jnp.concatenate(
            [
                pair(even, 2 * step + 2),
                pair(odd, 2 * step + 1),
                pair(even, 2 * step + 1),
                pair(odd, 2 * step),
            ],
            axis=0,
        )

    def rows(step):
        start = step if transposed else halo * run - step
        return spread[pl.ds(start, run)].reshape(run * parts, width)

    def add(first, count):
        left = jnp.concatenate([rows(first + i) for i in range(count)], axis=1)
        if transposed:
            right = jnp.concatenate([block(first + i) for i in range(count)], axis=1)
            dims = (((1,), (1,)), ((), ()))
        else:
            right = jnp.concatenate([block(first + i) for i in range(count)], axis=0)
            dims = (((1,), (0,)), ((), ()))
        total[...] += lax.dot_general(left, right, dims, preferred_element_type=jnp.float32)

    turns = steps // GROUP
    share = -(-turns // chunks)
    for chunk in range(chunks):
        for copy in copies(chunk):
            copy.wait()
        low = min(chunk * share, turns)
        high = min((chunk + 1) * share, turns)
        high = high if chunk == chunks - 1 else min(high, ((chunk + 1) * size - 4) // 2 // GROUP)
        low = low if chunk == 0 else min(low, (chunk * size - 4) // 2 // GROUP)

        def loop(turn_index, carry):
            add(turn_index * GROUP, GROUP)
            return carry

        lax.fori_loop(low, high, loop, 0)
    add(turns * GROUP, steps - turns * GROUP)
    out_ref[...] = total[...].reshape(out_ref.shape)


def convolve(own, halo, even, odd, transposed):
    run, parts, width = own.shape
    beside = halo.shape[1]
    tiles, atoms, _ = even.shape
    steps = (tiles - 4) // 2 + 1
    chunks = 4
    out_width = 2 * LANES if not transposed else PHASES * atoms
    flops = 2 * run * parts * width * out_width * steps
    return pl.pallas_call(
        functools.partial(conv_kernel, transposed, steps),
        in_specs=[
            pl.BlockSpec(memory_space=pltpu.VMEM),
            pl.BlockSpec(memory_space=pltpu.VMEM),
            pl.BlockSpec(memory_space=pl.ANY),
            pl.BlockSpec(memory_space=pl.ANY),
        ],
        out_specs=pl.BlockSpec(memory_space=pltpu.VMEM),
        out_shape=jax.ShapeDtypeStruct((run, parts, out_width), jnp.float32),
        scratch_shapes=[
            pltpu.VMEM(even.shape, jnp.bfloat16),
            pltpu.VMEM(odd.shape, jnp.bfloat16),
            pltpu.VMEM((run, parts + beside, width), jnp.float32),
            pltpu.VMEM(((beside + 1) * run, parts, width), jnp.bfloat16),
            pltpu.VMEM((run * parts, out_width), jnp.float32),
            pltpu.SemaphoreType.DMA((2, chunks)),
        ],
        compiler_params=pltpu.CompilerParams(vmem_limit_bytes=VMEM),
        cost_estimate=pl.CostEstimate(
            flops=flops, bytes_accessed=even.size * 4 + own.size * 8, transcendentals=0
        ),
        name="correlate" if transposed else "synthesize",
    )(own, halo, even, odd)


def shifted(value, axis, steps):
    count = lax.axis_size(axis)
    first, last = max(0, -steps), min(count, count - steps)
    return lax.ppermute(value, axis, [(i, i + steps) for i in range(first, last)])


def summed(value, axis):
    count = lax.axis_size(axis)
    step = 1
    while step < count:
        value = value + lax.ppermute(value, axis, [(i, i ^ step) for i in range(count)])
        step *= 2
    return value


def body(signal, codes_init, atom_bank, step_size, threshold):
    atoms, chans, taps = atom_bank.shape
    held = LANES // 2
    if chans < held:
        atom_bank = jnp.pad(atom_bank, ((0, 0), (0, held - chans), (0, 0)))
        signal = jnp.pad(signal, ((0, held - chans), (0, 0)))
    even, odd = bank_tiles(atom_bank)
    beside = taps // (RUN * PHASES)
    recorded = to_blocks(signal)
    current = to_blocks(codes_init)
    step = jnp.tile(step_size, PHASES)
    bound = jnp.tile(step_size * threshold, PHASES)
    for _ in range(ITERS):
        lowered = current.astype(jnp.bfloat16)
        earlier = shifted(lowered[:, -beside:], "tm", 1)
        recon = summed(convolve(lowered, earlier, even, odd, False), "atom")
        misfit = recon - recorded.astype(jnp.float32)
        rounded = misfit.astype(jnp.bfloat16)
        following = shifted(rounded[:, :beside], "tm", -1)
        gradient = summed(convolve(rounded, following, even, odd, True), "chan")
        moved = current - step * gradient
        current = moved - jnp.clip(moved, -bound, bound)
    return from_blocks(current), from_blocks(misfit)[:chans]


def solution(mesh):
    placed = (P("chan", "tm"), P("atom", "tm"), P("atom", "chan", None), P("atom"), P("atom"))
    return jax.shard_map(
        body,
        mesh=mesh,
        in_specs=placed,
        out_specs=(P("atom", "tm"), P("chan", "tm")),
        check_vma=False,
    )
```

time: 1970 us -> 130 us (0.07)
  local copies, waits for them, and re-layouts: 1610 us -> 7.35 us
  matrix products: 203 us -> 0 us
  waiting for transfers between devices: 119 us -> 38.7 us
  Pallas kernels: 0 us -> 60.5 us
    while x1984 -> x0, local copies, waits for them, and re-layouts: 1500 us -> none
    dot_general x64 -> x0, matrix products: 203 us -> none  [the longest x32 102 us: correlate_accumulate(): jnp.dot(weights[turn_index], stacked, preferred_element_type=jnp.float32)]
    psum x4 -> x0, waiting for transfers between devices: 112 us -> none  [the longest x2 64.4 us: body(): gradient = lax.psum(partial_grad, 'chan')]
    pallas_call x0 -> x5, Pallas kernels: none -> 60.5 us  [the longest x4 43.3 us: convolve(): pl.pallas_call(functools.partial(conv_kernel, transposed, steps), in_spec...]
    concatenate x64 -> x0, local copies, waits for them, and re-layouts: 48.6 us -> none  [the longest x32 24.3 us: synthesize_accumulate(): jnp.concatenate([window[:, group - 1 - offset:group - 1 - offset + length...]
    ppermute x4 -> x10, waiting for transfers between devices: 6.51 us -> 38.7 us  [the longest x6 27 us: summed(): lax.ppermute(value, axis, [(i, i ^ step) for i in range(count)])]
    reshape x2 -> x6, local copies, waits for them, and re-layouts: 24.7 us -> 1.21 us  [the longest x4 0.72 us: from_blocks(): value.reshape(run, parts, PHASES, rows).transpose(3, 1, 0, 2)]
  transfers between devices with their start and end apart: 8 -> 10, of which waited for: 6 -> 9; matrix products, arithmetic and copies ran while one was open for 3% -> 1% of each run, Pallas kernels for 0% -> 13%
where the time goes in v1:
time: 130 us
  Pallas kernels  60.5 us (47%)
  waiting for transfers between devices  38.7 us (30%)
  starting transfers between devices  17.5 us (13%)
  local copies, waits for them, and re-layouts  7.35 us (6%)
  other arithmetic  4.67 us (4%)
    pallas_call x4, Pallas kernels, convolve(): pl.pallas_call(functools.partial(conv_kernel, transposed, steps), in_spec...  43.3 us
    ppermute x6, waiting for transfers between devices, summed(): lax.ppermute(value, axis, [(i, i ^ step) for i in range(count)])  27 us
    pallas_call x1, Pallas kernels, bank_tiles(): pl.pallas_call(functools.partial(bank_kernel, taps, rows), grid=(atoms //...  17.3 us
    ppermute x4, waiting for transfers between devices, shifted(): lax.ppermute(value, axis, [(i, i + steps) for i in range(first, last)])  11.7 us
    ppermute x4, starting transfers between devices, shifted(): lax.ppermute(value, axis, [(i, i + steps) for i in range(first, last)])  11.1 us
    ppermute x6, starting transfers between devices, summed(): lax.ppermute(value, axis, [(i, i ^ step) for i in range(count)])  6.42 us
    unnamed x26, local copies, waits for them, and re-layouts  5.6 us
  transfers between devices with their start and end apart: 10, of which 9 were waited for; matrix products, arithmetic and copies ran while one was open for 1% of the time, Pallas kernels for 13%

profile of v1, /device:TPU:0, one launch (start us, length us, event | category | flops | bytes accessed | tf_op | source)
XLA Modules:
  0.0 129.7 jit_solution(10450012911859239873)
XLA Ops:
  0.6 1.1 copy.11
  1.8 0.3 reshape.46
  2.1 0.1 copy.30.own_ref
  2.3 0.0 copy-start.1
  2.3 4.9 %collective-permute-start = (bf16[16,8,256]{2,1,0:T(8,128)(2,1)S(1)}, bf16[16,8,256]{2,1,0:T(8,128)(2,1)S(1)}, u32[]{:S(2)}, u32[]{:S(2)}) collective-permute-start(bf16[16,8,256]{2,1,0:T(8,128)(2,1)S(1)} %slice.16), channel_id=1, source_target_pairs={{0,8},{8,16},{16,24},{1,9},{9,17},{17,25},{2,10},{10,18},{18,26},{... | collective-permute-start | bytes 196616 | tf_op jit(solution)/shard_map/ppermute | solution.py:223
  7.2 17.3 %bank_tiles.1 = (bf16[260,64,128]{2,1,0:T(8,128)(2,1)}, bf16[260,64,128]{2,1,0:T(8,128)(2,1)}) custom-call(bf16[64,64,512]{2,1,0:T(8,128)(2,1)} %bank_ref.1), custom_call_target="tpu_custom_call" | custom-call | tf_op jit(solution)/shard_map/bank_tiles/pallas_call | solution.py:96
  24.6 0.6 copy-done.6
  25.2 10.7 %synthesize.2 = f32[16,16,256]{2,1,0:T(8,128)} custom-call(bf16[16,16,256]{2,1,0:T(8,128)(2,1)} %copy-done.1, bf16[16,8,256]{2,1,0:T(8,128)(2,1)} %copy-done.6, bf16[260,64,128]{2,1,0:T(8,128)(2,1)} %get-tuple-element.4.even_hbm, bf16[260,64,128]{2,1,0:T(8,128)(2,1)} %get-tuple-element.5.odd_hbm), custom_call_target="tpu_custom_call" | custom-call | flops 4328521728 | bytes 9043968 | tf_op jit(solution)/shard_map/synthesize/pallas_call | solution.py:194
  35.9 1.6 %collective-permute-start.1 = (f32[16,16,256]{2,1,0:T(8,128)}, f32[16,16,256]{2,1,0:T(8,128)S(1)}, u32[]{:S(2)}, u32[]{:S(2)}) collective-permute-start(f32[16,16,256]{2,1,0:T(8,128)} %synthesize.2), channel_id=1, source_target_pairs={{0,4},{4,0},{1,5},{5,1},{2,6},{6,2},{3,7},{7,3},{8,12},{12,8},{9,1... | collective-permute-start | bytes 786440 | tf_op jit(solution)/shard_map/ppermute | solution.py:230
  37.4 0.1 copy.21
  37.5 0.3 reshape.47
  37.9 6.0 %collective-permute-done.1 = f32[16,16,256]{2,1,0:T(8,128)S(1)} collective-permute-done((f32[16,16,256]{2,1,0:T(8,128)}, f32[16,16,256]{2,1,0:T(8,128)S(1)}, u32[]{:S(2)}, u32[]{:S(2)}) %collective-permute-start.1) | collective-permute-done | bytes 262176 | tf_op jit(solution)/shard_map/ppermute | solution.py:230
  43.9 1.1 subtract_convert_fusion.own_ref
  45.0 1.4 %collective-permute-start.2 = (bf16[16,8,256]{2,1,0:T(8,128)(2,1)S(1)}, bf16[16,8,256]{2,1,0:T(8,128)(2,1)S(1)}, u32[]{:S(2)}, u32[]{:S(2)}) collective-permute-start(bf16[16,8,256]{2,1,0:T(8,128)(2,1)S(1)} %slice.17), channel_id=1, source_target_pairs={{8,0},{16,8},{24,16},{9,1},{17,9},{25,17},{10,2},{18,10},{26,18},{... | collective-permute-start | bytes 196616 | tf_op jit(solution)/shard_map/ppermute | solution.py:223
  46.5 4.9 %collective-permute-done.2.halo_ref = bf16[16,8,256]{2,1,0:T(8,128)(2,1)S(1)} collective-permute-done((bf16[16,8,256]{2,1,0:T(8,128)(2,1)S(1)}, bf16[16,8,256]{2,1,0:T(8,128)(2,1)S(1)}, u32[]{:S(2)}, u32[]{:S(2)}) %collective-permute-start.2) | collective-permute-done | bytes 65568 | tf_op jit(solution)/shard_map/ppermute | solution.py:223
  51.3 0.6 copy-done.8
  52.0 11.0 %correlate.2 = f32[16,16,256]{2,1,0:T(8,128)} custom-call(bf16[16,16,256]{2,1,0:T(8,128)(2,1)} %copy-done.2, bf16[16,8,256]{2,1,0:T(8,128)(2,1)} %copy-done.8, bf16[260,64,128]{2,1,0:T(8,128)(2,1)} %get-tuple-element.4.even_hbm, bf16[260,64,128]{2,1,0:T(8,128)(2,1)} %get-tuple-element.5.odd_hbm), custom_call_target="tpu_custom_call" | custom-call | flops 4328521728 | bytes 9043968 | tf_op jit(solution)/shard_map/correlate/pallas_call | solution.py:194
  62.9 0.1 collective-permute-start.3
  63.0 1.7 %collective-permute-done.3 = f32[16,16,256]{2,1,0:T(8,128)S(1)} collective-permute-done((f32[16,16,256]{2,1,0:T(8,128)}, f32[16,16,256]{2,1,0:T(8,128)S(1)}, u32[]{:S(2)}, u32[]{:S(2)}) %collective-permute-start.3) | collective-permute-done | bytes 262176 | tf_op jit(solution)/shard_map/ppermute | solution.py:230
  64.8 1.0 add.19
  65.8 1.6 %collective-permute-start.4 = (f32[16,16,256]{2,1,0:T(8,128)S(1)}, f32[16,16,256]{2,1,0:T(8,128)S(1)}, u32[]{:S(2)}, u32[]{:S(2)}) collective-permute-start(f32[16,16,256]{2,1,0:T(8,128)S(1)} %add.19), channel_id=1, source_target_pairs={{0,2},{1,3},{2,0},{3,1},{4,6},{5,7},{6,4},{7,5},{8,10},{9,11},{10,... | collective-permute-start | bytes 786440 | tf_op jit(solution)/shard_map/ppermute | solution.py:230
  67.4 0.1 min.20
  67.5 0.1 mul.19
  67.5 6.6 %collective-permute-done.4 = f32[16,16,256]{2,1,0:T(8,128)S(1)} collective-permute-done((f32[16,16,256]{2,1,0:T(8,128)S(1)}, f32[16,16,256]{2,1,0:T(8,128)S(1)}, u32[]{:S(2)}, u32[]{:S(2)}) %collective-permute-start.4) | collective-permute-done | bytes 262176 | tf_op jit(solution)/shard_map/ppermute | solution.py:230
  74.2 0.2 fusion.own_ref
  74.4 3.5 %collective-permute-start.5 = (bf16[16,8,256]{2,1,0:T(8,128)(2,1)S(1)}, bf16[16,8,256]{2,1,0:T(8,128)(2,1)S(1)}, u32[]{:S(2)}, u32[]{:S(2)}) collective-permute-start(bf16[16,8,256]{2,1,0:T(8,128)(2,1)S(1)} %slice.18), channel_id=1, source_target_pairs={{0,8},{8,16},{16,24},{1,9},{9,17},{17,25},{2,10},{10,18},{18,26},{... | collective-permute-start | bytes 196616 | tf_op jit(solution)/shard_map/ppermute | solution.py:223
  77.9 1.9 %collective-permute-done.5.halo_ref = bf16[16,8,256]{2,1,0:T(8,128)(2,1)S(1)} collective-permute-done((bf16[16,8,256]{2,1,0:T(8,128)(2,1)S(1)}, bf16[16,8,256]{2,1,0:T(8,128)(2,1)S(1)}, u32[]{:S(2)}, u32[]{:S(2)}) %collective-permute-start.5) | collective-permute-done | bytes 65568 | tf_op jit(solution)/shard_map/ppermute | solution.py:223
  79.8 0.6 copy-done.9
  80.4 10.6 %synthesize.3 = f32[16,16,256]{2,1,0:T(8,128)} custom-call(bf16[16,16,256]{2,1,0:T(8,128)(2,1)} %copy-done.3, bf16[16,8,256]{2,1,0:T(8,128)(2,1)} %copy-done.9, bf16[260,64,128]{2,1,0:T(8,128)(2,1)} %get-tuple-element.4.even_hbm, bf16[260,64,128]{2,1,0:T(8,128)(2,1)} %get-tuple-element.5.odd_hbm), custom_call_target="tpu_custom_call" | custom-call | flops 4328521728 | bytes 9043968 | tf_op jit(solution)/shard_map/synthesize/pallas_call | solution.py:194
  91.0 1.5 %collective-permute-start.6 = (f32[16,16,256]{2,1,0:T(8,128)}, f32[16,16,256]{2,1,0:T(8,128)S(1)}, u32[]{:S(2)}, u32[]{:S(2)}) collective-permute-start(f32[16,16,256]{2,1,0:T(8,128)} %synthesize.3), channel_id=1, source_target_pairs={{0,4},{4,0},{1,5},{5,1},{2,6},{6,2},{3,7},{7,3},{8,12},{12,8},{9,1... | collective-permute-start | bytes 786440 | tf_op jit(solution)/shard_map/ppermute | solution.py:230
  92.6 5.4 %collective-permute-done.6 = f32[16,16,256]{2,1,0:T(8,128)S(1)} collective-permute-done((f32[16,16,256]{2,1,0:T(8,128)}, f32[16,16,256]{2,1,0:T(8,128)S(1)}, u32[]{:S(2)}, u32[]{:S(2)}) %collective-permute-start.6) | collective-permute-done | bytes 262176 | tf_op jit(solution)/shard_map/ppermute | solution.py:230
  98.0 1.1 fusion.1
  99.1 1.3 collective-permute-start.7
  100.4 4.9 %collective-permute-done.7.halo_ref = bf16[16,8,256]{2,1,0:T(8,128)(2,1)S(1)} collective-permute-done((bf16[16,8,256]{2,1,0:T(8,128)(2,1)S(1)}, bf16[16,8,256]{2,1,0:T(8,128)(2,1)S(1)}, u32[]{:S(2)}, u32[]{:S(2)}) %collective-permute-start.7) | collective-permute-done | bytes 65568 | tf_op jit(solution)/shard_map/ppermute | solution.py:223
  105.4 0.6 copy-done.7
  106.0 11.0 %correlate.3 = f32[16,16,256]{2,1,0:T(8,128)} custom-call(bf16[16,16,256]{2,1,0:T(8,128)(2,1)} %copy-done, bf16[16,8,256]{2,1,0:T(8,128)(2,1)} %copy-done.7, bf16[260,64,128]{2,1,0:T(8,128)(2,1)} %get-tuple-element.4.even_hbm, bf16[260,64,128]{2,1,0:T(8,128)(2,1)} %get-tuple-element.5.odd_hbm), custom_call_target="tpu_custom_call" | custom-call | flops 4328521728 | bytes 9043968 | tf_op jit(solution)/shard_map/correlate/pallas_call | solution.py:194
  117.0 0.1 collective-permute-start.8
  117.0 1.7 %collective-permute-done.8 = f32[16,16,256]{2,1,0:T(8,128)S(1)} collective-permute-done((f32[16,16,256]{2,1,0:T(8,128)}, f32[16,16,256]{2,1,0:T(8,128)S(1)}, u32[]{:S(2)}, u32[]{:S(2)}) %collective-permute-start.8) | collective-permute-done | bytes 262176 | tf_op jit(solution)/shard_map/ppermute | solution.py:230
  118.8 1.0 add.22
  119.8 1.6 %collective-permute-start.9 = (f32[16,16,256]{2,1,0:T(8,128)S(1)}, f32[16,16,256]{2,1,0:T(8,128)S(1)}, u32[]{:S(2)}, u32[]{:S(2)}) collective-permute-start(f32[16,16,256]{2,1,0:T(8,128)S(1)} %add.22), channel_id=1, source_target_pairs={{0,2},{1,3},{2,0},{3,1},{4,6},{5,7},{6,4},{7,5},{8,10},{9,11},{10,... | collective-permute-start | bytes 786440 | tf_op jit(solution)/shard_map/ppermute | solution.py:230
  121.4 0.2 reshape.42
  121.6 0.1 copy.16
  121.7 0.9 copy.18
  122.6 5.6 %collective-permute-done.9 = f32[16,16,256]{2,1,0:T(8,128)S(1)} collective-permute-done((f32[16,16,256]{2,1,0:T(8,128)S(1)}, f32[16,16,256]{2,1,0:T(8,128)S(1)}, u32[]{:S(2)}, u32[]{:S(2)}) %collective-permute-start.9) | collective-permute-done | bytes 262176 | tf_op jit(solution)/shard_map/ppermute | solution.py:230
  128.2 0.2 minimum_subtract_fusion
  128.4 0.2 reshape.40
  128.7 0.1 copy.15
  128.8 0.9 copy.17
  (26 shorter events, 0.1 us)
Async XLA Ops:
  2.3 22.3 %copy-start.1 = (bf16[16,16,256]{2,1,0:T(8,128)(2,1)}, bf16[16,16,256]{2,1,0:T(8,128)(2,1)S(1)}, u32[]{:S(2)}) copy-start(bf16[16,16,256]{2,1,0:T(8,128)(2,1)S(1)} %copy.30.own_ref) | copy-start | bytes 393220
  2.3 22.2 %collective-permute-start = (bf16[16,8,256]{2,1,0:T(8,128)(2,1)S(1)}, bf16[16,8,256]{2,1,0:T(8,128)(2,1)S(1)}, u32[]{:S(2)}, u32[]{:S(2)}) collective-permute-start(bf16[16,8,256]{2,1,0:T(8,128)(2,1)S(1)} %slice.16), channel_id=1, source_target_pairs={{0,8},{8,16},{16,24},{1,9},{9,17},{17,25},{2,10},{10,18},{18,26},{... | collective-permute-start | bytes 196616 | tf_op jit(solution)/shard_map/ppermute | solution.py:223
  24.5 0.6 copy-start.6
  25.2 12.2 %copy-start.4 = (bf16[64,1024]{1,0:T(8,128)(2,1)S(1)}, bf16[64,1024]{1,0:T(8,128)(2,1)}, u32[]{:S(2)}) copy-start(bf16[64,1024]{1,0:T(8,128)(2,1)} %param.5) | copy-start | bytes 393220
  35.9 8.0 %collective-permute-start.1 = (f32[16,16,256]{2,1,0:T(8,128)}, f32[16,16,256]{2,1,0:T(8,128)S(1)}, u32[]{:S(2)}, u32[]{:S(2)}) collective-permute-start(f32[16,16,256]{2,1,0:T(8,128)} %synthesize.2), channel_id=1, source_target_pairs={{0,4},{4,0},{1,5},{5,1},{2,6},{6,2},{3,7},{7,3},{8,12},{12,8},{9,1... | collective-permute-start | bytes 786440 | tf_op jit(solution)/shard_map/ppermute | solution.py:230
  45.0 6.3 %copy-start.2 = (bf16[16,16,256]{2,1,0:T(8,128)(2,1)}, bf16[16,16,256]{2,1,0:T(8,128)(2,1)S(1)}, u32[]{:S(2)}) copy-start(bf16[16,16,256]{2,1,0:T(8,128)(2,1)S(1)} %subtract_convert_fusion.own_ref) | copy-start | bytes 393220
  45.0 22.3 %copy-start.5 = (f32[64]{0:T(128)S(1)}, f32[64]{0:T(128)}, u32[]{:S(2)}) copy-start(f32[64]{0:T(128)} %param.8) | copy-start | bytes 772
  45.0 22.3 %copy-start.10 = (f32[64]{0:T(128)S(1)}, f32[64]{0:T(128)}, u32[]{:S(2)}) copy-start(f32[64]{0:T(128)} %param.9) | copy-start | bytes 772
  45.0 6.3 %collective-permute-start.2 = (bf16[16,8,256]{2,1,0:T(8,128)(2,1)S(1)}, bf16[16,8,256]{2,1,0:T(8,128)(2,1)S(1)}, u32[]{:S(2)}, u32[]{:S(2)}) collective-permute-start(bf16[16,8,256]{2,1,0:T(8,128)(2,1)S(1)} %slice.17), channel_id=1, source_target_pairs={{8,0},{16,8},{24,16},{9,1},{17,9},{25,17},{10,2},{18,10},{26,18},{... | collective-permute-start | bytes 196616 | tf_op jit(solution)/shard_map/ppermute | solution.py:223
  51.3 0.6 copy-start.8
  62.9 1.8 %collective-permute-start.3 = (f32[16,16,256]{2,1,0:T(8,128)}, f32[16,16,256]{2,1,0:T(8,128)S(1)}, u32[]{:S(2)}, u32[]{:S(2)}) collective-permute-start(f32[16,16,256]{2,1,0:T(8,128)} %correlate.2), channel_id=1, source_target_pairs={{0,1},{1,0},{2,3},{3,2},{4,5},{5,4},{6,7},{7,6},{8,9},{9,8},{10,11... | collective-permute-start | bytes 786440 | tf_op jit(solution)/shard_map/ppermute | solution.py:230
  65.8 8.4 %collective-permute-start.4 = (f32[16,16,256]{2,1,0:T(8,128)S(1)}, f32[16,16,256]{2,1,0:T(8,128)S(1)}, u32[]{:S(2)}, u32[]{:S(2)}) collective-permute-start(f32[16,16,256]{2,1,0:T(8,128)S(1)} %add.19), channel_id=1, source_target_pairs={{0,2},{1,3},{2,0},{3,1},{4,6},{5,7},{6,4},{7,5},{8,10},{9,11},{10,... | collective-permute-start | bytes 786440 | tf_op jit(solution)/shard_map/ppermute | solution.py:230
  74.4 5.4 %copy-start.3 = (bf16[16,16,256]{2,1,0:T(8,128)(2,1)}, bf16[16,16,256]{2,1,0:T(8,128)(2,1)S(1)}, u32[]{:S(2)}) copy-start(bf16[16,16,256]{2,1,0:T(8,128)(2,1)S(1)} %fusion.own_ref) | copy-start | bytes 393220
  74.4 5.4 %collective-permute-start.5 = (bf16[16,8,256]{2,1,0:T(8,128)(2,1)S(1)}, bf16[16,8,256]{2,1,0:T(8,128)(2,1)S(1)}, u32[]{:S(2)}, u32[]{:S(2)}) collective-permute-start(bf16[16,8,256]{2,1,0:T(8,128)(2,1)S(1)} %slice.18), channel_id=1, source_target_pairs={{0,8},{8,16},{16,24},{1,9},{9,17},{17,25},{2,10},{10,18},{18,26},{... | collective-permute-start | bytes 196616 | tf_op jit(solution)/shard_map/ppermute | solution.py:223
  79.8 0.6 copy-start.9
  91.0 6.9 %collective-permute-start.6 = (f32[16,16,256]{2,1,0:T(8,128)}, f32[16,16,256]{2,1,0:T(8,128)S(1)}, u32[]{:S(2)}, u32[]{:S(2)}) collective-permute-start(f32[16,16,256]{2,1,0:T(8,128)} %synthesize.3), channel_id=1, source_target_pairs={{0,4},{4,0},{1,5},{5,1},{2,6},{6,2},{3,7},{7,3},{8,12},{12,8},{9,1... | collective-permute-start | bytes 786440 | tf_op jit(solution)/shard_map/ppermute | solution.py:230
  99.1 6.2 %copy-start = (bf16[16,16,256]{2,1,0:T(8,128)(2,1)}, bf16[16,16,256]{2,1,0:T(8,128)(2,1)S(1)}, u32[]{:S(2)}) copy-start(bf16[16,16,256]{2,1,0:T(8,128)(2,1)S(1)} %get-tuple-element.8.own_ref) | copy-start | bytes 393220
  99.1 6.2 %collective-permute-start.7 = (bf16[16,8,256]{2,1,0:T(8,128)(2,1)S(1)}, bf16[16,8,256]{2,1,0:T(8,128)(2,1)S(1)}, u32[]{:S(2)}, u32[]{:S(2)}) collective-permute-start(bf16[16,8,256]{2,1,0:T(8,128)(2,1)S(1)} %slice.19), channel_id=1, source_target_pairs={{8,0},{16,8},{24,16},{9,1},{17,9},{25,17},{10,2},{18,10},{26,18},{... | collective-permute-start | bytes 196616 | tf_op jit(solution)/shard_map/ppermute | solution.py:223
  105.3 0.6 copy-start.7
  117.0 1.8 %collective-permute-start.8 = (f32[16,16,256]{2,1,0:T(8,128)}, f32[16,16,256]{2,1,0:T(8,128)S(1)}, u32[]{:S(2)}, u32[]{:S(2)}) collective-permute-start(f32[16,16,256]{2,1,0:T(8,128)} %correlate.3), channel_id=1, source_target_pairs={{0,1},{1,0},{2,3},{3,2},{4,5},{5,4},{6,7},{7,6},{8,9},{9,8},{10,11... | collective-permute-start | bytes 786440 | tf_op jit(solution)/shard_map/ppermute | solution.py:230
  119.8 8.4 %collective-permute-start.9 = (f32[16,16,256]{2,1,0:T(8,128)S(1)}, f32[16,16,256]{2,1,0:T(8,128)S(1)}, u32[]{:S(2)}, u32[]{:S(2)}) collective-permute-start(f32[16,16,256]{2,1,0:T(8,128)S(1)} %add.22), channel_id=1, source_target_pairs={{0,2},{1,3},{2,0},{3,1},{4,6},{5,7},{6,4},{7,5},{8,10},{9,11},{10,... | collective-permute-start | bytes 786440 | tf_op jit(solution)/shard_map/ppermute | solution.py:230

commit v2 on v1

--- a/solution.py
+++ b/solution.py
@@ -12,7 +12,7 @@
 RUN = 16
 GROUP = 8
 LANES = 128
-VMEM = 56 * 1024 * 1024
+VMEM = 24 * 1024 * 1024
 
 
 def to_blocks(value):
@@ -35,8 +35,8 @@
     )
 
 
-def bank_kernel(taps, rows, bank_ref, even_ref, odd_ref, flat):
-    atoms, chans, _ = bank_ref.shape
+def bank_kernel(taps, rows, low_ref, high_ref, even_ref, odd_ref, flat):
+    atoms, chans, _ = low_ref.shape
     tiles = even_ref.shape[0]
     margin = 8
     step = min(256, taps)
@@ -47,22 +47,23 @@
     zeros = jnp.zeros((margin, LANES), jnp.float32)
 
     def turn(pair, carry):
-        first = bank_ref[2 * pair]
-        second = bank_ref[2 * pair + 1]
-        doubled = jnp.concatenate([first, first, second, second], axis=0)
+        first, second = 2 * pair, 2 * pair + 1
+        stacked = jnp.concatenate(
+            [low_ref[first], high_ref[first], low_ref[second], high_ref[second]], axis=0
+        )
         for which in range(2):
-            base = pl.multiple_of((2 * pair + which) * rows, 8)
+            base = (2 * pair + which) * rows
             flat[pl.ds(base, margin), :] = zeros
             flat[pl.ds(base + margin + taps, margin), :] = zeros
         for part in range(taps // step):
             turned = lax.dot_general(
                 eye,
-                doubled[:, part * step : (part + 1) * step],
+                stacked[:, part * step : (part + 1) * step],
                 (((1,), (1,)), ((), ())),
                 preferred_element_type=jnp.float32,
             )
             for which in range(2):
-                base = pl.multiple_of((2 * pair + which) * rows + margin + part * step, 8)
+                base = (2 * pair + which) * rows + margin + part * step
                 flat[pl.ds(base, step), :] = turned[:, which * LANES : (which + 1) * LANES]
         return carry
 
@@ -71,15 +72,20 @@
     low = lax.broadcasted_iota(jnp.int32, (atoms, LANES), 1) < chans
 
     def tap(index):
-        return flat[pl.ds(index + margin, atoms, stride=rows), :]
+        value = flat[pl.ds(index + margin, atoms, stride=rows), :]
+        return value, pltpu.roll(value, chans, 1)
+
+    def store(ref, tile, early, late):
+        ref[tile, 0] = jnp.where(low, early[0], late[1]).astype(jnp.bfloat16)
+        ref[tile, 1] = jnp.where(low, early[1], late[0]).astype(jnp.bfloat16)
 
     def merge(turn_index, carry):
         for inner in range(4):
             tile = turn_index * 4 + inner
             middle = tap(2 * tile - 3)
             later = tap(2 * tile - 2)
-            even_ref[tile] = jnp.where(low, carry, middle).astype(jnp.bfloat16)
-            odd_ref[tile] = jnp.where(low, middle, later).astype(jnp.bfloat16)
+            store(even_ref, tile, carry, middle)
+            store(odd_ref, tile, middle, later)
             carry = later
         return carry
 
@@ -89,20 +95,26 @@
 def bank_tiles(atom_bank):
     atoms, chans, taps = atom_bank.shape
     tiles = taps // 2 + 4
-    rows = taps + 16
+    rows = taps + 17
     block = 16
-    shape = jax.ShapeDtypeStruct((tiles, atoms, LANES), jnp.bfloat16)
-    spec = pl.BlockSpec((tiles, block, LANES), lambda i: (0, i, 0))
-    return pl.pallas_call(
+    half = atoms // 2
+    turns = half // block
+    shape = jax.ShapeDtypeStruct((tiles, 2, half, LANES), jnp.bfloat16)
+    spec = pl.BlockSpec((tiles, 2, block, LANES), lambda i: (0, 0, i, 0))
+    even, odd = pl.pallas_call(
         functools.partial(bank_kernel, taps, rows),
-        grid=(atoms // block,),
-        in_specs=[pl.BlockSpec((block, chans, taps), lambda i: (i, 0, 0))],
+        grid=(turns,),
+        in_specs=[
+            pl.BlockSpec((block, chans, taps), lambda i: (i, 0, 0)),
+            pl.BlockSpec((block, chans, taps), lambda i: (i + turns, 0, 0)),
+        ],
         out_specs=[spec, spec],
         out_shape=[shape, shape],
         scratch_shapes=[pltpu.VMEM((block * rows, LANES), jnp.float32)],
         compiler_params=pltpu.CompilerParams(vmem_limit_bytes=VMEM),
         name="bank_tiles",
-    )(atom_bank)
+    )(atom_bank, atom_bank)
+    return even.reshape(tiles, atoms, LANES), odd.reshape(tiles, atoms, LANES)
 
 
 def conv_kernel(transposed, steps, own_ref, halo_ref, even_hbm, odd_hbm, out_ref, even, odd, base, spread, total, sems):
@@ -154,7 +166,7 @@
         start = step if transposed else halo * run - step
         return spread[pl.ds(start, run)].reshape(run * parts, width)
 
-    def add(first, count):
+    def add(which, first, count):
         left = jnp.concatenate([rows(first + i) for i in range(count)], axis=1)
         if transposed:
             right = jnp.concatenate([block(first + i) for i in range(count)], axis=1)
@@ -162,7 +174,7 @@
         else:
             right = jnp.concatenate([block(first + i) for i in range(count)], axis=0)
             dims = (((1,), (0,)), ((), ()))
-        total[...] += lax.dot_general(left, right, dims, preferred_element_type=jnp.float32)
+        total[which] += lax.dot_general(left, right, dims, preferred_element_type=jnp.float32)
 
     turns = steps // GROUP
     share = -(-turns // chunks)
@@ -175,12 +187,13 @@
         low = low if chunk == 0 else min(low, (chunk * size - 4) // 2 // GROUP)
 
         def loop(turn_index, carry):
-            add(turn_index * GROUP, GROUP)
+            add(0, turn_index * GROUP, GROUP // 2)
+            add(1, turn_index * GROUP + GROUP // 2, GROUP // 2)
             return carry
 
         lax.fori_loop(low, high, loop, 0)
-    add(turns * GROUP, steps - turns * GROUP)
-    out_ref[...] = total[...].reshape(out_ref.shape)
+    add(0, turns * GROUP, steps - turns * GROUP)
+    out_ref[...] = (total[0] + total[1]).reshape(out_ref.shape).astype(out_ref.dtype)
 
 
 def convolve(own, halo, even, odd, transposed):
@@ -200,13 +213,15 @@
             pl.BlockSpec(memory_space=pl.ANY),
         ],
         out_specs=pl.BlockSpec(memory_space=pltpu.VMEM),
-        out_shape=jax.ShapeDtypeStruct((run, parts, out_width), jnp.float32),
+        out_shape=jax.ShapeDtypeStruct(
+            (run, parts, out_width), jnp.float32 if transposed else jnp.bfloat16
+        ),
         scratch_shapes=[
             pltpu.VMEM(even.shape, jnp.bfloat16),
             pltpu.VMEM(odd.shape, jnp.bfloat16),
             pltpu.VMEM((run, parts + beside, width), jnp.float32),
             pltpu.VMEM(((beside + 1) * run, parts, width), jnp.bfloat16),
-            pltpu.VMEM((run * parts, out_width), jnp.float32),
+            pltpu.VMEM((2, run * parts, out_width), jnp.float32),
             pltpu.SemaphoreType.DMA((2, chunks)),
         ],
         compiler_params=pltpu.CompilerParams(vmem_limit_bytes=VMEM),
@@ -227,7 +242,8 @@
     count = lax.axis_size(axis)
     step = 1
     while step < count:
-        value = value + lax.ppermute(value, axis, [(i, i ^ step) for i in range(count)])
+        other = lax.ppermute(value, axis, [(i, i ^ step) for i in range(count)])
+        value = value.astype(jnp.float32) + other.astype(jnp.float32)
         step *= 2
     return value
 

time: 130 us -> 120 us (0.923)
  Pallas kernels: 60.5 us -> 51.2 us
  local copies, waits for them, and re-layouts: 7.35 us -> 15.8 us
  waiting for transfers between devices: 38.7 us -> 33.7 us
  other arithmetic: 4.67 us -> 0.85 us
    unnamed x26 -> x24, local copies, waits for them, and re-layouts: 5.6 us -> 14.1 us
    pallas_call x4, Pallas kernels: 43.3 us -> 35 us  [convolve(): pl.pallas_call(functools.partial(conv_kernel, transposed, steps), in_spec...]
    ppermute x6, waiting for transfers between devices: 27 us -> 21.8 us  [summed(): other = lax.ppermute(value, axis, [(i, i ^ step) for i in range(count)])]
    convert_element_type x2, other arithmetic: 2.25 us -> 0.33 us  [body(): rounded = misfit.astype(jnp.bfloat16)]
    add x2, other arithmetic: 1.98 us -> 0.08 us  [summed(): value = value.astype(jnp.float32) + other.astype(jnp.float32)]
  transfers between devices with their start and end apart: 10 -> 10, of which waited for: 9 -> 9; matrix products, arithmetic and copies ran while one was open for 1% -> 2% of each run, Pallas kernels for 13% -> 14%
where the time goes in v2:
time: 120 us
  Pallas kernels  51.2 us (43%)
  waiting for transfers between devices  33.7 us (28%)
  starting transfers between devices  17.4 us (14%)
  local copies, waits for them, and re-layouts  15.8 us (13%)
    pallas_call x4, Pallas kernels, convolve(): pl.pallas_call(functools.partial(conv_kernel, transposed, steps), in_spec...  35 us
    ppermute x6, waiting for transfers between devices, summed(): other = lax.ppermute(value, axis, [(i, i ^ step) for i in range(count)])  21.8 us
    pallas_call x1, Pallas kernels, bank_tiles(): pl.pallas_call(functools.partial(bank_kernel, taps, rows), grid=(turns,),...  16.2 us
    unnamed x24, local copies, waits for them, and re-layouts  14.1 us
    ppermute x4, waiting for transfers between devices, shifted(): lax.ppermute(value, axis, [(i, i + steps) for i in range(first, last)])  12 us
    ppermute x4, starting transfers between devices, shifted(): lax.ppermute(value, axis, [(i, i + steps) for i in range(first, last)])  11 us
    ppermute x6, starting transfers between devices, summed(): other = lax.ppermute(value, axis, [(i, i ^ step) for i in range(count)])  6.37 us
  transfers between devices with their start and end apart: 10, of which 9 were waited for; matrix products, arithmetic and copies ran while one was open for 2% of the time, Pallas kernels for 14%

profile of v2, /device:TPU:0, one launch (start us, length us, event | category | flops | bytes accessed | tf_op | source)
XLA Modules:
  0.0 119.9 jit_solution(12244499308366059372)
XLA Ops:
  0.6 1.1 copy.11
  1.8 0.3 reshape.54
  2.1 0.1 copy.30.own_ref
  2.3 4.9 %collective-permute-start = (bf16[16,8,256]{2,1,0:T(8,128)(2,1)S(1)}, bf16[16,8,256]{2,1,0:T(8,128)(2,1)S(1)}, u32[]{:S(2)}, u32[]{:S(2)}) collective-permute-start(bf16[16,8,256]{2,1,0:T(8,128)(2,1)S(1)} %slice.16), channel_id=1, source_target_pairs={{0,8},{8,16},{16,24},{1,9},{9,17},{17,25},{2,10},{10,18},{18,26},{... | collective-permute-start | bytes 196616 | tf_op jit(solution)/shard_map/ppermute | solution.py:238
  7.2 0.0 copy-start
  7.2 2.2 %copy-done = bf16[64,64,512]{2,1,0:T(8,128)(2,1)S(1)} copy-done((bf16[64,64,512]{2,1,0:T(8,128)(2,1)S(1)}, bf16[64,64,512]{2,1,0:T(8,128)(2,1)}, u32[]{:S(2)}) %copy-start) | copy-done | bytes 4194328
  9.4 16.2 %bank_tiles.1 = (bf16[260,2,32,128]{3,2,1,0:T(8,128)(2,1)S(1)}, bf16[260,2,32,128]{3,2,1,0:T(8,128)(2,1)S(1)}) custom-call(bf16[64,64,512]{2,1,0:T(8,128)(2,1)S(1)} %copy-done, bf16[64,64,512]{2,1,0:T(8,128)(2,1)S(1)} %copy-done), custom_call_target="tpu_custom_call" | custom-call | tf_op jit(solution)/shard_map/bank_tiles/pallas_call | solution.py:104
  25.7 0.0 copy-start.7
  25.7 8.6 %synthesize.2 = bf16[16,16,256]{2,1,0:T(8,128)(2,1)S(1)} custom-call(bf16[16,16,256]{2,1,0:T(8,128)(2,1)S(1)} %copy.30.own_ref, bf16[16,8,256]{2,1,0:T(8,128)(2,1)S(1)} %collective-permute-done.halo_ref, bf16[260,64,128]{2,1,0:T(8,128)(2,1)S(1)} %bitcast.20, bf16[260,64,128]{2,1,0:T(8,128)(2,1)S(1)} %bitcast.24), custom_call_target="tpu_custom_call" | custom-call | flops 4328521728 | bytes 9043968 | tf_op jit(solution)/shard_map/synthesize/pallas_call | solution.py:207
  34.3 1.5 %collective-permute-start.1 = (bf16[16,16,256]{2,1,0:T(8,128)(2,1)S(1)}, bf16[16,16,256]{2,1,0:T(8,128)(2,1)S(1)}, u32[]{:S(2)}, u32[]{:S(2)}) collective-permute-start(bf16[16,16,256]{2,1,0:T(8,128)(2,1)S(1)} %synthesize.2), channel_id=1, source_target_pairs={{0,4},{4,0},{1,5},{5,1},{2,6},{6,2},{3,7},{7,3},{8,12},{12,8},{9,1... | collective-permute-start | bytes 393224 | tf_op jit(solution)/shard_map/ppermute | solution.py:245
  35.8 0.1 copy.21
  36.0 0.3 reshape.55
  36.3 3.0 %collective-permute-done.1 = bf16[16,16,256]{2,1,0:T(8,128)(2,1)S(1)} collective-permute-done((bf16[16,16,256]{2,1,0:T(8,128)(2,1)S(1)}, bf16[16,16,256]{2,1,0:T(8,128)(2,1)S(1)}, u32[]{:S(2)}, u32[]{:S(2)}) %collective-permute-start.1) | collective-permute-done | bytes 131104 | tf_op jit(solution)/shard_map/ppermute | solution.py:245
  39.3 0.2 subtract_convert_fusion.own_ref
  39.5 1.3 %collective-permute-start.2 = (bf16[16,8,256]{2,1,0:T(8,128)(2,1)S(1)}, bf16[16,8,256]{2,1,0:T(8,128)(2,1)S(1)}, u32[]{:S(2)}, u32[]{:S(2)}) collective-permute-start(bf16[16,8,256]{2,1,0:T(8,128)(2,1)S(1)} %slice.17), channel_id=1, source_target_pairs={{8,0},{16,8},{24,16},{9,1},{17,9},{25,17},{10,2},{18,10},{26,18},{... | collective-permute-start | bytes 196616 | tf_op jit(solution)/shard_map/ppermute | solution.py:238
  40.8 4.9 %collective-permute-done.2.halo_ref = bf16[16,8,256]{2,1,0:T(8,128)(2,1)S(1)} collective-permute-done((bf16[16,8,256]{2,1,0:T(8,128)(2,1)S(1)}, bf16[16,8,256]{2,1,0:T(8,128)(2,1)S(1)}, u32[]{:S(2)}, u32[]{:S(2)}) %collective-permute-start.2) | collective-permute-done | bytes 65568 | tf_op jit(solution)/shard_map/ppermute | solution.py:238
  45.7 2.2 %copy-done.2 = bf16[260,2,32,128]{3,2,1,0:T(8,128)(2,1)S(1)} copy-done((bf16[260,2,32,128]{3,2,1,0:T(8,128)(2,1)S(1)}, bf16[260,2,32,128]{3,2,1,0:T(8,128)(2,1)}, u32[]{:S(2)}) %copy-start.2) | copy-done | bytes 4259864
  47.9 2.2 %copy-done.5 = bf16[260,2,32,128]{3,2,1,0:T(8,128)(2,1)S(1)} copy-done((bf16[260,2,32,128]{3,2,1,0:T(8,128)(2,1)S(1)}, bf16[260,2,32,128]{3,2,1,0:T(8,128)(2,1)}, u32[]{:S(2)}) %copy-start.5) | copy-done | bytes 4259864
  50.1 8.9 %correlate.2 = f32[16,16,256]{2,1,0:T(8,128)S(1)} custom-call(bf16[16,16,256]{2,1,0:T(8,128)(2,1)S(1)} %subtract_convert_fusion.own_ref, bf16[16,8,256]{2,1,0:T(8,128)(2,1)S(1)} %collective-permute-done.2.halo_ref, bf16[260,64,128]{2,1,0:T(8,128)(2,1)S(1)} %bitcast.21, bf16[260,64,128]{2,1,0:T(8,128)(2,1)S(1)} %bitcast.25), custom_call_target="tpu_custom_call" | custom-call | flops 4328521728 | bytes 9043968 | tf_op jit(solution)/shard_map/correlate/pallas_call | solution.py:207
  59.0 0.1 collective-permute-start.3
  59.1 1.5 %collective-permute-done.3 = f32[16,16,256]{2,1,0:T(8,128)S(1)} collective-permute-done((f32[16,16,256]{2,1,0:T(8,128)S(1)}, f32[16,16,256]{2,1,0:T(8,128)S(1)}, u32[]{:S(2)}, u32[]{:S(2)}) %collective-permute-start.3) | collective-permute-done | bytes 262176 | tf_op jit(solution)/shard_map/ppermute | solution.py:245
  60.7 1.6 %collective-permute-start.4 = (f32[16,16,256]{2,1,0:T(8,128)S(1)}, f32[16,16,256]{2,1,0:T(8,128)S(1)}, u32[]{:S(2)}, u32[]{:S(2)}) collective-permute-start(f32[16,16,256]{2,1,0:T(8,128)S(1)} %add.19), channel_id=1, source_target_pairs={{0,2},{1,3},{2,0},{3,1},{4,6},{5,7},{6,4},{7,5},{8,10},{9,11},{10,... | collective-permute-start | bytes 786440 | tf_op jit(solution)/shard_map/ppermute | solution.py:245
  62.3 0.1 min.20
  62.4 0.1 mul.19
  62.5 6.6 %collective-permute-done.4 = f32[16,16,256]{2,1,0:T(8,128)S(1)} collective-permute-done((f32[16,16,256]{2,1,0:T(8,128)S(1)}, f32[16,16,256]{2,1,0:T(8,128)S(1)}, u32[]{:S(2)}, u32[]{:S(2)}) %collective-permute-start.4) | collective-permute-done | bytes 262176 | tf_op jit(solution)/shard_map/ppermute | solution.py:245
  69.1 0.2 fusion.own_ref
  69.3 3.5 %collective-permute-start.5 = (bf16[16,8,256]{2,1,0:T(8,128)(2,1)S(1)}, bf16[16,8,256]{2,1,0:T(8,128)(2,1)S(1)}, u32[]{:S(2)}, u32[]{:S(2)}) collective-permute-start(bf16[16,8,256]{2,1,0:T(8,128)(2,1)S(1)} %slice.18), channel_id=1, source_target_pairs={{0,8},{8,16},{16,24},{1,9},{9,17},{17,25},{2,10},{10,18},{18,26},{... | collective-permute-start | bytes 196616 | tf_op jit(solution)/shard_map/ppermute | solution.py:238
  72.8 1.9 %collective-permute-done.5.halo_ref = bf16[16,8,256]{2,1,0:T(8,128)(2,1)S(1)} collective-permute-done((bf16[16,8,256]{2,1,0:T(8,128)(2,1)S(1)}, bf16[16,8,256]{2,1,0:T(8,128)(2,1)S(1)}, u32[]{:S(2)}, u32[]{:S(2)}) %collective-permute-start.5) | collective-permute-done | bytes 65568 | tf_op jit(solution)/shard_map/ppermute | solution.py:238
  74.7 2.2 %copy-done.3 = bf16[260,2,32,128]{3,2,1,0:T(8,128)(2,1)S(1)} copy-done((bf16[260,2,32,128]{3,2,1,0:T(8,128)(2,1)S(1)}, bf16[260,2,32,128]{3,2,1,0:T(8,128)(2,1)}, u32[]{:S(2)}) %copy-start.3) | copy-done | bytes 4259864
  76.9 2.2 %copy-done.6 = bf16[260,2,32,128]{3,2,1,0:T(8,128)(2,1)S(1)} copy-done((bf16[260,2,32,128]{3,2,1,0:T(8,128)(2,1)S(1)}, bf16[260,2,32,128]{3,2,1,0:T(8,128)(2,1)}, u32[]{:S(2)}) %copy-start.6) | copy-done | bytes 4259864
  79.1 8.6 %synthesize.3 = bf16[16,16,256]{2,1,0:T(8,128)(2,1)S(1)} custom-call(bf16[16,16,256]{2,1,0:T(8,128)(2,1)S(1)} %fusion.own_ref, bf16[16,8,256]{2,1,0:T(8,128)(2,1)S(1)} %collective-permute-done.5.halo_ref, bf16[260,64,128]{2,1,0:T(8,128)(2,1)S(1)} %bitcast.22, bf16[260,64,128]{2,1,0:T(8,128)(2,1)S(1)} %bitcast.26), custom_call_target="tpu_custom_call" | custom-call | flops 4328521728 | bytes 9043968 | tf_op jit(solution)/shard_map/synthesize/pallas_call | solution.py:207
  87.7 1.5 %collective-permute-start.6 = (bf16[16,16,256]{2,1,0:T(8,128)(2,1)S(1)}, bf16[16,16,256]{2,1,0:T(8,128)(2,1)S(1)}, u32[]{:S(2)}, u32[]{:S(2)}) collective-permute-start(bf16[16,16,256]{2,1,0:T(8,128)(2,1)S(1)} %synthesize.3), channel_id=1, source_target_pairs={{0,4},{4,0},{1,5},{5,1},{2,6},{6,2},{3,7},{7,3},{8,12},{12,8},{9,1... | collective-permute-start | bytes 393224 | tf_op jit(solution)/shard_map/ppermute | solution.py:245
  89.2 3.5 %collective-permute-done.6 = bf16[16,16,256]{2,1,0:T(8,128)(2,1)S(1)} collective-permute-done((bf16[16,16,256]{2,1,0:T(8,128)(2,1)S(1)}, bf16[16,16,256]{2,1,0:T(8,128)(2,1)S(1)}, u32[]{:S(2)}, u32[]{:S(2)}) %collective-permute-start.6) | collective-permute-done | bytes 131104 | tf_op jit(solution)/shard_map/ppermute | solution.py:245
  92.7 0.2 fusion.1
  92.9 1.3 %collective-permute-start.7 = (bf16[16,8,256]{2,1,0:T(8,128)(2,1)S(1)}, bf16[16,8,256]{2,1,0:T(8,128)(2,1)S(1)}, u32[]{:S(2)}, u32[]{:S(2)}) collective-permute-start(bf16[16,8,256]{2,1,0:T(8,128)(2,1)S(1)} %slice.19), channel_id=1, source_target_pairs={{8,0},{16,8},{24,16},{9,1},{17,9},{25,17},{10,2},{18,10},{26,18},{... | collective-permute-start | bytes 196616 | tf_op jit(solution)/shard_map/ppermute | solution.py:238
  94.2 5.2 %collective-permute-done.7.halo_ref = bf16[16,8,256]{2,1,0:T(8,128)(2,1)S(1)} collective-permute-done((bf16[16,8,256]{2,1,0:T(8,128)(2,1)S(1)}, bf16[16,8,256]{2,1,0:T(8,128)(2,1)S(1)}, u32[]{:S(2)}, u32[]{:S(2)}) %collective-permute-start.7) | collective-permute-done | bytes 65568 | tf_op jit(solution)/shard_map/ppermute | solution.py:238
  99.4 8.9 %correlate.3 = f32[16,16,256]{2,1,0:T(8,128)S(1)} custom-call(bf16[16,16,256]{2,1,0:T(8,128)(2,1)S(1)} %get-tuple-element.8.own_ref, bf16[16,8,256]{2,1,0:T(8,128)(2,1)S(1)} %collective-permute-done.7.halo_ref, bf16[260,64,128]{2,1,0:T(8,128)(2,1)S(1)} %bitcast.23, bf16[260,64,128]{2,1,0:T(8,128)(2,1)S(1)} %bitcast.27), custom_call_target="tpu_custom_call" | custom-call | flops 4328521728 | bytes 9043968 | tf_op jit(solution)/shard_map/correlate/pallas_call | solution.py:207
  108.3 0.1 collective-permute-start.8
  108.4 1.5 %collective-permute-done.8 = f32[16,16,256]{2,1,0:T(8,128)S(1)} collective-permute-done((f32[16,16,256]{2,1,0:T(8,128)S(1)}, f32[16,16,256]{2,1,0:T(8,128)S(1)}, u32[]{:S(2)}, u32[]{:S(2)}) %collective-permute-start.8) | collective-permute-done | bytes 262176 | tf_op jit(solution)/shard_map/ppermute | solution.py:245
  110.0 1.6 %collective-permute-start.9 = (f32[16,16,256]{2,1,0:T(8,128)S(1)}, f32[16,16,256]{2,1,0:T(8,128)S(1)}, u32[]{:S(2)}, u32[]{:S(2)}) collective-permute-start(f32[16,16,256]{2,1,0:T(8,128)S(1)} %add.22), channel_id=1, source_target_pairs={{0,2},{1,3},{2,0},{3,1},{4,6},{5,7},{6,4},{7,5},{8,10},{9,11},{10,... | collective-permute-start | bytes 786440 | tf_op jit(solution)/shard_map/ppermute | solution.py:245
  111.5 0.2 reshape.50
  111.8 0.1 copy.16
  111.9 0.9 copy.18
  112.8 5.6 %collective-permute-done.9 = f32[16,16,256]{2,1,0:T(8,128)S(1)} collective-permute-done((f32[16,16,256]{2,1,0:T(8,128)S(1)}, f32[16,16,256]{2,1,0:T(8,128)S(1)}, u32[]{:S(2)}, u32[]{:S(2)}) %collective-permute-start.9) | collective-permute-done | bytes 262176 | tf_op jit(solution)/shard_map/ppermute | solution.py:245
  118.4 0.2 minimum_subtract_fusion
  118.6 0.2 reshape.48
  118.9 0.1 copy.15
  119.0 0.9 copy.17
  (24 shorter events, 0.1 us)
Async XLA Ops:
  2.3 23.4 %collective-permute-start = (bf16[16,8,256]{2,1,0:T(8,128)(2,1)S(1)}, bf16[16,8,256]{2,1,0:T(8,128)(2,1)S(1)}, u32[]{:S(2)}, u32[]{:S(2)}) collective-permute-start(bf16[16,8,256]{2,1,0:T(8,128)(2,1)S(1)} %slice.16), channel_id=1, source_target_pairs={{0,8},{8,16},{16,24},{1,9},{9,17},{17,25},{2,10},{10,18},{18,26},{... | collective-permute-start | bytes 196616 | tf_op jit(solution)/shard_map/ppermute | solution.py:238
  7.2 2.2 %copy-start = (bf16[64,64,512]{2,1,0:T(8,128)(2,1)S(1)}, bf16[64,64,512]{2,1,0:T(8,128)(2,1)}, u32[]{:S(2)}) copy-start(bf16[64,64,512]{2,1,0:T(8,128)(2,1)} %high_ref.1) | copy-start | bytes 12582916
  25.7 8.6 %copy-start.1 = (bf16[260,2,32,128]{3,2,1,0:T(8,128)(2,1)}, bf16[260,2,32,128]{3,2,1,0:T(8,128)(2,1)S(1)}, u32[]{:S(2)}) copy-start(bf16[260,2,32,128]{3,2,1,0:T(8,128)(2,1)S(1)} %get-tuple-element.4) | copy-start | bytes 12779524
  25.7 8.6 %copy-start.4 = (bf16[260,2,32,128]{3,2,1,0:T(8,128)(2,1)}, bf16[260,2,32,128]{3,2,1,0:T(8,128)(2,1)S(1)}, u32[]{:S(2)}) copy-start(bf16[260,2,32,128]{3,2,1,0:T(8,128)(2,1)S(1)} %get-tuple-element.5) | copy-start | bytes 12779524
  25.7 10.2 %copy-start.7 = (bf16[64,1024]{1,0:T(8,128)(2,1)S(1)}, bf16[64,1024]{1,0:T(8,128)(2,1)}, u32[]{:S(2)}) copy-start(bf16[64,1024]{1,0:T(8,128)(2,1)} %param.5) | copy-start | bytes 393220
  34.3 5.0 %collective-permute-start.1 = (bf16[16,16,256]{2,1,0:T(8,128)(2,1)S(1)}, bf16[16,16,256]{2,1,0:T(8,128)(2,1)S(1)}, u32[]{:S(2)}, u32[]{:S(2)}) collective-permute-start(bf16[16,16,256]{2,1,0:T(8,128)(2,1)S(1)} %synthesize.2), channel_id=1, source_target_pairs={{0,4},{4,0},{1,5},{5,1},{2,6},{6,2},{3,7},{7,3},{8,12},{12,8},{9,1... | collective-permute-start | bytes 393224 | tf_op jit(solution)/shard_map/ppermute | solution.py:245
  39.5 22.8 %copy-start.8 = (f32[64]{0:T(128)S(1)}, f32[64]{0:T(128)}, u32[]{:S(2)}) copy-start(f32[64]{0:T(128)} %param.8) | copy-start | bytes 772
  39.5 22.8 %copy-start.9 = (f32[64]{0:T(128)S(1)}, f32[64]{0:T(128)}, u32[]{:S(2)}) copy-start(f32[64]{0:T(128)} %param.9) | copy-start | bytes 772
  39.5 6.2 %collective-permute-start.2 = (bf16[16,8,256]{2,1,0:T(8,128)(2,1)S(1)}, bf16[16,8,256]{2,1,0:T(8,128)(2,1)S(1)}, u32[]{:S(2)}, u32[]{:S(2)}) collective-permute-start(bf16[16,8,256]{2,1,0:T(8,128)(2,1)S(1)} %slice.17), channel_id=1, source_target_pairs={{8,0},{16,8},{24,16},{9,1},{17,9},{25,17},{10,2},{18,10},{26,18},{... | collective-permute-start | bytes 196616 | tf_op jit(solution)/shard_map/ppermute | solution.py:238
  45.7 2.2 %copy-start.2 = (bf16[260,2,32,128]{3,2,1,0:T(8,128)(2,1)S(1)}, bf16[260,2,32,128]{3,2,1,0:T(8,128)(2,1)}, u32[]{:S(2)}) copy-start(bf16[260,2,32,128]{3,2,1,0:T(8,128)(2,1)} %copy-done.1) | copy-start | bytes 12779524
  47.9 2.2 %copy-start.5 = (bf16[260,2,32,128]{3,2,1,0:T(8,128)(2,1)S(1)}, bf16[260,2,32,128]{3,2,1,0:T(8,128)(2,1)}, u32[]{:S(2)}) copy-start(bf16[260,2,32,128]{3,2,1,0:T(8,128)(2,1)} %copy-done.4) | copy-start | bytes 12779524
  59.0 1.6 %collective-permute-start.3 = (f32[16,16,256]{2,1,0:T(8,128)S(1)}, f32[16,16,256]{2,1,0:T(8,128)S(1)}, u32[]{:S(2)}, u32[]{:S(2)}) collective-permute-start(f32[16,16,256]{2,1,0:T(8,128)S(1)} %correlate.2), channel_id=1, source_target_pairs={{0,1},{1,0},{2,3},{3,2},{4,5},{5,4},{6,7},{7,6},{8,9},{9,8},{10,11... | collective-permute-start | bytes 786440 | tf_op jit(solution)/shard_map/ppermute | solution.py:245
  60.7 8.4 %collective-permute-start.4 = (f32[16,16,256]{2,1,0:T(8,128)S(1)}, f32[16,16,256]{2,1,0:T(8,128)S(1)}, u32[]{:S(2)}, u32[]{:S(2)}) collective-permute-start(f32[16,16,256]{2,1,0:T(8,128)S(1)} %add.19), channel_id=1, source_target_pairs={{0,2},{1,3},{2,0},{3,1},{4,6},{5,7},{6,4},{7,5},{8,10},{9,11},{10,... | collective-permute-start | bytes 786440 | tf_op jit(solution)/shard_map/ppermute | solution.py:245
  69.3 5.4 %collective-permute-start.5 = (bf16[16,8,256]{2,1,0:T(8,128)(2,1)S(1)}, bf16[16,8,256]{2,1,0:T(8,128)(2,1)S(1)}, u32[]{:S(2)}, u32[]{:S(2)}) collective-permute-start(bf16[16,8,256]{2,1,0:T(8,128)(2,1)S(1)} %slice.18), channel_id=1, source_target_pairs={{0,8},{8,16},{16,24},{1,9},{9,17},{17,25},{2,10},{10,18},{18,26},{... | collective-permute-start | bytes 196616 | tf_op jit(solution)/shard_map/ppermute | solution.py:238
  74.7 2.2 %copy-start.3 = (bf16[260,2,32,128]{3,2,1,0:T(8,128)(2,1)S(1)}, bf16[260,2,32,128]{3,2,1,0:T(8,128)(2,1)}, u32[]{:S(2)}) copy-start(bf16[260,2,32,128]{3,2,1,0:T(8,128)(2,1)} %copy-done.1) | copy-start | bytes 12779524
  76.9 2.2 %copy-start.6 = (bf16[260,2,32,128]{3,2,1,0:T(8,128)(2,1)S(1)}, bf16[260,2,32,128]{3,2,1,0:T(8,128)(2,1)}, u32[]{:S(2)}) copy-start(bf16[260,2,32,128]{3,2,1,0:T(8,128)(2,1)} %copy-done.4) | copy-start | bytes 12779524
  87.7 5.0 %collective-permute-start.6 = (bf16[16,16,256]{2,1,0:T(8,128)(2,1)S(1)}, bf16[16,16,256]{2,1,0:T(8,128)(2,1)S(1)}, u32[]{:S(2)}, u32[]{:S(2)}) collective-permute-start(bf16[16,16,256]{2,1,0:T(8,128)(2,1)S(1)} %synthesize.3), channel_id=1, source_target_pairs={{0,4},{4,0},{1,5},{5,1},{2,6},{6,2},{3,7},{7,3},{8,12},{12,8},{9,1... | collective-permute-start | bytes 393224 | tf_op jit(solution)/shard_map/ppermute | solution.py:245
  92.9 6.5 %collective-permute-start.7 = (bf16[16,8,256]{2,1,0:T(8,128)(2,1)S(1)}, bf16[16,8,256]{2,1,0:T(8,128)(2,1)S(1)}, u32[]{:S(2)}, u32[]{:S(2)}) collective-permute-start(bf16[16,8,256]{2,1,0:T(8,128)(2,1)S(1)} %slice.19), channel_id=1, source_target_pairs={{8,0},{16,8},{24,16},{9,1},{17,9},{25,17},{10,2},{18,10},{26,18},{... | collective-permute-start | bytes 196616 | tf_op jit(solution)/shard_map/ppermute | solution.py:238
  108.3 1.6 %collective-permute-start.8 = (f32[16,16,256]{2,1,0:T(8,128)S(1)}, f32[16,16,256]{2,1,0:T(8,128)S(1)}, u32[]{:S(2)}, u32[]{:S(2)}) collective-permute-start(f32[16,16,256]{2,1,0:T(8,128)S(1)} %correlate.3), channel_id=1, source_target_pairs={{0,1},{1,0},{2,3},{3,2},{4,5},{5,4},{6,7},{7,6},{8,9},{9,8},{10,11... | collective-permute-start | bytes 786440 | tf_op jit(solution)/shard_map/ppermute | solution.py:245
  110.0 8.4 %collective-permute-start.9 = (f32[16,16,256]{2,1,0:T(8,128)S(1)}, f32[16,16,256]{2,1,0:T(8,128)S(1)}, u32[]{:S(2)}, u32[]{:S(2)}) collective-permute-start(f32[16,16,256]{2,1,0:T(8,128)S(1)} %add.22), channel_id=1, source_target_pairs={{0,2},{1,3},{2,0},{3,1},{4,6},{5,7},{6,4},{7,5},{8,10},{9,11},{10,... | collective-permute-start | bytes 786440 | tf_op jit(solution)/shard_map/ppermute | solution.py:245

commit v3 on v1

v3 whole, which is shorter than its diff:
```python
import functools

import jax
import jax.numpy as jnp
from jax import lax
from jax.experimental import pallas as pl
from jax.experimental.pallas import tpu as pltpu
from jax.sharding import PartitionSpec as P

ITERS = 2
PHASES = 4
RUN = 16
LANES = 128
VMEM = 24 * 1024 * 1024


def to_blocks(value):
    rows, slab = value.shape
    parts = slab // (RUN * PHASES)
    return (
        value.reshape(rows, parts, RUN, PHASES)
        .transpose(2, 1, 3, 0)
        .reshape(RUN, parts, PHASES * rows)
    )


def from_blocks(value):
    run, parts, width = value.shape
    rows = width // PHASES
    return (
        value.reshape(run, parts, PHASES, rows)
        .transpose(3, 1, 0, 2)
        .reshape(rows, parts * run * PHASES)
    )


def bank_kernel(rows, bank_hbm, even_ref, odd_ref, bank, flat, sems):
    atoms, chans, taps = bank.shape
    tiles = even_ref.shape[0]
    half, turns = atoms // 2, sems.shape[0]
    block = half // turns
    margin = 8
    step = min(256, taps)
    eye = (
        lax.broadcasted_iota(jnp.int32, (step, step), 0)
        == lax.broadcasted_iota(jnp.int32, (step, step), 1)
    ).astype(jnp.bfloat16)
    zeros = jnp.zeros((margin, LANES), jnp.float32)
    low = lax.broadcasted_iota(jnp.int32, (block, LANES), 1) < chans

    copies = [
        [
            pltpu.make_async_copy(bank_hbm.at[span], bank.at[span], sems.at[group, which])
            for which, span in enumerate(
                (pl.ds(group * block, block), pl.ds(half + group * block, block))
            )
        ]
        for group in range(turns)
    ]
    for pair in copies:
        for copy in pair:
            copy.start()

    def tap(index):
        value = flat[pl.ds(index + margin, block, stride=rows), :]
        return value, pltpu.roll(value, chans, 1)

    for group in range(turns):
        for copy in copies[group]:
            copy.wait()

        def turn(pair, carry):
            first = group * block + 2 * pair
            stacked = jnp.concatenate(
                [bank[first], bank[half + first], bank[first + 1], bank[half + first + 1]], axis=0
            )
            for which in range(2):
                base = (2 * pair + which) * rows
                flat[pl.ds(base, margin), :] = zeros
                flat[pl.ds(base + margin + taps, margin), :] = zeros
            for part in range(taps // step):
                turned = lax.dot_general(
                    eye,
                    stacked[:, part * step : (part + 1) * step],
                    (((1,), (1,)), ((), ())),
                    preferred_element_type=jnp.float32,
                )
                for which in range(2):
                    base = (2 * pair + which) * rows + margin + part * step
                    flat[pl.ds(base, step), :] = turned[:, which * LANES : (which + 1) * LANES]
            return carry

        lax.fori_loop(0, block // 2, turn, 0)

        def store(ref, tile, early, late):
            start = group * block
            ref[tile, start : start + block] = jnp.where(low, early[0], late[1]).astype(jnp.bfloat16)
            start += half
            ref[tile, start : start + block] = jnp.where(low, early[1], late[0]).astype(jnp.bfloat16)

        unroll = next(n for n in (20, 13, 8, 5, 4, 2, 1) if tiles % n == 0)

        def merge(turn_index, carry):
            for inner in range(unroll):
                tile = turn_index * unroll + inner
                middle = tap(2 * tile - 3)
                later = tap(2 * tile - 2)
                store(even_ref, tile, carry, middle)
                store(odd_ref, tile, middle, later)
                carry = later
            return carry

        lax.fori_loop(0, tiles // unroll, merge, tap(-4))


def bank_tiles(atom_bank):
    atoms, chans, taps = atom_bank.shape
    tiles = taps // 2 + 4
    rows = taps + 17
    block = 16
    turns = atoms // 2 // block
    shape = jax.ShapeDtypeStruct((tiles, atoms, LANES), jnp.bfloat16)
    spec = pl.BlockSpec(memory_space=pltpu.VMEM)
    return pl.pallas_call(
        functools.partial(bank_kernel, rows),
        in_specs=[pl.BlockSpec(memory_space=pl.ANY)],
        out_specs=[spec, spec],
        out_shape=[shape, shape],
        scratch_shapes=[
            pltpu.VMEM(atom_bank.shape, jnp.bfloat16),
            pltpu.VMEM((block * rows, LANES), jnp.float32),
            pltpu.SemaphoreType.DMA((turns, 2)),
        ],
        compiler_params=pltpu.CompilerParams(vmem_limit_bytes=24 * 1024 * 1024),
        name="bank_tiles",
    )(atom_bank)


def conv_kernel(transposed, steps, group, split, own_ref, halo_ref, even, odd, out_ref, base, spread, total):
    run, parts, width = own_ref.shape
    halo = halo_ref.shape[1]
    lanes = width // LANES

    own = own_ref[...].astype(jnp.float32)
    beside = halo_ref[...].astype(jnp.float32)
    if transposed:
        base[:, :parts] = own
        base[:, parts:] = beside
    else:
        base[:, :halo] = beside
        base[:, halo:] = own
    for shift in range(halo + 1):
        window = base[:, shift : shift + parts].astype(jnp.bfloat16)
        for lane in range(lanes):
            spread[lane, shift * run : (shift + 1) * run] = window[:, :, lane * LANES : (lane + 1) * LANES]

    total[...] = jnp.zeros_like(total)

    def block(step):
        def pair(ref, start):
            return jnp.concatenate([ref[start], ref[start + 1]], axis=1)

        return jnp.concatenate(
            [
                pair(even, 2 * step + 2),
                pair(odd, 2 * step + 1),
                pair(even, 2 * step + 1),
                pair(odd, 2 * step),
            ],
            axis=0,
        )

    def rows(step):
        start = step if transposed else halo * run - step
        return [
            spread[lane, pl.ds(start, run)].reshape(run * parts, LANES) for lane in range(lanes)
        ]

    def add(which, first, count):
        left = jnp.concatenate([part for i in range(count) for part in rows(first + i)], axis=1)
        if transposed:
            right = jnp.concatenate([block(first + i) for i in range(count)], axis=1)
            dims = (((1,), (1,)), ((), ()))
        else:
            right = jnp.concatenate([block(first + i) for i in range(count)], axis=0)
            dims = (((1,), (0,)), ((), ()))
        total[which] += lax.dot_general(left, right, dims, preferred_element_type=jnp.float32)

    cuts = [group * i // split for i in range(split + 1)]

    def loop(turn_index, carry):
        for i in range(split):
            add(i, turn_index * group + cuts[i], cuts[i + 1] - cuts[i])
        return carry

    turns = steps // group
    lax.fori_loop(0, turns, loop, 0)
    if steps > turns * group:
        add(0, turns * group, steps - turns * group)
    result = total[0]
    for i in range(1, split):
        result = result + total[i]
    out_ref[...] = result.reshape(out_ref.shape).astype(out_ref.dtype)


def convolve(own, halo, even, odd, transposed, group, split):
    run, parts, width = own.shape
    beside = halo.shape[1]
    tiles, atoms, _ = even.shape
    steps = (tiles - 4) // 2 + 1
    out_width = 2 * LANES if not transposed else PHASES * atoms
    flops = 2 * run * parts * width * out_width * steps
    return pl.pallas_call(
        functools.partial(conv_kernel, transposed, steps, group, split),
        in_specs=[pl.BlockSpec(memory_space=pltpu.VMEM)] * 4,
        out_specs=pl.BlockSpec(memory_space=pltpu.VMEM),
        out_shape=jax.ShapeDtypeStruct(
            (run, parts, out_width), jnp.float32 if transposed else jnp.bfloat16
        ),
        scratch_shapes=[
            pltpu.VMEM((run, parts + beside, width), jnp.float32),
            pltpu.VMEM((width // LANES, (beside + 1) * run, parts, LANES), jnp.bfloat16),
            pltpu.VMEM((split, run * parts, out_width), jnp.float32),
        ],
        compiler_params=pltpu.CompilerParams(vmem_limit_bytes=VMEM),
        cost_estimate=pl.CostEstimate(
            flops=flops, bytes_accessed=even.size * 4 + own.size * 8, transcendentals=0
        ),
        name="correlate" if transposed else "synthesize",
    )(own, halo, even, odd)


def shifted(value, axis, steps):
    count = lax.axis_size(axis)
    first, last = max(0, -steps), min(count, count - steps)
    return lax.ppermute(value, axis, [(i, i + steps) for i in range(first, last)])


def summed(value, axis):
    count = lax.axis_size(axis)
    step = 1
    while step < count:
        if step > 1:
            value = value.astype(jnp.bfloat16)
        other = lax.ppermute(value, axis, [(i, i ^ step) for i in range(count)])
        value = value.astype(jnp.float32) + other.astype(jnp.float32)
        step *= 2
    return value


def body(signal, codes_init, atom_bank, step_size, threshold):
    atoms, chans, taps = atom_bank.shape
    held = LANES // 2
    if chans < held:
        atom_bank = jnp.pad(atom_bank, ((0, 0), (0, held - chans), (0, 0)))
        signal = jnp.pad(signal, ((0, held - chans), (0, 0)))
    even, odd = bank_tiles(atom_bank)
    beside = taps // (RUN * PHASES)
    recorded = to_blocks(signal)
    current = to_blocks(codes_init)
    step = jnp.tile(step_size, PHASES)
    bound = jnp.tile(step_size * threshold, PHASES)
    for sweep in range(ITERS):
        shape = (16, 2) if sweep == 0 else (43, 2)
        lowered = current.astype(jnp.bfloat16)
        earlier = shifted(lowered[:, -beside:], "tm", 1)
        recon = summed(convolve(lowered, earlier, even, odd, False, *shape), "atom")
        misfit = recon - recorded.astype(jnp.float32)
        rounded = misfit.astype(jnp.bfloat16)
        following = shifted(rounded[:, :beside], "tm", -1)
        gradient = summed(convolve(rounded, following, even, odd, True, *shape), "chan")
        moved = current - step * gradient
        current = moved - jnp.clip(moved, -bound, bound)
    return from_blocks(current), from_blocks(misfit)[:chans]


def solution(mesh):
    placed = (P("chan", "tm"), P("atom", "tm"), P("atom", "chan", None), P("atom"), P("atom"))
    return jax.shard_map(
        body,
        mesh=mesh,
        in_specs=placed,
        out_specs=(P("atom", "tm"), P("chan", "tm")),
        check_vma=False,
    )
```

time: 130 us -> 96.2 us (0.74)
  Pallas kernels: 60.5 us -> 32.8 us
  waiting for transfers between devices: 38.7 us -> 28.1 us
  local copies, waits for them, and re-layouts: 7.35 us -> 15.8 us
  other arithmetic: 4.67 us -> 0.8 us
    pallas_call x5, Pallas kernels: 60.5 us -> 32.8 us  [the longest x4 24.4 us: convolve(): pl.pallas_call(functools.partial(conv_kernel, transposed, steps, group, s...]
    ppermute x6, waiting for transfers between devices: 27 us -> 16.2 us  [summed(): other = lax.ppermute(value, axis, [(i, i ^ step) for i in range(count)])]
    unnamed x26 -> x24, local copies, waits for them, and re-layouts: 5.6 us -> 14.1 us
    add x2 -> x0, other arithmetic: 1.98 us -> none  [summed(): value + lax.ppermute(value, axis, [(i, i ^ step) for i in range(count)])]
    convert_element_type x2, other arithmetic: 2.25 us -> 0.33 us  [body(): rounded = misfit.astype(jnp.bfloat16)]
  transfers between devices with their start and end apart: 10 -> 10, of which waited for: 9 -> 9; matrix products, arithmetic and copies ran while one was open for 1% -> 2% of each run, Pallas kernels for 13% -> 9%
where the time goes in v3:
time: 96.2 us; the launch traced here: 95.8 us
  Pallas kernels  32.8 us (34%)
  waiting for transfers between devices  28.1 us (29%)
  starting transfers between devices  17.4 us (18%)
  local copies, waits for them, and re-layouts  15.8 us (16%)
    pallas_call x4, Pallas kernels, convolve(): pl.pallas_call(functools.partial(conv_kernel, transposed, steps, group, s...  24.4 us
    ppermute x6, waiting for transfers between devices, summed(): other = lax.ppermute(value, axis, [(i, i ^ step) for i in range(count)])  16.2 us
    unnamed x24, local copies, waits for them, and re-layouts  14.1 us
    ppermute x4, waiting for transfers between devices, shifted(): lax.ppermute(value, axis, [(i, i + steps) for i in range(first, last)])  12 us
    ppermute x4, starting transfers between devices, shifted(): lax.ppermute(value, axis, [(i, i + steps) for i in range(first, last)])  11 us
    pallas_call x1, Pallas kernels, bank_tiles(): pl.pallas_call(functools.partial(bank_kernel, rows), in_specs=[pl.BlockSp...  8.43 us
    ppermute x6, starting transfers between devices, summed(): other = lax.ppermute(value, axis, [(i, i ^ step) for i in range(count)])  6.36 us
  transfers between devices with their start and end apart: 10, of which 9 were waited for; matrix products, arithmetic and copies ran while one was open for 2% of the time, Pallas kernels for 9%

profile of v3, /device:TPU:0, one launch (start us, length us, event | category | flops | bytes accessed | tf_op | source)
XLA Modules:
  0.0 95.8 jit_solution(6285413832804453798)
XLA Ops:
  0.6 1.1 %copy.11 = f32[64,1024]{0,1:T(8,128)S(1)} copy(f32[64,1024]{1,0:T(8,128)} %param.6) | data formatting | bytes 524288 | tf_op args[1]
  1.8 0.3 reshape.46
  2.1 0.1 copy.30.own_ref
  2.3 4.9 %collective-permute-start = (bf16[16,8,256]{2,1,0:T(8,128)(2,1)S(1)}, bf16[16,8,256]{2,1,0:T(8,128)(2,1)S(1)}, u32[]{:S(2)}, u32[]{:S(2)}) collective-permute-start(bf16[16,8,256]{2,1,0:T(8,128)(2,1)S(1)} %slice.16), channel_id=1, source_target_pairs={{0,8},{8,16},{16,24},{1,9},{9,17},{17,25},{2,10},{10,18},{18,26},{... | collective-permute-start | bytes 196616 | tf_op jit(solution)/shard_map/ppermute | solution.py:236
  7.2 2.2 %copy-done = bf16[64,64,512]{2,1,0:T(8,128)(2,1)S(1)} copy-done((bf16[64,64,512]{2,1,0:T(8,128)(2,1)S(1)}, bf16[64,64,512]{2,1,0:T(8,128)(2,1)}, u32[]{:S(2)}) %copy-start) | copy-done | bytes 4194328
  9.4 8.4 %bank_tiles.1 = (bf16[260,64,128]{2,1,0:T(8,128)(2,1)S(1)}, bf16[260,64,128]{2,1,0:T(8,128)(2,1)S(1)}) custom-call(bf16[64,64,512]{2,1,0:T(8,128)(2,1)S(1)} %copy-done), custom_call_target="tpu_custom_call" | custom-call | tf_op jit(solution)/shard_map/bank_tiles/pallas_call | solution.py:124
  17.9 6.5 %synthesize.2 = bf16[16,16,256]{2,1,0:T(8,128)(2,1)S(1)} custom-call(bf16[16,16,256]{2,1,0:T(8,128)(2,1)S(1)} %copy.30.own_ref, bf16[16,8,256]{2,1,0:T(8,128)(2,1)S(1)} %collective-permute-done.halo_ref, bf16[260,64,128]{2,1,0:T(8,128)(2,1)S(1)} %get-tuple-element.4.even, bf16[260,64,128]{2,1,0:T(8,128)(2,1)S(1)} %get-tuple-element.5.odd), custom_call_target="tpu_custom_call" | custom-call | flops 4328521728 | bytes 9043968 | tf_op jit(solution)/shard_map/synthesize/pallas_call | solution.py:213
  24.5 1.5 %collective-permute-start.1 = (bf16[16,16,256]{2,1,0:T(8,128)(2,1)S(1)}, bf16[16,16,256]{2,1,0:T(8,128)(2,1)S(1)}, u32[]{:S(2)}, u32[]{:S(2)}) collective-permute-start(bf16[16,16,256]{2,1,0:T(8,128)(2,1)S(1)} %synthesize.2), channel_id=1, source_target_pairs={{0,4},{4,0},{1,5},{5,1},{2,6},{6,2},{3,7},{7,3},{8,12},{12,8},{9,1... | collective-permute-start | bytes 393224 | tf_op jit(solution)/shard_map/ppermute | solution.py:245
  26.0 0.1 copy.21
  26.1 0.3 reshape.47
  26.5 3.0 %collective-permute-done.1 = bf16[16,16,256]{2,1,0:T(8,128)(2,1)S(1)} collective-permute-done((bf16[16,16,256]{2,1,0:T(8,128)(2,1)S(1)}, bf16[16,16,256]{2,1,0:T(8,128)(2,1)S(1)}, u32[]{:S(2)}, u32[]{:S(2)}) %collective-permute-start.1) | collective-permute-done | bytes 131104 | tf_op jit(solution)/shard_map/ppermute | solution.py:245
  29.5 0.2 subtract_convert_fusion.own_ref
  29.7 0.0 copy-start.8
  29.7 0.0 copy-start.9
  29.7 1.3 %collective-permute-start.2 = (bf16[16,8,256]{2,1,0:T(8,128)(2,1)S(1)}, bf16[16,8,256]{2,1,0:T(8,128)(2,1)S(1)}, u32[]{:S(2)}, u32[]{:S(2)}) collective-permute-start(bf16[16,8,256]{2,1,0:T(8,128)(2,1)S(1)} %slice.17), channel_id=1, source_target_pairs={{8,0},{16,8},{24,16},{9,1},{17,9},{25,17},{10,2},{18,10},{26,18},{... | collective-permute-start | bytes 196616 | tf_op jit(solution)/shard_map/ppermute | solution.py:236
  31.0 4.9 %collective-permute-done.2.halo_ref = bf16[16,8,256]{2,1,0:T(8,128)(2,1)S(1)} collective-permute-done((bf16[16,8,256]{2,1,0:T(8,128)(2,1)S(1)}, bf16[16,8,256]{2,1,0:T(8,128)(2,1)S(1)}, u32[]{:S(2)}, u32[]{:S(2)}) %collective-permute-start.2) | collective-permute-done | bytes 65568 | tf_op jit(solution)/shard_map/ppermute | solution.py:236
  35.9 2.2 %copy-done.2 = bf16[260,64,128]{2,1,0:T(8,128)(2,1)S(1)} copy-done((bf16[260,64,128]{2,1,0:T(8,128)(2,1)S(1)}, bf16[260,64,128]{2,1,0:T(8,128)(2,1)}, u32[]{:S(2)}) %copy-start.2) | copy-done | bytes 4259864
  38.1 2.2 %copy-done.5 = bf16[260,64,128]{2,1,0:T(8,128)(2,1)S(1)} copy-done((bf16[260,64,128]{2,1,0:T(8,128)(2,1)S(1)}, bf16[260,64,128]{2,1,0:T(8,128)(2,1)}, u32[]{:S(2)}) %copy-start.5) | copy-done | bytes 4259864
  40.3 6.7 %correlate.2 = f32[16,16,256]{2,1,0:T(8,128)S(1)} custom-call(bf16[16,16,256]{2,1,0:T(8,128)(2,1)S(1)} %subtract_convert_fusion.own_ref, bf16[16,8,256]{2,1,0:T(8,128)(2,1)S(1)} %collective-permute-done.2.halo_ref, bf16[260,64,128]{2,1,0:T(8,128)(2,1)S(1)} %copy-done.2, bf16[260,64,128]{2,1,0:T(8,128)(2,1)S(1)} %copy-done.5), custom_call_target="tpu_custom_call" | custom-call | flops 4328521728 | bytes 9043968 | tf_op jit(solution)/shard_map/correlate/pallas_call | solution.py:213
  47.0 0.1 collective-permute-start.3
  47.1 1.5 %collective-permute-done.3 = f32[16,16,256]{2,1,0:T(8,128)S(1)} collective-permute-done((f32[16,16,256]{2,1,0:T(8,128)S(1)}, f32[16,16,256]{2,1,0:T(8,128)S(1)}, u32[]{:S(2)}, u32[]{:S(2)}) %collective-permute-start.3) | collective-permute-done | bytes 262176 | tf_op jit(solution)/shard_map/ppermute | solution.py:245
  48.6 1.6 %collective-permute-start.4 = (bf16[16,16,256]{2,1,0:T(8,128)(2,1)S(1)}, bf16[16,16,256]{2,1,0:T(8,128)(2,1)S(1)}, u32[]{:S(2)}, u32[]{:S(2)}) collective-permute-start(bf16[16,16,256]{2,1,0:T(8,128)(2,1)S(1)} %add_convert_fusion.1), channel_id=1, source_target_pairs={{0,2},{1,3},{2,0},{3,1},{4,6},{5,7},{6,4},{7,5},{8,10},{9,11},{10,... | collective-permute-start | bytes 393224 | tf_op jit(solution)/shard_map/ppermute | solution.py:245
  50.2 0.1 min.20
  50.3 0.1 mul.19
  50.4 3.8 %collective-permute-done.4 = bf16[16,16,256]{2,1,0:T(8,128)(2,1)S(1)} collective-permute-done((bf16[16,16,256]{2,1,0:T(8,128)(2,1)S(1)}, bf16[16,16,256]{2,1,0:T(8,128)(2,1)S(1)}, u32[]{:S(2)}, u32[]{:S(2)}) %collective-permute-start.4) | collective-permute-done | bytes 131104 | tf_op jit(solution)/shard_map/ppermute | solution.py:245
  54.2 0.2 fusion.own_ref
  54.4 3.5 %collective-permute-start.5 = (bf16[16,8,256]{2,1,0:T(8,128)(2,1)S(1)}, bf16[16,8,256]{2,1,0:T(8,128)(2,1)S(1)}, u32[]{:S(2)}, u32[]{:S(2)}) collective-permute-start(bf16[16,8,256]{2,1,0:T(8,128)(2,1)S(1)} %slice.18), channel_id=1, source_target_pairs={{0,8},{8,16},{16,24},{1,9},{9,17},{17,25},{2,10},{10,18},{18,26},{... | collective-permute-start | bytes 196616 | tf_op jit(solution)/shard_map/ppermute | solution.py:236
  57.9 1.9 %collective-permute-done.5.halo_ref = bf16[16,8,256]{2,1,0:T(8,128)(2,1)S(1)} collective-permute-done((bf16[16,8,256]{2,1,0:T(8,128)(2,1)S(1)}, bf16[16,8,256]{2,1,0:T(8,128)(2,1)S(1)}, u32[]{:S(2)}, u32[]{:S(2)}) %collective-permute-start.5) | collective-permute-done | bytes 65568 | tf_op jit(solution)/shard_map/ppermute | solution.py:236
  59.8 2.2 %copy-done.3 = bf16[260,64,128]{2,1,0:T(8,128)(2,1)S(1)} copy-done((bf16[260,64,128]{2,1,0:T(8,128)(2,1)S(1)}, bf16[260,64,128]{2,1,0:T(8,128)(2,1)}, u32[]{:S(2)}) %copy-start.3) | copy-done | bytes 4259864
  62.0 2.2 %copy-done.6 = bf16[260,64,128]{2,1,0:T(8,128)(2,1)S(1)} copy-done((bf16[260,64,128]{2,1,0:T(8,128)(2,1)S(1)}, bf16[260,64,128]{2,1,0:T(8,128)(2,1)}, u32[]{:S(2)}) %copy-start.6) | copy-done | bytes 4259864
  64.2 5.5 %synthesize.3 = bf16[16,16,256]{2,1,0:T(8,128)(2,1)S(1)} custom-call(bf16[16,16,256]{2,1,0:T(8,128)(2,1)S(1)} %fusion.own_ref, bf16[16,8,256]{2,1,0:T(8,128)(2,1)S(1)} %collective-permute-done.5.halo_ref, bf16[260,64,128]{2,1,0:T(8,128)(2,1)S(1)} %copy-done.3, bf16[260,64,128]{2,1,0:T(8,128)(2,1)S(1)} %copy-done.6), custom_call_target="tpu_custom_call" | custom-call | flops 4328521728 | bytes 9043968 | tf_op jit(solution)/shard_map/synthesize/pallas_call | solution.py:213
  69.8 1.5 %collective-permute-start.6 = (bf16[16,16,256]{2,1,0:T(8,128)(2,1)S(1)}, bf16[16,16,256]{2,1,0:T(8,128)(2,1)S(1)}, u32[]{:S(2)}, u32[]{:S(2)}) collective-permute-start(bf16[16,16,256]{2,1,0:T(8,128)(2,1)S(1)} %synthesize.3), channel_id=1, source_target_pairs={{0,4},{4,0},{1,5},{5,1},{2,6},{6,2},{3,7},{7,3},{8,12},{12,8},{9,1... | collective-permute-start | bytes 393224 | tf_op jit(solution)/shard_map/ppermute | solution.py:245
  71.3 3.5 %collective-permute-done.6 = bf16[16,16,256]{2,1,0:T(8,128)(2,1)S(1)} collective-permute-done((bf16[16,16,256]{2,1,0:T(8,128)(2,1)S(1)}, bf16[16,16,256]{2,1,0:T(8,128)(2,1)S(1)}, u32[]{:S(2)}, u32[]{:S(2)}) %collective-permute-start.6) | collective-permute-done | bytes 131104 | tf_op jit(solution)/shard_map/ppermute | solution.py:245
  74.8 0.2 fusion.1
  75.0 1.3 %collective-permute-start.7 = (bf16[16,8,256]{2,1,0:T(8,128)(2,1)S(1)}, bf16[16,8,256]{2,1,0:T(8,128)(2,1)S(1)}, u32[]{:S(2)}, u32[]{:S(2)}) collective-permute-start(bf16[16,8,256]{2,1,0:T(8,128)(2,1)S(1)} %slice.19), channel_id=1, source_target_pairs={{8,0},{16,8},{24,16},{9,1},{17,9},{25,17},{10,2},{18,10},{26,18},{... | collective-permute-start | bytes 196616 | tf_op jit(solution)/shard_map/ppermute | solution.py:236
  76.3 5.2 %collective-permute-done.7.halo_ref = bf16[16,8,256]{2,1,0:T(8,128)(2,1)S(1)} collective-permute-done((bf16[16,8,256]{2,1,0:T(8,128)(2,1)S(1)}, bf16[16,8,256]{2,1,0:T(8,128)(2,1)S(1)}, u32[]{:S(2)}, u32[]{:S(2)}) %collective-permute-start.7) | collective-permute-done | bytes 65568 | tf_op jit(solution)/shard_map/ppermute | solution.py:236
  81.5 5.6 %correlate.3 = f32[16,16,256]{2,1,0:T(8,128)S(1)} custom-call(bf16[16,16,256]{2,1,0:T(8,128)(2,1)S(1)} %get-tuple-element.8.own_ref, bf16[16,8,256]{2,1,0:T(8,128)(2,1)S(1)} %collective-permute-done.7.halo_ref, bf16[260,64,128]{2,1,0:T(8,128)(2,1)S(1)} %copy-done.3, bf16[260,64,128]{2,1,0:T(8,128)(2,1)S(1)} %copy-done.6), custom_call_target="tpu_custom_call" | custom-call | flops 4328521728 | bytes 9043968 | tf_op jit(solution)/shard_map/correlate/pallas_call | solution.py:213
  87.1 0.1 collective-permute-start.8
  87.2 1.5 %collective-permute-done.8 = f32[16,16,256]{2,1,0:T(8,128)S(1)} collective-permute-done((f32[16,16,256]{2,1,0:T(8,128)S(1)}, f32[16,16,256]{2,1,0:T(8,128)S(1)}, u32[]{:S(2)}, u32[]{:S(2)}) %collective-permute-start.8) | collective-permute-done | bytes 262176 | tf_op jit(solution)/shard_map/ppermute | solution.py:245
  88.7 1.6 %collective-permute-start.9 = (bf16[16,16,256]{2,1,0:T(8,128)(2,1)S(1)}, bf16[16,16,256]{2,1,0:T(8,128)(2,1)S(1)}, u32[]{:S(2)}, u32[]{:S(2)}) collective-permute-start(bf16[16,16,256]{2,1,0:T(8,128)(2,1)S(1)} %add_convert_fusion), channel_id=1, source_target_pairs={{0,2},{1,3},{2,0},{3,1},{4,6},{5,7},{6,4},{7,5},{8,10},{9,11},{10,... | collective-permute-start | bytes 393224 | tf_op jit(solution)/shard_map/ppermute | solution.py:245
  90.3 0.2 reshape.42
  90.6 0.1 copy.16
  90.7 0.9 copy.18
  91.6 2.8 %collective-permute-done.9 = bf16[16,16,256]{2,1,0:T(8,128)(2,1)S(1)} collective-permute-done((bf16[16,16,256]{2,1,0:T(8,128)(2,1)S(1)}, bf16[16,16,256]{2,1,0:T(8,128)(2,1)S(1)}, u32[]{:S(2)}, u32[]{:S(2)}) %collective-permute-start.9) | collective-permute-done | bytes 131104 | tf_op jit(solution)/shard_map/ppermute | solution.py:245
  94.3 0.2 minimum_subtract_fusion
  94.5 0.2 reshape.40
  94.8 0.1 copy.15
  94.9 0.9 copy.17
  (24 shorter events, 0.2 us)
Async XLA Ops:
  2.3 15.6 %collective-permute-start = (bf16[16,8,256]{2,1,0:T(8,128)(2,1)S(1)}, bf16[16,8,256]{2,1,0:T(8,128)(2,1)S(1)}, u32[]{:S(2)}, u32[]{:S(2)}) collective-permute-start(bf16[16,8,256]{2,1,0:T(8,128)(2,1)S(1)} %slice.16), channel_id=1, source_target_pairs={{0,8},{8,16},{16,24},{1,9},{9,17},{17,25},{2,10},{10,18},{18,26},{... | collective-permute-start | bytes 196616 | tf_op jit(solution)/shard_map/ppermute | solution.py:236
  7.2 2.2 %copy-start = (bf16[64,64,512]{2,1,0:T(8,128)(2,1)S(1)}, bf16[64,64,512]{2,1,0:T(8,128)(2,1)}, u32[]{:S(2)}) copy-start(bf16[64,64,512]{2,1,0:T(8,128)(2,1)} %bank_hbm.1) | copy-start | bytes 12582916
  17.9 6.6 %copy-start.1 = (bf16[260,64,128]{2,1,0:T(8,128)(2,1)}, bf16[260,64,128]{2,1,0:T(8,128)(2,1)S(1)}, u32[]{:S(2)}) copy-start(bf16[260,64,128]{2,1,0:T(8,128)(2,1)S(1)} %get-tuple-element.4.even) | copy-start | bytes 12779524
  17.9 6.6 %copy-start.4 = (bf16[260,64,128]{2,1,0:T(8,128)(2,1)}, bf16[260,64,128]{2,1,0:T(8,128)(2,1)S(1)}, u32[]{:S(2)}) copy-start(bf16[260,64,128]{2,1,0:T(8,128)(2,1)S(1)} %get-tuple-element.5.odd) | copy-start | bytes 12779524
  17.9 8.1 %copy-start.7 = (bf16[64,1024]{1,0:T(8,128)(2,1)S(1)}, bf16[64,1024]{1,0:T(8,128)(2,1)}, u32[]{:S(2)}) copy-start(bf16[64,1024]{1,0:T(8,128)(2,1)} %param.5) | copy-start | bytes 393220
  24.5 5.0 %collective-permute-start.1 = (bf16[16,16,256]{2,1,0:T(8,128)(2,1)S(1)}, bf16[16,16,256]{2,1,0:T(8,128)(2,1)S(1)}, u32[]{:S(2)}, u32[]{:S(2)}) collective-permute-start(bf16[16,16,256]{2,1,0:T(8,128)(2,1)S(1)} %synthesize.2), channel_id=1, source_target_pairs={{0,4},{4,0},{1,5},{5,1},{2,6},{6,2},{3,7},{7,3},{8,12},{12,8},{9,1... | collective-permute-start | bytes 393224 | tf_op jit(solution)/shard_map/ppermute | solution.py:245
  29.7 20.6 %copy-start.8 = (f32[64]{0:T(128)S(1)}, f32[64]{0:T(128)}, u32[]{:S(2)}) copy-start(f32[64]{0:T(128)} %param.8) | copy-start | bytes 772
  29.7 20.6 %copy-start.9 = (f32[64]{0:T(128)S(1)}, f32[64]{0:T(128)}, u32[]{:S(2)}) copy-start(f32[64]{0:T(128)} %param.9) | copy-start | bytes 772
  29.7 6.2 %collective-permute-start.2 = (bf16[16,8,256]{2,1,0:T(8,128)(2,1)S(1)}, bf16[16,8,256]{2,1,0:T(8,128)(2,1)S(1)}, u32[]{:S(2)}, u32[]{:S(2)}) collective-permute-start(bf16[16,8,256]{2,1,0:T(8,128)(2,1)S(1)} %slice.17), channel_id=1, source_target_pairs={{8,0},{16,8},{24,16},{9,1},{17,9},{25,17},{10,2},{18,10},{26,18},{... | collective-permute-start | bytes 196616 | tf_op jit(solution)/shard_map/ppermute | solution.py:236
  35.9 2.2 %copy-start.2 = (bf16[260,64,128]{2,1,0:T(8,128)(2,1)S(1)}, bf16[260,64,128]{2,1,0:T(8,128)(2,1)}, u32[]{:S(2)}) copy-start(bf16[260,64,128]{2,1,0:T(8,128)(2,1)} %copy-done.1) | copy-start | bytes 12779524
  38.1 2.2 %copy-start.5 = (bf16[260,64,128]{2,1,0:T(8,128)(2,1)S(1)}, bf16[260,64,128]{2,1,0:T(8,128)(2,1)}, u32[]{:S(2)}) copy-start(bf16[260,64,128]{2,1,0:T(8,128)(2,1)} %copy-done.4) | copy-start | bytes 12779524
  47.0 1.6 %collective-permute-start.3 = (f32[16,16,256]{2,1,0:T(8,128)S(1)}, f32[16,16,256]{2,1,0:T(8,128)S(1)}, u32[]{:S(2)}, u32[]{:S(2)}) collective-permute-start(f32[16,16,256]{2,1,0:T(8,128)S(1)} %correlate.2), channel_id=1, source_target_pairs={{0,1},{1,0},{2,3},{3,2},{4,5},{5,4},{6,7},{7,6},{8,9},{9,8},{10,11... | collective-permute-start | bytes 786440 | tf_op jit(solution)/shard_map/ppermute | solution.py:245
  48.6 5.6 %collective-permute-start.4 = (bf16[16,16,256]{2,1,0:T(8,128)(2,1)S(1)}, bf16[16,16,256]{2,1,0:T(8,128)(2,1)S(1)}, u32[]{:S(2)}, u32[]{:S(2)}) collective-permute-start(bf16[16,16,256]{2,1,0:T(8,128)(2,1)S(1)} %add_convert_fusion.1), channel_id=1, source_target_pairs={{0,2},{1,3},{2,0},{3,1},{4,6},{5,7},{6,4},{7,5},{8,10},{9,11},{10,... | collective-permute-start | bytes 393224 | tf_op jit(solution)/shard_map/ppermute | solution.py:245
  54.4 5.4 %collective-permute-start.5 = (bf16[16,8,256]{2,1,0:T(8,128)(2,1)S(1)}, bf16[16,8,256]{2,1,0:T(8,128)(2,1)S(1)}, u32[]{:S(2)}, u32[]{:S(2)}) collective-permute-start(bf16[16,8,256]{2,1,0:T(8,128)(2,1)S(1)} %slice.18), channel_id=1, source_target_pairs={{0,8},{8,16},{16,24},{1,9},{9,17},{17,25},{2,10},{10,18},{18,26},{... | collective-permute-start | bytes 196616 | tf_op jit(solution)/shard_map/ppermute | solution.py:236
  59.8 2.2 %copy-start.3 = (bf16[260,64,128]{2,1,0:T(8,128)(2,1)S(1)}, bf16[260,64,128]{2,1,0:T(8,128)(2,1)}, u32[]{:S(2)}) copy-start(bf16[260,64,128]{2,1,0:T(8,128)(2,1)} %copy-done.1) | copy-start | bytes 12779524
  62.0 2.2 %copy-start.6 = (bf16[260,64,128]{2,1,0:T(8,128)(2,1)S(1)}, bf16[260,64,128]{2,1,0:T(8,128)(2,1)}, u32[]{:S(2)}) copy-start(bf16[260,64,128]{2,1,0:T(8,128)(2,1)} %copy-done.4) | copy-start | bytes 12779524
  69.8 5.0 %collective-permute-start.6 = (bf16[16,16,256]{2,1,0:T(8,128)(2,1)S(1)}, bf16[16,16,256]{2,1,0:T(8,128)(2,1)S(1)}, u32[]{:S(2)}, u32[]{:S(2)}) collective-permute-start(bf16[16,16,256]{2,1,0:T(8,128)(2,1)S(1)} %synthesize.3), channel_id=1, source_target_pairs={{0,4},{4,0},{1,5},{5,1},{2,6},{6,2},{3,7},{7,3},{8,12},{12,8},{9,1... | collective-permute-start | bytes 393224 | tf_op jit(solution)/shard_map/ppermute | solution.py:245
  75.0 6.5 %collective-permute-start.7 = (bf16[16,8,256]{2,1,0:T(8,128)(2,1)S(1)}, bf16[16,8,256]{2,1,0:T(8,128)(2,1)S(1)}, u32[]{:S(2)}, u32[]{:S(2)}) collective-permute-start(bf16[16,8,256]{2,1,0:T(8,128)(2,1)S(1)} %slice.19), channel_id=1, source_target_pairs={{8,0},{16,8},{24,16},{9,1},{17,9},{25,17},{10,2},{18,10},{26,18},{... | collective-permute-start | bytes 196616 | tf_op jit(solution)/shard_map/ppermute | solution.py:236
  87.1 1.6 %collective-permute-start.8 = (f32[16,16,256]{2,1,0:T(8,128)S(1)}, f32[16,16,256]{2,1,0:T(8,128)S(1)}, u32[]{:S(2)}, u32[]{:S(2)}) collective-permute-start(f32[16,16,256]{2,1,0:T(8,128)S(1)} %correlate.3), channel_id=1, source_target_pairs={{0,1},{1,0},{2,3},{3,2},{4,5},{5,4},{6,7},{7,6},{8,9},{9,8},{10,11... | collective-permute-start | bytes 786440 | tf_op jit(solution)/shard_map/ppermute | solution.py:245
  88.7 5.6 %collective-permute-start.9 = (bf16[16,16,256]{2,1,0:T(8,128)(2,1)S(1)}, bf16[16,16,256]{2,1,0:T(8,128)(2,1)S(1)}, u32[]{:S(2)}, u32[]{:S(2)}) collective-permute-start(bf16[16,16,256]{2,1,0:T(8,128)(2,1)S(1)} %add_convert_fusion), channel_id=1, source_target_pairs={{0,2},{1,3},{2,0},{3,1},{4,6},{5,7},{6,4},{7,5},{8,10},{9,11},{10,... | collective-permute-start | bytes 393224 | tf_op jit(solution)/shard_map/ppermute | solution.py:245

commit v4 on v3

--- a/solution.py
+++ b/solution.py
@@ -9,29 +9,78 @@
 
 ITERS = 2
 PHASES = 4
-RUN = 16
+PARTS = 16
 LANES = 128
 VMEM = 24 * 1024 * 1024
 
 
-def to_blocks(value):
-    rows, slab = value.shape
-    parts = slab // (RUN * PHASES)
-    return (
-        value.reshape(rows, parts, RUN, PHASES)
-        .transpose(2, 1, 3, 0)
-        .reshape(RUN, parts, PHASES * rows)
-    )
-
-
-def from_blocks(value):
-    run, parts, width = value.shape
-    rows = width // PHASES
-    return (
-        value.reshape(run, parts, PHASES, rows)
-        .transpose(3, 1, 0, 2)
-        .reshape(rows, parts * run * PHASES)
-    )
+def blocks_kernel(count, *refs):
+    values, outs, flat = refs[:count], refs[count:-1], refs[-1]
+    for index, value_ref in enumerate(values):
+        halves = outs[2 * index : 2 * index + 2]
+        rows, slab = value_ref.shape
+        run, parts, _ = halves[0].shape
+        length = run * PHASES
+        pitch = length + 1
+        value = value_ref[...].astype(jnp.float32)
+        turned = jnp.concatenate([value, value], axis=0).T
+        for part in range(slab // length):
+            flat[part * pitch : part * pitch + length] = turned[part * length : (part + 1) * length]
+        low = lax.broadcasted_iota(jnp.int32, (parts, LANES), 1) < rows
+        for half, out in enumerate(halves):
+            for q in range(run):
+                first = half * parts * pitch + q * PHASES
+                phases = [flat[pl.ds(first + s, parts, stride=pitch), :] for s in range(PHASES)]
+                out[q] = jnp.concatenate(
+                    [jnp.where(low, phases[s], phases[s + 1]) for s in range(0, PHASES, 2)], axis=1
+                )
+
+
+def to_blocks(taps, *values):
+    run = taps // (PHASES * PARTS)
+    half = jax.ShapeDtypeStruct((run, PARTS, PHASES * LANES // 2), jnp.float32)
+    slab = values[0].shape[1]
+    return pl.pallas_call(
+        functools.partial(blocks_kernel, len(values)),
+        in_specs=[pl.BlockSpec(memory_space=pltpu.VMEM)] * len(values),
+        out_specs=[pl.BlockSpec(memory_space=pltpu.VMEM)] * (2 * len(values)),
+        out_shape=[half] * (2 * len(values)),
+        scratch_shapes=[pltpu.VMEM((slab + slab // (run * PHASES) + 7, LANES), jnp.float32)],
+        compiler_params=pltpu.CompilerParams(vmem_limit_bytes=VMEM),
+        name="to_blocks",
+    )(*values)
+
+
+def series_kernel(low_ref, high_ref, out_ref, flat):
+    rows, slab = out_ref.shape
+    run, parts, _ = low_ref.shape
+    length = run * PHASES
+    pitch = length + 1
+    for half, value_ref in enumerate((low_ref, high_ref)):
+        for q in range(run):
+            first = half * parts * pitch + q * PHASES
+            for s in range(0, PHASES, 2):
+                pair = value_ref[q, :, s // 2 * LANES : (s // 2 + 1) * LANES]
+                flat[pl.ds(first + s, parts, stride=pitch), :] = pair
+                flat[pl.ds(first + s + 1, parts, stride=pitch), :] = pltpu.roll(pair, LANES // 2, 1)
+    turned = jnp.concatenate(
+        [flat[part * pitch : part * pitch + length] for part in range(slab // length)], axis=0
+    ).T
+    out_ref[...] = turned[:rows]
+
+
+def from_blocks(low, high):
+    run, parts, width = low.shape
+    slab = 2 * run * parts * PHASES
+    return pl.pallas_call(
+        series_kernel,
+        in_specs=[pl.BlockSpec(memory_space=pltpu.VMEM)] * 2,
+        out_specs=pl.BlockSpec(memory_space=pltpu.VMEM),
+        out_shape=jax.ShapeDtypeStruct((width // PHASES, slab), jnp.float32),
+        scratch_shapes=[pltpu.VMEM((slab + slab // (run * PHASES) + 7, LANES), jnp.float32)],
+        compiler_params=pltpu.CompilerParams(vmem_limit_bytes=VMEM),
+        name="from_blocks",
+    )(low, high)
 
 
 def bank_kernel(rows, bank_hbm, even_ref, odd_ref, bank, flat, sems):
@@ -136,25 +185,18 @@
     )(atom_bank)
 
 
-def conv_kernel(transposed, steps, group, split, own_ref, halo_ref, even, odd, out_ref, base, spread, total):
+def conv_kernel(transposed, steps, group, own_ref, beside_ref, even, odd, out_ref, base, spread, total):
     run, parts, width = own_ref.shape
-    halo = halo_ref.shape[1]
     lanes = width // LANES
 
-    own = own_ref[...].astype(jnp.float32)
-    beside = halo_ref[...].astype(jnp.float32)
-    if transposed:
-        base[:, :parts] = own
-        base[:, parts:] = beside
-    else:
-        base[:, :halo] = beside
-        base[:, halo:] = own
-    for shift in range(halo + 1):
+    first, second = (own_ref, beside_ref) if transposed else (beside_ref, own_ref)
+    base[:, :parts] = first[...].astype(jnp.float32)
+    base[:, parts:] = second[...].astype(jnp.float32)
+
+    def fill(shift):
         window = base[:, shift : shift + parts].astype(jnp.bfloat16)
         for lane in range(lanes):
             spread[lane, shift * run : (shift + 1) * run] = window[:, :, lane * LANES : (lane + 1) * LANES]
-
-    total[...] = jnp.zeros_like(total)
 
     def block(step):
         def pair(ref, start):
@@ -171,12 +213,12 @@
         )
 
     def rows(step):
-        start = step if transposed else halo * run - step
+        start = step if transposed else parts * run - step
         return [
             spread[lane, pl.ds(start, run)].reshape(run * parts, LANES) for lane in range(lanes)
         ]
 
-    def add(which, first, count):
+    def product(first, count):
         left = jnp.concatenate([part for i in range(count) for part in rows(first + i)], axis=1)
         if transposed:
             right = jnp.concatenate([block(first + i) for i in range(count)], axis=1)
@@ -184,50 +226,58 @@
         else:
             right = jnp.concatenate([block(first + i) for i in range(count)], axis=0)
             dims = (((1,), (0,)), ((), ()))
-        total[which] += lax.dot_general(left, right, dims, preferred_element_type=jnp.float32)
-
-    cuts = [group * i // split for i in range(split + 1)]
-
-    def loop(turn_index, carry):
-        for i in range(split):
-            add(i, turn_index * group + cuts[i], cuts[i + 1] - cuts[i])
-        return carry
-
-    turns = steps // group
-    lax.fori_loop(0, turns, loop, 0)
-    if steps > turns * group:
-        add(0, turns * group, steps - turns * group)
-    result = total[0]
-    for i in range(1, split):
-        result = result + total[i]
-    out_ref[...] = result.reshape(out_ref.shape).astype(out_ref.dtype)
-
-
-def convolve(own, halo, even, odd, transposed, group, split):
+        return lax.dot_general(left, right, dims, preferred_element_type=jnp.float32)
+
+    order = list(range(parts + 1)) if transposed else list(range(parts, -1, -1))
+    if group is None:
+        fill(order[0])
+        total[0] = product(0, 1)
+        total[1] = jnp.zeros_like(total[1])
+        for turn in range(parts):
+            fill(order[turn + 1])
+            total[turn % 2] += product(1 + turn * run, run)
+    else:
+        for shift in order:
+            fill(shift)
+        total[...] = jnp.zeros_like(total)
+
+        def loop(turn, carry):
+            near = group // 2
+            total[0] += product(turn * group, near)
+            total[1] += product(turn * group + near, group - near)
+            return carry
+
+        turns = steps // group
+        lax.fori_loop(0, turns, loop, 0)
+        if steps > turns * group:
+            total[0] += product(turns * group, steps - turns * group)
+    out_ref[...] = (total[0] + total[1]).reshape(out_ref.shape).astype(out_ref.dtype)
+
+
+def convolve(own, beside, even, odd, transposed, group):
     run, parts, width = own.shape
-    beside = halo.shape[1]
     tiles, atoms, _ = even.shape
-    steps = (tiles - 4) // 2 + 1
-    out_width = 2 * LANES if not transposed else PHASES * atoms
+    steps = run * parts + 1
+    out_width = PHASES * atoms if transposed else 2 * LANES
     flops = 2 * run * parts * width * out_width * steps
     return pl.pallas_call(
-        functools.partial(conv_kernel, transposed, steps, group, split),
+        functools.partial(conv_kernel, transposed, steps, group),
         in_specs=[pl.BlockSpec(memory_space=pltpu.VMEM)] * 4,
         out_specs=pl.BlockSpec(memory_space=pltpu.VMEM),
         out_shape=jax.ShapeDtypeStruct(
             (run, parts, out_width), jnp.float32 if transposed else jnp.bfloat16
         ),
         scratch_shapes=[
-            pltpu.VMEM((run, parts + beside, width), jnp.float32),
-            pltpu.VMEM((width // LANES, (beside + 1) * run, parts, LANES), jnp.bfloat16),
-            pltpu.VMEM((split, run * parts, out_width), jnp.float32),
+            pltpu.VMEM((run, 2 * parts, width), jnp.float32),
+            pltpu.VMEM((width // LANES, (parts + 1) * run, parts, LANES), jnp.bfloat16),
+            pltpu.VMEM((2, run * parts, out_width), jnp.float32),
         ],
         compiler_params=pltpu.CompilerParams(vmem_limit_bytes=VMEM),
         cost_estimate=pl.CostEstimate(
             flops=flops, bytes_accessed=even.size * 4 + own.size * 8, transcendentals=0
         ),
         name="correlate" if transposed else "synthesize",
-    )(own, halo, even, odd)
+    )(own, beside, even, odd)
 
 
 def shifted(value, axis, steps):
@@ -254,24 +304,31 @@
     if chans < held:
         atom_bank = jnp.pad(atom_bank, ((0, 0), (0, held - chans), (0, 0)))
         signal = jnp.pad(signal, ((0, held - chans), (0, 0)))
+    low, high, heard_low, heard_high = to_blocks(taps, codes_init, signal)
     even, odd = bank_tiles(atom_bank)
-    beside = taps // (RUN * PHASES)
-    recorded = to_blocks(signal)
-    current = to_blocks(codes_init)
-    step = jnp.tile(step_size, PHASES)
-    bound = jnp.tile(step_size * threshold, PHASES)
+    step = jnp.concatenate([step_size] * PHASES)
+    bound = jnp.concatenate([step_size * threshold] * PHASES)
+
+    def shrink(current, gradient):
+        moved = current - step * gradient
+        return moved - jnp.clip(moved, -bound, bound)
+
     for sweep in range(ITERS):
-        shape = (16, 2) if sweep == 0 else (43, 2)
-        lowered = current.astype(jnp.bfloat16)
-        earlier = shifted(lowered[:, -beside:], "tm", 1)
-        recon = summed(convolve(lowered, earlier, even, odd, False, *shape), "atom")
-        misfit = recon - recorded.astype(jnp.float32)
-        rounded = misfit.astype(jnp.bfloat16)
-        following = shifted(rounded[:, :beside], "tm", -1)
-        gradient = summed(convolve(rounded, following, even, odd, True, *shape), "chan")
-        moved = current - step * gradient
-        current = moved - jnp.clip(moved, -bound, bound)
-    return from_blocks(current), from_blocks(misfit)[:chans]
+        group = None if sweep == 0 else 43
+        low16, high16 = low.astype(jnp.bfloat16), high.astype(jnp.bfloat16)
+        earlier = shifted(high16, "tm", 1)
+        recon_high = summed(convolve(high16, low16, even, odd, False, group), "atom")
+        recon_low = summed(convolve(low16, earlier, even, odd, False, group), "atom")
+        misfit_high = recon_high - heard_high
+        misfit_low = recon_low - heard_low
+        rounded_high = misfit_high.astype(jnp.bfloat16)
+        rounded_low = misfit_low.astype(jnp.bfloat16)
+        following = shifted(rounded_low, "tm", -1)
+        gradient_low = summed(convolve(rounded_low, rounded_high, even, odd, True, group), "chan")
+        gradient_high = summed(convolve(rounded_high, following, even, odd, True, group), "chan")
+        low = shrink(low, gradient_low)
+        high = shrink(high, gradient_high)
+    return from_blocks(low, high), from_blocks(misfit_low, misfit_high)[:chans]
 
 
 def solution(mesh):

time: 96.2 us -> 87 us (0.904)
  waiting for transfers between devices: 28.1 us -> 12.1 us
  Pallas kernels: 32.8 us -> 46.2 us
  local copies, waits for them, and re-layouts: 15.8 us -> 4.04 us
  starting transfers between devices: 17.4 us -> 22.9 us
    pallas_call x4 -> x11, Pallas kernels: 24.4 us -> 37.8 us  [the longest x8 35.5 us: convolve(): pl.pallas_call(functools.partial(conv_kernel, transposed, steps, group),...]
    ppermute x4, waiting for transfers between devices: 12 us -> 0.01 us  [shifted(): lax.ppermute(value, axis, [(i, i + steps) for i in range(first, last)])]
    unnamed x24 -> x10, local copies, waits for them, and re-layouts: 14.1 us -> 4.04 us
    ppermute x6 -> x12, starting transfers between devices: 6.36 us -> 10.4 us  [summed(): other = lax.ppermute(value, axis, [(i, i ^ step) for i in range(count)])]
    ppermute x6 -> x12, waiting for transfers between devices: 16.2 us -> 12.1 us  [summed(): other = lax.ppermute(value, axis, [(i, i ^ step) for i in range(count)])]
    ppermute x4, starting transfers between devices: 11 us -> 12.5 us  [shifted(): lax.ppermute(value, axis, [(i, i + steps) for i in range(first, last)])]
    reshape x6 -> x0, local copies, waits for them, and re-layouts: 1.21 us -> none  [the longest x4 0.72 us: from_blocks(): value.reshape(run, parts, PHASES, rows).transpose(3, 1, 0, 2)]
  transfers between devices with their start and end apart: 10 -> 16, of which waited for: 9 -> 6; matrix products, arithmetic and copies ran while one was open for 2% -> 0% of each run, Pallas kernels for 9% -> 52%
where the time goes in v4:
time: 87 us; the launch traced here: 86.7 us
  Pallas kernels  46.2 us (53%)
  starting transfers between devices  22.9 us (26%)
  waiting for transfers between devices  12.1 us (14%)
  local copies, waits for them, and re-layouts  4.04 us (5%)
    pallas_call x8, Pallas kernels, convolve(): pl.pallas_call(functools.partial(conv_kernel, transposed, steps, group),...  35.5 us
    ppermute x4, starting transfers between devices, shifted(): lax.ppermute(value, axis, [(i, i + steps) for i in range(first, last)])  12.5 us
    ppermute x12, waiting for transfers between devices, summed(): other = lax.ppermute(value, axis, [(i, i ^ step) for i in range(count)])  12.1 us
    ppermute x12, starting transfers between devices, summed(): other = lax.ppermute(value, axis, [(i, i ^ step) for i in range(count)])  10.4 us
    pallas_call x1, Pallas kernels, bank_tiles(): pl.pallas_call(functools.partial(bank_kernel, rows), in_specs=[pl.BlockSp...  8.4 us
    unnamed x10, local copies, waits for them, and re-layouts  4.04 us
    pallas_call x2, Pallas kernels, from_blocks(): pl.pallas_call(series_kernel, in_specs=[pl.BlockSpec(memory_space=pltpu.V...  2 us
  transfers between devices with their start and end apart: 16, of which 6 were waited for; matrix products, arithmetic and copies ran while one was open for 0% of the time, Pallas kernels for 52%

profile of v4, /device:TPU:0, one launch (start us, length us, event | category | flops | bytes accessed | tf_op | source)
XLA Modules:
  0.0 86.7 jit_solution(10093919873972851865)
XLA Ops:
  0.6 0.9 %copy-done.1 = f32[64,1024]{1,0:T(8,128)S(1)} copy-done((f32[64,1024]{1,0:T(8,128)S(1)}, f32[64,1024]{1,0:T(8,128)}, u32[]{:S(2)}) %copy-start.1) | copy-done | bytes 262168
  1.6 0.9 %copy-done.2 = bf16[64,1024]{1,0:T(8,128)(2,1)S(1)} copy-done((bf16[64,1024]{1,0:T(8,128)(2,1)S(1)}, bf16[64,1024]{1,0:T(8,128)(2,1)}, u32[]{:S(2)}) %copy-start.2) | copy-done | bytes 131096
  2.5 0.3 to_blocks.1
  2.8 4.9 %collective-permute-start = (bf16[8,16,256]{2,1,0:T(8,128)(2,1)S(1)}, bf16[8,16,256]{2,1,0:T(8,128)(2,1)S(1)}, u32[]{:S(2)}, u32[]{:S(2)}) collective-permute-start(bf16[8,16,256]{2,1,0:T(8,128)(2,1)S(1)} %convert_element_type.85.own_ref), channel_id=1, source_target_pairs={{0,8},{8,16},{16,24},{1,9},{9,17},{17,25},{2,10},{10,18},{18,26},{... | collective-permute-start | bytes 196616 | tf_op jit(solution)/shard_map/ppermute | solution.py:286
  7.8 0.0 copy-start
  7.8 2.2 %copy-done = bf16[64,64,512]{2,1,0:T(8,128)(2,1)S(1)} copy-done((bf16[64,64,512]{2,1,0:T(8,128)(2,1)S(1)}, bf16[64,64,512]{2,1,0:T(8,128)(2,1)}, u32[]{:S(2)}) %copy-start) | copy-done | bytes 4194328
  10.0 8.4 %bank_tiles.1 = (bf16[260,64,128]{2,1,0:T(8,128)(2,1)S(1)}, bf16[260,64,128]{2,1,0:T(8,128)(2,1)S(1)}) custom-call(bf16[64,64,512]{2,1,0:T(8,128)(2,1)S(1)} %copy-done), custom_call_target="tpu_custom_call" | custom-call | tf_op jit(solution)/shard_map/bank_tiles/pallas_call | solution.py:173
  18.4 0.0 copy-start.3
  18.4 0.0 copy-start.4
  18.4 2.4 %synthesize.5 = bf16[8,16,256]{2,1,0:T(8,128)(2,1)S(1)} custom-call(bf16[8,16,256]{2,1,0:T(8,128)(2,1)S(1)} %convert_element_type.85.own_ref, bf16[8,16,256]{2,1,0:T(8,128)(2,1)S(1)} %convert_element_type.84.own_ref.beside_ref, bf16[260,64,128]{2,1,0:T(8,128)(2,1)S(1)} %get-tuple-element.10.even, bf16[260,64,128]{2,1,0:T(8,128)(2,1)S(1)} %get-tuple-element.11.odd), custom_call_target="tpu_custom_call" | custom-call | flops 2164260864 | bytes 8781824 | tf_op jit(solution)/shard_map/synthesize/pallas_call | solution.py:263
  20.8 1.6 %collective-permute-start.2 = (bf16[8,16,256]{2,1,0:T(8,128)(2,1)S(1)}, bf16[8,16,256]{2,1,0:T(8,128)(2,1)S(1)}, u32[]{:S(2)}, u32[]{:S(2)}) collective-permute-start(bf16[8,16,256]{2,1,0:T(8,128)(2,1)S(1)} %synthesize.5), channel_id=1, source_target_pairs={{0,4},{4,0},{1,5},{5,1},{2,6},{6,2},{3,7},{7,3},{8,12},{12,8},{9,1... | collective-permute-start | bytes 196616 | tf_op jit(solution)/shard_map/ppermute | solution.py:295
  22.4 0.1 fusion.4
  22.5 0.0 collective-permute-done.beside_ref
  22.5 2.4 %synthesize.4 = bf16[8,16,256]{2,1,0:T(8,128)(2,1)S(1)} custom-call(bf16[8,16,256]{2,1,0:T(8,128)(2,1)S(1)} %convert_element_type.84.own_ref.beside_ref, bf16[8,16,256]{2,1,0:T(8,128)(2,1)S(1)} %collective-permute-done.beside_ref, bf16[260,64,128]{2,1,0:T(8,128)(2,1)S(1)} %get-tuple-element.10.even, bf16[260,64,128]{2,1,0:T(8,128)(2,1)S(1)} %get-tuple-element.11.odd), custom_call_target="tpu_custom_call" | custom-call | flops 2164260864 | bytes 8781824 | tf_op jit(solution)/shard_map/synthesize/pallas_call | solution.py:263
  24.9 0.6 collective-permute-start.1
  25.4 0.0 collective-permute-done.2
  25.5 3.7 %collective-permute-done.1 = bf16[8,16,256]{2,1,0:T(8,128)(2,1)S(1)} collective-permute-done((bf16[8,16,256]{2,1,0:T(8,128)(2,1)S(1)}, bf16[8,16,256]{2,1,0:T(8,128)(2,1)S(1)}, u32[]{:S(2)}, u32[]{:S(2)}) %collective-permute-start.1) | collective-permute-done | bytes 65568 | tf_op jit(solution)/shard_map/ppermute | solution.py:295
  29.2 1.5 %collective-permute-start.5 = (bf16[8,16,256]{2,1,0:T(8,128)(2,1)S(1)}, bf16[8,16,256]{2,1,0:T(8,128)(2,1)S(1)}, u32[]{:S(2)}, u32[]{:S(2)}) collective-permute-start(bf16[8,16,256]{2,1,0:T(8,128)(2,1)S(1)} %subtract_convert_fusion.1.own_ref), channel_id=1, source_target_pairs={{8,0},{16,8},{24,16},{9,1},{17,9},{25,17},{10,2},{18,10},{26,18},{... | collective-permute-start | bytes 196616 | tf_op jit(solution)/shard_map/ppermute | solution.py:286
  30.7 5.6 %correlate.4 = f32[8,16,256]{2,1,0:T(8,128)S(1)} custom-call(bf16[8,16,256]{2,1,0:T(8,128)(2,1)S(1)} %subtract_convert_fusion.1.own_ref, bf16[8,16,256]{2,1,0:T(8,128)(2,1)S(1)} %subtract_convert_fusion.beside_ref.own_ref, bf16[260,64,128]{2,1,0:T(8,128)(2,1)S(1)} %get-tuple-element.10.even, bf16[260,64,128]{2,1,0:T(8,128)(2,1)S(1)} %get-tuple-element.11.odd), custom_call_target="tpu_custom_call" | custom-call | flops 2164260864 | bytes 8781824 | tf_op jit(solution)/shard_map/correlate/pallas_call | solution.py:263
  36.3 0.1 collective-permute-start.3
  36.4 0.0 collective-permute-done.5.beside_ref
  36.4 5.6 %correlate.5 = f32[8,16,256]{2,1,0:T(8,128)S(1)} custom-call(bf16[8,16,256]{2,1,0:T(8,128)(2,1)S(1)} %subtract_convert_fusion.beside_ref.own_ref, bf16[8,16,256]{2,1,0:T(8,128)(2,1)S(1)} %collective-permute-done.5.beside_ref, bf16[260,64,128]{2,1,0:T(8,128)(2,1)S(1)} %get-tuple-element.10.even, bf16[260,64,128]{2,1,0:T(8,128)(2,1)S(1)} %get-tuple-element.11.odd), custom_call_target="tpu_custom_call" | custom-call | flops 2164260864 | bytes 8781824 | tf_op jit(solution)/shard_map/correlate/pallas_call | solution.py:263
  42.0 0.5 collective-permute-start.6
  42.6 1.6 %collective-permute-start.4 = (bf16[8,16,256]{2,1,0:T(8,128)(2,1)S(1)}, bf16[8,16,256]{2,1,0:T(8,128)(2,1)S(1)}, u32[]{:S(2)}, u32[]{:S(2)}) collective-permute-start(bf16[8,16,256]{2,1,0:T(8,128)(2,1)S(1)} %add_convert_fusion.3), channel_id=1, source_target_pairs={{0,2},{1,3},{2,0},{3,1},{4,6},{5,7},{6,4},{7,5},{8,10},{9,11},{10,... | collective-permute-start | bytes 196616 | tf_op jit(solution)/shard_map/ppermute | solution.py:295
  44.2 0.0 collective-permute-done.6
  44.2 1.0 %collective-permute-start.7 = (bf16[8,16,256]{2,1,0:T(8,128)(2,1)S(1)}, bf16[8,16,256]{2,1,0:T(8,128)(2,1)S(1)}, u32[]{:S(2)}, u32[]{:S(2)}) collective-permute-start(bf16[8,16,256]{2,1,0:T(8,128)(2,1)S(1)} %add_convert_fusion.2), channel_id=1, source_target_pairs={{0,2},{1,3},{2,0},{3,1},{4,6},{5,7},{6,4},{7,5},{8,10},{9,11},{10,... | collective-permute-start | bytes 196616 | tf_op jit(solution)/shard_map/ppermute | solution.py:295
  45.2 0.1 pad_maximum_fusion
  45.3 2.0 %collective-permute-done.4 = bf16[8,16,256]{2,1,0:T(8,128)(2,1)S(1)} collective-permute-done((bf16[8,16,256]{2,1,0:T(8,128)(2,1)S(1)}, bf16[8,16,256]{2,1,0:T(8,128)(2,1)S(1)}, u32[]{:S(2)}, u32[]{:S(2)}) %collective-permute-start.4) | collective-permute-done | bytes 65568 | tf_op jit(solution)/shard_map/ppermute | solution.py:295
  47.3 1.2 %collective-permute-done.7 = bf16[8,16,256]{2,1,0:T(8,128)(2,1)S(1)} collective-permute-done((bf16[8,16,256]{2,1,0:T(8,128)(2,1)S(1)}, bf16[8,16,256]{2,1,0:T(8,128)(2,1)S(1)}, u32[]{:S(2)}, u32[]{:S(2)}) %collective-permute-start.7) | collective-permute-done | bytes 65568 | tf_op jit(solution)/shard_map/ppermute | solution.py:295
  48.5 0.1 fusion.1
  48.6 4.5 %collective-permute-start.8 = (bf16[8,16,256]{2,1,0:T(8,128)(2,1)S(1)}, bf16[8,16,256]{2,1,0:T(8,128)(2,1)S(1)}, u32[]{:S(2)}, u32[]{:S(2)}) collective-permute-start(bf16[8,16,256]{2,1,0:T(8,128)(2,1)S(1)} %get-tuple-element.22.own_ref), channel_id=1, source_target_pairs={{0,8},{8,16},{16,24},{1,9},{9,17},{17,25},{2,10},{10,18},{18,26},{... | collective-permute-start | bytes 196616 | tf_op jit(solution)/shard_map/ppermute | solution.py:286
  53.2 3.4 %synthesize.7 = bf16[8,16,256]{2,1,0:T(8,128)(2,1)S(1)} custom-call(bf16[8,16,256]{2,1,0:T(8,128)(2,1)S(1)} %get-tuple-element.22.own_ref, bf16[8,16,256]{2,1,0:T(8,128)(2,1)S(1)} %get-tuple-element.23.own_ref.beside_ref, bf16[260,64,128]{2,1,0:T(8,128)(2,1)S(1)} %get-tuple-element.10.even, bf16[260,64,128]{2,1,0:T(8,128)(2,1)S(1)} %get-tuple-element.11.odd), custom_call_target="tpu_custom_call" | custom-call | flops 2164260864 | bytes 8781824 | tf_op jit(solution)/shard_map/synthesize/pallas_call | solution.py:263
  56.6 0.6 collective-permute-start.10
  57.2 3.4 %synthesize.6 = bf16[8,16,256]{2,1,0:T(8,128)(2,1)S(1)} custom-call(bf16[8,16,256]{2,1,0:T(8,128)(2,1)S(1)} %get-tuple-element.23.own_ref.beside_ref, bf16[8,16,256]{2,1,0:T(8,128)(2,1)S(1)} %collective-permute-done.8.beside_ref, bf16[260,64,128]{2,1,0:T(8,128)(2,1)S(1)} %get-tuple-element.10.even, bf16[260,64,128]{2,1,0:T(8,128)(2,1)S(1)} %get-tuple-element.11.odd), custom_call_target="tpu_custom_call" | custom-call | flops 2164260864 | bytes 8781824 | tf_op jit(solution)/shard_map/synthesize/pallas_call | solution.py:263
  60.6 1.6 %collective-permute-start.9 = (bf16[8,16,256]{2,1,0:T(8,128)(2,1)S(1)}, bf16[8,16,256]{2,1,0:T(8,128)(2,1)S(1)}, u32[]{:S(2)}, u32[]{:S(2)}) collective-permute-start(bf16[8,16,256]{2,1,0:T(8,128)(2,1)S(1)} %synthesize.6), channel_id=1, source_target_pairs={{0,4},{4,0},{1,5},{5,1},{2,6},{6,2},{3,7},{7,3},{8,12},{12,8},{9,1... | collective-permute-start | bytes 196616 | tf_op jit(solution)/shard_map/ppermute | solution.py:295
  62.2 2.7 %collective-permute-done.9 = bf16[8,16,256]{2,1,0:T(8,128)(2,1)S(1)} collective-permute-done((bf16[8,16,256]{2,1,0:T(8,128)(2,1)S(1)}, bf16[8,16,256]{2,1,0:T(8,128)(2,1)S(1)}, u32[]{:S(2)}, u32[]{:S(2)}) %collective-permute-start.9) | collective-permute-done | bytes 65568 | tf_op jit(solution)/shard_map/ppermute | solution.py:295
  64.9 1.5 %collective-permute-start.13 = (bf16[8,16,256]{2,1,0:T(8,128)(2,1)S(1)}, bf16[8,16,256]{2,1,0:T(8,128)(2,1)S(1)}, u32[]{:S(2)}, u32[]{:S(2)}) collective-permute-start(bf16[8,16,256]{2,1,0:T(8,128)(2,1)S(1)} %get-tuple-element.16.own_ref), channel_id=1, source_target_pairs={{8,0},{16,8},{24,16},{9,1},{17,9},{25,17},{10,2},{18,10},{26,18},{... | collective-permute-start | bytes 196616 | tf_op jit(solution)/shard_map/ppermute | solution.py:286
  66.5 6.3 %correlate.6 = f32[8,16,256]{2,1,0:T(8,128)S(1)} custom-call(bf16[8,16,256]{2,1,0:T(8,128)(2,1)S(1)} %get-tuple-element.16.own_ref, bf16[8,16,256]{2,1,0:T(8,128)(2,1)S(1)} %get-tuple-element.14.beside_ref.own_ref, bf16[260,64,128]{2,1,0:T(8,128)(2,1)S(1)} %get-tuple-element.10.even, bf16[260,64,128]{2,1,0:T(8,128)(2,1)S(1)} %get-tuple-element.11.odd), custom_call_target="tpu_custom_call" | custom-call | flops 2164260864 | bytes 8781824 | tf_op jit(solution)/shard_map/correlate/pallas_call | solution.py:263
  72.8 0.1 collective-permute-start.11
  72.9 6.4 %correlate.7 = f32[8,16,256]{2,1,0:T(8,128)S(1)} custom-call(bf16[8,16,256]{2,1,0:T(8,128)(2,1)S(1)} %get-tuple-element.14.beside_ref.own_ref, bf16[8,16,256]{2,1,0:T(8,128)(2,1)S(1)} %collective-permute-done.13.beside_ref, bf16[260,64,128]{2,1,0:T(8,128)(2,1)S(1)} %get-tuple-element.10.even, bf16[260,64,128]{2,1,0:T(8,128)(2,1)S(1)} %get-tuple-element.11.odd), custom_call_target="tpu_custom_call" | custom-call | flops 2164260864 | bytes 8781824 | tf_op jit(solution)/shard_map/correlate/pallas_call | solution.py:263
  79.3 0.5 collective-permute-start.14
  79.8 1.4 %collective-permute-start.12 = (bf16[8,16,256]{2,1,0:T(8,128)(2,1)S(1)}, bf16[8,16,256]{2,1,0:T(8,128)(2,1)S(1)}, u32[]{:S(2)}, u32[]{:S(2)}) collective-permute-start(bf16[8,16,256]{2,1,0:T(8,128)(2,1)S(1)} %add_convert_fusion.1), channel_id=1, source_target_pairs={{0,2},{1,3},{2,0},{3,1},{4,6},{5,7},{6,4},{7,5},{8,10},{9,11},{10,... | collective-permute-start | bytes 196616 | tf_op jit(solution)/shard_map/ppermute | solution.py:295
  81.2 1.0 %collective-permute-start.15 = (bf16[8,16,256]{2,1,0:T(8,128)(2,1)S(1)}, bf16[8,16,256]{2,1,0:T(8,128)(2,1)S(1)}, u32[]{:S(2)}, u32[]{:S(2)}) collective-permute-start(bf16[8,16,256]{2,1,0:T(8,128)(2,1)S(1)} %add_convert_fusion), channel_id=1, source_target_pairs={{0,2},{1,3},{2,0},{3,1},{4,6},{5,7},{6,4},{7,5},{8,10},{9,11},{10,... | collective-permute-start | bytes 196616 | tf_op jit(solution)/shard_map/ppermute | solution.py:295
  82.2 1.0 %from_blocks.3 = f32[64,1024]{1,0:T(8,128)} custom-call(f32[8,16,256]{2,1,0:T(8,128)S(1)} %get-tuple-element.17.low_ref, f32[8,16,256]{2,1,0:T(8,128)S(1)} %get-tuple-element.15.high_ref), custom_call_target="tpu_custom_call" | custom-call | tf_op jit(solution)/shard_map/from_blocks/pallas_call | solution.py:75
  83.2 1.4 %collective-permute-done.12 = bf16[8,16,256]{2,1,0:T(8,128)(2,1)S(1)} collective-permute-done((bf16[8,16,256]{2,1,0:T(8,128)(2,1)S(1)}, bf16[8,16,256]{2,1,0:T(8,128)(2,1)S(1)}, u32[]{:S(2)}, u32[]{:S(2)}) %collective-permute-start.12) | collective-permute-done | bytes 65568 | tf_op jit(solution)/shard_map/ppermute | solution.py:295
  84.6 1.0 %collective-permute-done.15 = bf16[8,16,256]{2,1,0:T(8,128)(2,1)S(1)} collective-permute-done((bf16[8,16,256]{2,1,0:T(8,128)(2,1)S(1)}, bf16[8,16,256]{2,1,0:T(8,128)(2,1)S(1)}, u32[]{:S(2)}, u32[]{:S(2)}) %collective-permute-start.15) | collective-permute-done | bytes 65568 | tf_op jit(solution)/shard_map/ppermute | solution.py:295
  85.5 0.1 minimum_subtract_fusion
  85.7 1.0 %from_blocks.2 = f32[64,1024]{1,0:T(8,128)} custom-call(f32[8,16,256]{2,1,0:T(8,128)S(1)} %get-tuple-element.21.low_ref, f32[8,16,256]{2,1,0:T(8,128)S(1)} %get-tuple-element.20.high_ref), custom_call_target="tpu_custom_call" | custom-call | tf_op jit(solution)/shard_map/from_blocks/pallas_call | solution.py:75
  (21 shorter events, 0.2 us)
Async XLA Ops:
  0.6 1.0 %copy-start.1 = (f32[64,1024]{1,0:T(8,128)S(1)}, f32[64,1024]{1,0:T(8,128)}, u32[]{:S(2)}) copy-start(f32[64,1024]{1,0:T(8,128)} %refs_0_.1) | copy-start | bytes 786436
  1.6 0.9 %copy-start.2 = (bf16[64,1024]{1,0:T(8,128)(2,1)S(1)}, bf16[64,1024]{1,0:T(8,128)(2,1)}, u32[]{:S(2)}) copy-start(bf16[64,1024]{1,0:T(8,128)(2,1)} %refs_1_.1) | copy-start | bytes 393220
  2.8 19.6 %collective-permute-start = (bf16[8,16,256]{2,1,0:T(8,128)(2,1)S(1)}, bf16[8,16,256]{2,1,0:T(8,128)(2,1)S(1)}, u32[]{:S(2)}, u32[]{:S(2)}) collective-permute-start(bf16[8,16,256]{2,1,0:T(8,128)(2,1)S(1)} %convert_element_type.85.own_ref), channel_id=1, source_target_pairs={{0,8},{8,16},{16,24},{1,9},{9,17},{17,25},{2,10},{10,18},{18,26},{... | collective-permute-start | bytes 196616 | tf_op jit(solution)/shard_map/ppermute | solution.py:286
  7.8 2.2 %copy-start = (bf16[64,64,512]{2,1,0:T(8,128)(2,1)S(1)}, bf16[64,64,512]{2,1,0:T(8,128)(2,1)}, u32[]{:S(2)}) copy-start(bf16[64,64,512]{2,1,0:T(8,128)(2,1)} %bank_hbm.1) | copy-start | bytes 12582916
  18.4 4.0 %copy-start.3 = (f32[64]{0:T(128)S(1)}, f32[64]{0:T(128)}, u32[]{:S(2)}) copy-start(f32[64]{0:T(128)} %param.9) | copy-start | bytes 772
  18.4 4.0 %copy-start.4 = (f32[64]{0:T(128)S(1)}, f32[64]{0:T(128)}, u32[]{:S(2)}) copy-start(f32[64]{0:T(128)} %param.8) | copy-start | bytes 772
  20.8 4.7 %collective-permute-start.2 = (bf16[8,16,256]{2,1,0:T(8,128)(2,1)S(1)}, bf16[8,16,256]{2,1,0:T(8,128)(2,1)S(1)}, u32[]{:S(2)}, u32[]{:S(2)}) collective-permute-start(bf16[8,16,256]{2,1,0:T(8,128)(2,1)S(1)} %synthesize.5), channel_id=1, source_target_pairs={{0,4},{4,0},{1,5},{5,1},{2,6},{6,2},{3,7},{7,3},{8,12},{12,8},{9,1... | collective-permute-start | bytes 196616 | tf_op jit(solution)/shard_map/ppermute | solution.py:295
  24.9 4.3 %collective-permute-start.1 = (bf16[8,16,256]{2,1,0:T(8,128)(2,1)S(1)}, bf16[8,16,256]{2,1,0:T(8,128)(2,1)S(1)}, u32[]{:S(2)}, u32[]{:S(2)}) collective-permute-start(bf16[8,16,256]{2,1,0:T(8,128)(2,1)S(1)} %synthesize.4), channel_id=1, source_target_pairs={{0,4},{4,0},{1,5},{5,1},{2,6},{6,2},{3,7},{7,3},{8,12},{12,8},{9,1... | collective-permute-start | bytes 196616 | tf_op jit(solution)/shard_map/ppermute | solution.py:295
  29.2 7.2 %collective-permute-start.5 = (bf16[8,16,256]{2,1,0:T(8,128)(2,1)S(1)}, bf16[8,16,256]{2,1,0:T(8,128)(2,1)S(1)}, u32[]{:S(2)}, u32[]{:S(2)}) collective-permute-start(bf16[8,16,256]{2,1,0:T(8,128)(2,1)S(1)} %subtract_convert_fusion.1.own_ref), channel_id=1, source_target_pairs={{8,0},{16,8},{24,16},{9,1},{17,9},{25,17},{10,2},{18,10},{26,18},{... | collective-permute-start | bytes 196616 | tf_op jit(solution)/shard_map/ppermute | solution.py:286
  36.3 6.3 %collective-permute-start.3 = (f32[8,16,256]{2,1,0:T(8,128)S(1)}, f32[8,16,256]{2,1,0:T(8,128)S(1)}, u32[]{:S(2)}, u32[]{:S(2)}) collective-permute-start(f32[8,16,256]{2,1,0:T(8,128)S(1)} %correlate.4), channel_id=1, source_target_pairs={{0,1},{1,0},{2,3},{3,2},{4,5},{5,4},{6,7},{7,6},{8,9},{9,8},{10,11... | collective-permute-start | bytes 393224 | tf_op jit(solution)/shard_map/ppermute | solution.py:295
  42.0 2.2 %collective-permute-start.6 = (f32[8,16,256]{2,1,0:T(8,128)S(1)}, f32[8,16,256]{2,1,0:T(8,128)S(1)}, u32[]{:S(2)}, u32[]{:S(2)}) collective-permute-start(f32[8,16,256]{2,1,0:T(8,128)S(1)} %correlate.5), channel_id=1, source_target_pairs={{0,1},{1,0},{2,3},{3,2},{4,5},{5,4},{6,7},{7,6},{8,9},{9,8},{10,11... | collective-permute-start | bytes 393224 | tf_op jit(solution)/shard_map/ppermute | solution.py:295
  42.6 4.7 %collective-permute-start.4 = (bf16[8,16,256]{2,1,0:T(8,128)(2,1)S(1)}, bf16[8,16,256]{2,1,0:T(8,128)(2,1)S(1)}, u32[]{:S(2)}, u32[]{:S(2)}) collective-permute-start(bf16[8,16,256]{2,1,0:T(8,128)(2,1)S(1)} %add_convert_fusion.3), channel_id=1, source_target_pairs={{0,2},{1,3},{2,0},{3,1},{4,6},{5,7},{6,4},{7,5},{8,10},{9,11},{10,... | collective-permute-start | bytes 196616 | tf_op jit(solution)/shard_map/ppermute | solution.py:295
  44.2 4.3 %collective-permute-start.7 = (bf16[8,16,256]{2,1,0:T(8,128)(2,1)S(1)}, bf16[8,16,256]{2,1,0:T(8,128)(2,1)S(1)}, u32[]{:S(2)}, u32[]{:S(2)}) collective-permute-start(bf16[8,16,256]{2,1,0:T(8,128)(2,1)S(1)} %add_convert_fusion.2), channel_id=1, source_target_pairs={{0,2},{1,3},{2,0},{3,1},{4,6},{5,7},{6,4},{7,5},{8,10},{9,11},{10,... | collective-permute-start | bytes 196616 | tf_op jit(solution)/shard_map/ppermute | solution.py:295
  48.6 8.6 %collective-permute-start.8 = (bf16[8,16,256]{2,1,0:T(8,128)(2,1)S(1)}, bf16[8,16,256]{2,1,0:T(8,128)(2,1)S(1)}, u32[]{:S(2)}, u32[]{:S(2)}) collective-permute-start(bf16[8,16,256]{2,1,0:T(8,128)(2,1)S(1)} %get-tuple-element.22.own_ref), channel_id=1, source_target_pairs={{0,8},{8,16},{16,24},{1,9},{9,17},{17,25},{2,10},{10,18},{18,26},{... | collective-permute-start | bytes 196616 | tf_op jit(solution)/shard_map/ppermute | solution.py:286
  56.6 5.6 %collective-permute-start.10 = (bf16[8,16,256]{2,1,0:T(8,128)(2,1)S(1)}, bf16[8,16,256]{2,1,0:T(8,128)(2,1)S(1)}, u32[]{:S(2)}, u32[]{:S(2)}) collective-permute-start(bf16[8,16,256]{2,1,0:T(8,128)(2,1)S(1)} %synthesize.7), channel_id=1, source_target_pairs={{0,4},{4,0},{1,5},{5,1},{2,6},{6,2},{3,7},{7,3},{8,12},{12,8},{9,1... | collective-permute-start | bytes 196616 | tf_op jit(solution)/shard_map/ppermute | solution.py:295
  60.6 4.3 %collective-permute-start.9 = (bf16[8,16,256]{2,1,0:T(8,128)(2,1)S(1)}, bf16[8,16,256]{2,1,0:T(8,128)(2,1)S(1)}, u32[]{:S(2)}, u32[]{:S(2)}) collective-permute-start(bf16[8,16,256]{2,1,0:T(8,128)(2,1)S(1)} %synthesize.6), channel_id=1, source_target_pairs={{0,4},{4,0},{1,5},{5,1},{2,6},{6,2},{3,7},{7,3},{8,12},{12,8},{9,1... | collective-permute-start | bytes 196616 | tf_op jit(solution)/shard_map/ppermute | solution.py:295
  64.9 8.0 %collective-permute-start.13 = (bf16[8,16,256]{2,1,0:T(8,128)(2,1)S(1)}, bf16[8,16,256]{2,1,0:T(8,128)(2,1)S(1)}, u32[]{:S(2)}, u32[]{:S(2)}) collective-permute-start(bf16[8,16,256]{2,1,0:T(8,128)(2,1)S(1)} %get-tuple-element.16.own_ref), channel_id=1, source_target_pairs={{8,0},{16,8},{24,16},{9,1},{17,9},{25,17},{10,2},{18,10},{26,18},{... | collective-permute-start | bytes 196616 | tf_op jit(solution)/shard_map/ppermute | solution.py:286
  72.8 7.0 %collective-permute-start.11 = (f32[8,16,256]{2,1,0:T(8,128)S(1)}, f32[8,16,256]{2,1,0:T(8,128)S(1)}, u32[]{:S(2)}, u32[]{:S(2)}) collective-permute-start(f32[8,16,256]{2,1,0:T(8,128)S(1)} %correlate.6), channel_id=1, source_target_pairs={{0,1},{1,0},{2,3},{3,2},{4,5},{5,4},{6,7},{7,6},{8,9},{9,8},{10,11... | collective-permute-start | bytes 393224 | tf_op jit(solution)/shard_map/ppermute | solution.py:295
  79.3 1.9 %collective-permute-start.14 = (f32[8,16,256]{2,1,0:T(8,128)S(1)}, f32[8,16,256]{2,1,0:T(8,128)S(1)}, u32[]{:S(2)}, u32[]{:S(2)}) collective-permute-start(f32[8,16,256]{2,1,0:T(8,128)S(1)} %correlate.7), channel_id=1, source_target_pairs={{0,1},{1,0},{2,3},{3,2},{4,5},{5,4},{6,7},{7,6},{8,9},{9,8},{10,11... | collective-permute-start | bytes 393224 | tf_op jit(solution)/shard_map/ppermute | solution.py:295
  79.8 4.7 %collective-permute-start.12 = (bf16[8,16,256]{2,1,0:T(8,128)(2,1)S(1)}, bf16[8,16,256]{2,1,0:T(8,128)(2,1)S(1)}, u32[]{:S(2)}, u32[]{:S(2)}) collective-permute-start(bf16[8,16,256]{2,1,0:T(8,128)(2,1)S(1)} %add_convert_fusion.1), channel_id=1, source_target_pairs={{0,2},{1,3},{2,0},{3,1},{4,6},{5,7},{6,4},{7,5},{8,10},{9,11},{10,... | collective-permute-start | bytes 196616 | tf_op jit(solution)/shard_map/ppermute | solution.py:295
  81.2 4.3 %collective-permute-start.15 = (bf16[8,16,256]{2,1,0:T(8,128)(2,1)S(1)}, bf16[8,16,256]{2,1,0:T(8,128)(2,1)S(1)}, u32[]{:S(2)}, u32[]{:S(2)}) collective-permute-start(bf16[8,16,256]{2,1,0:T(8,128)(2,1)S(1)} %add_convert_fusion), channel_id=1, source_target_pairs={{0,2},{1,3},{2,0},{3,1},{4,6},{5,7},{6,4},{7,5},{8,10},{9,11},{10,... | collective-permute-start | bytes 196616 | tf_op jit(solution)/shard_map/ppermute | solution.py:295

commit v5 on v4

--- a/solution.py
+++ b/solution.py
@@ -15,8 +15,16 @@
 
 
 def blocks_kernel(count, *refs):
-    values, outs, flat = refs[:count], refs[count:-1], refs[-1]
-    for index, value_ref in enumerate(values):
+    values, outs = refs[:count], refs[count : 3 * count]
+    held, flat, sems = refs[3 * count : 4 * count], refs[-2], refs[-1]
+    copies = [
+        pltpu.make_async_copy(value, place, sems.at[index])
+        for index, (value, place) in enumerate(zip(values, held))
+    ]
+    for copy in copies:
+        copy.start()
+    for index, value_ref in enumerate(held):
+        copies[index].wait()
         halves = outs[2 * index : 2 * index + 2]
         rows, slab = value_ref.shape
         run, parts, _ = halves[0].shape
@@ -42,10 +50,14 @@
     slab = values[0].shape[1]
     return pl.pallas_call(
         functools.partial(blocks_kernel, len(values)),
-        in_specs=[pl.BlockSpec(memory_space=pltpu.VMEM)] * len(values),
+        in_specs=[pl.BlockSpec(memory_space=pltpu.HBM)] * len(values),
         out_specs=[pl.BlockSpec(memory_space=pltpu.VMEM)] * (2 * len(values)),
         out_shape=[half] * (2 * len(values)),
-        scratch_shapes=[pltpu.VMEM((slab + slab // (run * PHASES) + 7, LANES), jnp.float32)],
+        scratch_shapes=[pltpu.VMEM(value.shape, value.dtype) for value in values]
+        + [
+            pltpu.VMEM((slab + slab // (run * PHASES) + 7, LANES), jnp.float32),
+            pltpu.SemaphoreType.DMA((len(values),)),
+        ],
         compiler_params=pltpu.CompilerParams(vmem_limit_bytes=VMEM),
         name="to_blocks",
     )(*values)
@@ -97,27 +109,33 @@
     zeros = jnp.zeros((margin, LANES), jnp.float32)
     low = lax.broadcasted_iota(jnp.int32, (block, LANES), 1) < chans
 
+    pieces = sems.shape[1]
+    size = block // pieces
     copies = [
         [
-            pltpu.make_async_copy(bank_hbm.at[span], bank.at[span], sems.at[group, which])
-            for which, span in enumerate(
-                (pl.ds(group * block, block), pl.ds(half + group * block, block))
-            )
+            [
+                pltpu.make_async_copy(bank_hbm.at[span], bank.at[span], sems.at[group, piece, which])
+                for which, span in enumerate(
+                    (
+                        pl.ds(group * block + piece * size, size),
+                        pl.ds(half + group * block + piece * size, size),
+                    )
+                )
+            ]
+            for piece in range(pieces)
         ]
         for group in range(turns)
     ]
-    for pair in copies:
-        for copy in pair:
-            copy.start()
+    for group in copies:
+        for piece in group:
+            for copy in piece:
+                copy.start()
 
     def tap(index):
         value = flat[pl.ds(index + margin, block, stride=rows), :]
         return value, pltpu.roll(value, chans, 1)
 
     for group in range(turns):
-        for copy in copies[group]:
-            copy.wait()
-
         def turn(pair, carry):
             first = group * block + 2 * pair
             stacked = jnp.concatenate(
@@ -139,7 +157,11 @@
                     flat[pl.ds(base, step), :] = turned[:, which * LANES : (which + 1) * LANES]
             return carry
 
-        lax.fori_loop(0, block // 2, turn, 0)
+        for piece in range(pieces):
+            for copy in copies[group][piece]:
+                copy.wait()
+            for pair in range(piece * size // 2, (piece + 1) * size // 2):
+                turn(pair, 0)
 
         def store(ref, tile, early, late):
             start = group * block
@@ -147,7 +169,7 @@
             start += half
             ref[tile, start : start + block] = jnp.where(low, early[1], late[0]).astype(jnp.bfloat16)
 
-        unroll = next(n for n in (20, 13, 8, 5, 4, 2, 1) if tiles % n == 0)
+        unroll = next(n for n in (65, 20, 13, 8, 5, 4, 2, 1) if tiles % n == 0)
 
         def merge(turn_index, carry):
             for inner in range(unroll):
@@ -172,20 +194,64 @@
     spec = pl.BlockSpec(memory_space=pltpu.VMEM)
     return pl.pallas_call(
         functools.partial(bank_kernel, rows),
-        in_specs=[pl.BlockSpec(memory_space=pl.ANY)],
+        in_specs=[pl.BlockSpec(memory_space=pltpu.HBM)],
         out_specs=[spec, spec],
         out_shape=[shape, shape],
         scratch_shapes=[
             pltpu.VMEM(atom_bank.shape, jnp.bfloat16),
             pltpu.VMEM((block * rows, LANES), jnp.float32),
-            pltpu.SemaphoreType.DMA((turns, 2)),
+            pltpu.SemaphoreType.DMA((turns, 4, 2)),
         ],
         compiler_params=pltpu.CompilerParams(vmem_limit_bytes=24 * 1024 * 1024),
         name="bank_tiles",
     )(atom_bank)
 
 
-def conv_kernel(transposed, steps, group, own_ref, beside_ref, even, odd, out_ref, base, spread, total):
+def turn_kernel(even_ref, odd_ref, even_out, odd_out):
+    tiles = even_ref.shape[0]
+    rows = even_out.shape[1]
+    eye = (
+        lax.broadcasted_iota(jnp.int32, (LANES, LANES), 0)
+        == lax.broadcasted_iota(jnp.int32, (LANES, LANES), 1)
+    ).astype(jnp.bfloat16)
+    unroll = next(n for n in (26, 20, 10, 4, 2) if tiles % n == 0)
+
+    def loop(turn, carry):
+        for inner in range(0, unroll, 2):
+            tile = turn * unroll + inner
+            stacked = jnp.concatenate(
+                [odd_ref[tile], even_ref[tile], odd_ref[tile + 1], even_ref[tile + 1]], axis=0
+            )
+            turned = lax.dot_general(
+                eye, stacked, (((1,), (1,)), ((), ())), preferred_element_type=jnp.float32
+            ).astype(jnp.bfloat16)
+            for which in range(2):
+                part = turned[:, which * LANES : (which + 1) * LANES]
+                odd_out[tile + which] = part[:rows]
+                even_out[tile + which] = part[rows:]
+        return carry
+
+    lax.fori_loop(0, tiles // unroll, loop, 0)
+
+
+def turn_tiles(even, odd):
+    tiles = even.shape[0]
+    shape = jax.ShapeDtypeStruct((tiles, LANES // 2, LANES), jnp.bfloat16)
+    spec = pl.BlockSpec(memory_space=pltpu.VMEM)
+    return pl.pallas_call(
+        turn_kernel,
+        in_specs=[spec, spec],
+        out_specs=[spec, spec],
+        out_shape=[shape, shape],
+        compiler_params=pltpu.CompilerParams(vmem_limit_bytes=VMEM),
+        cost_estimate=pl.CostEstimate(
+            flops=tiles * LANES**3 * 4, bytes_accessed=4 * even.size * 2, transcendentals=0
+        ),
+        name="turn_tiles",
+    )(even, odd)
+
+
+def conv_kernel(transposed, steps, own_ref, beside_ref, even, odd, out_ref, base, spread, total):
     run, parts, width = own_ref.shape
     lanes = width // LANES
 
@@ -199,69 +265,45 @@
             spread[lane, shift * run : (shift + 1) * run] = window[:, :, lane * LANES : (lane + 1) * LANES]
 
     def block(step):
-        def pair(ref, start):
-            return jnp.concatenate([ref[start], ref[start + 1]], axis=1)
-
+        if transposed:
+            picks = [(even, 1, 0), (odd, 2, 1), (even, 2, 1), (odd, 3, 2)]
+        else:
+            picks = [(even, 2, 3), (odd, 1, 2), (even, 1, 2), (odd, 0, 1)]
         return jnp.concatenate(
             [
-                pair(even, 2 * step + 2),
-                pair(odd, 2 * step + 1),
-                pair(even, 2 * step + 1),
-                pair(odd, 2 * step),
+                jnp.concatenate([ref[2 * step + left], ref[2 * step + right]], axis=1)
+                for ref, left, right in picks
             ],
             axis=0,
         )
 
     def rows(step):
         start = step if transposed else parts * run - step
-        return [
-            spread[lane, pl.ds(start, run)].reshape(run * parts, LANES) for lane in range(lanes)
-        ]
+        return [spread[lane, start : start + run].reshape(run * parts, LANES) for lane in range(lanes)]
 
     def product(first, count):
         left = jnp.concatenate([part for i in range(count) for part in rows(first + i)], axis=1)
-        if transposed:
-            right = jnp.concatenate([block(first + i) for i in range(count)], axis=1)
-            dims = (((1,), (1,)), ((), ()))
-        else:
-            right = jnp.concatenate([block(first + i) for i in range(count)], axis=0)
-            dims = (((1,), (0,)), ((), ()))
-        return lax.dot_general(left, right, dims, preferred_element_type=jnp.float32)
+        right = jnp.concatenate([block(first + i) for i in range(count)], axis=0)
+        return jnp.dot(left, right, preferred_element_type=jnp.float32)
 
     order = list(range(parts + 1)) if transposed else list(range(parts, -1, -1))
-    if group is None:
-        fill(order[0])
-        total[0] = product(0, 1)
-        total[1] = jnp.zeros_like(total[1])
-        for turn in range(parts):
-            fill(order[turn + 1])
-            total[turn % 2] += product(1 + turn * run, run)
-    else:
-        for shift in order:
-            fill(shift)
-        total[...] = jnp.zeros_like(total)
-
-        def loop(turn, carry):
-            near = group // 2
-            total[0] += product(turn * group, near)
-            total[1] += product(turn * group + near, group - near)
-            return carry
-
-        turns = steps // group
-        lax.fori_loop(0, turns, loop, 0)
-        if steps > turns * group:
-            total[0] += product(turns * group, steps - turns * group)
+    fill(order[0])
+    total[0] = product(0, 1)
+    total[1] = jnp.zeros_like(total[1])
+    for turn in range(parts):
+        fill(order[turn + 1])
+        total[turn % 2] += product(1 + turn * run, run)
     out_ref[...] = (total[0] + total[1]).reshape(out_ref.shape).astype(out_ref.dtype)
 
 
-def convolve(own, beside, even, odd, transposed, group):
+def convolve(own, beside, tiles, transposed):
     run, parts, width = own.shape
-    tiles, atoms, _ = even.shape
+    even, odd = tiles
     steps = run * parts + 1
-    out_width = PHASES * atoms if transposed else 2 * LANES
+    out_width = PHASES * LANES // 2
     flops = 2 * run * parts * width * out_width * steps
     return pl.pallas_call(
-        functools.partial(conv_kernel, transposed, steps, group),
+        functools.partial(conv_kernel, transposed, steps),
         in_specs=[pl.BlockSpec(memory_space=pltpu.VMEM)] * 4,
         out_specs=pl.BlockSpec(memory_space=pltpu.VMEM),
         out_shape=jax.ShapeDtypeStruct(
@@ -286,6 +328,18 @@
     return lax.ppermute(value, axis, [(i, i + steps) for i in range(first, last)])
 
 
+def shifted_by_pairs(value, axis, steps):
+    count = lax.axis_size(axis)
+    total = None
+    for parity in range(2):
+        moves = [(i, i + steps) for i in range(count) if 0 <= i + steps < count]
+        moves = [move for move in moves if min(move) % 2 == parity]
+        if moves:
+            part = lax.ppermute(value, axis, moves)
+            total = part if total is None else total + part
+    return jnp.zeros_like(value) if total is None else total
+
+
 def summed(value, axis):
     count = lax.axis_size(axis)
     step = 1
@@ -305,7 +359,7 @@
         atom_bank = jnp.pad(atom_bank, ((0, 0), (0, held - chans), (0, 0)))
         signal = jnp.pad(signal, ((0, held - chans), (0, 0)))
     low, high, heard_low, heard_high = to_blocks(taps, codes_init, signal)
-    even, odd = bank_tiles(atom_bank)
+    tiles = bank_tiles(atom_bank)
     step = jnp.concatenate([step_size] * PHASES)
     bound = jnp.concatenate([step_size * threshold] * PHASES)
 
@@ -313,19 +367,26 @@
         moved = current - step * gradient
         return moved - jnp.clip(moved, -bound, bound)
 
+    turned = None
     for sweep in range(ITERS):
-        group = None if sweep == 0 else 43
         low16, high16 = low.astype(jnp.bfloat16), high.astype(jnp.bfloat16)
         earlier = shifted(high16, "tm", 1)
-        recon_high = summed(convolve(high16, low16, even, odd, False, group), "atom")
-        recon_low = summed(convolve(low16, earlier, even, odd, False, group), "atom")
+        if sweep == 0:
+            recon_low = convolve(low16, earlier, tiles, False)
+            high16, recon_low = lax.optimization_barrier((high16, recon_low))
+            recon_high = convolve(high16, low16, tiles, False)
+            turned = turn_tiles(*tiles)
+        else:
+            recon_high = convolve(high16, low16, tiles, False)
+            recon_low = convolve(low16, earlier, tiles, False)
+        recon_low, recon_high = summed(recon_low, "atom"), summed(recon_high, "atom")
+        misfit_low = recon_low - heard_low
         misfit_high = recon_high - heard_high
-        misfit_low = recon_low - heard_low
+        rounded_low = misfit_low.astype(jnp.bfloat16)
         rounded_high = misfit_high.astype(jnp.bfloat16)
-        rounded_low = misfit_low.astype(jnp.bfloat16)
-        following = shifted(rounded_low, "tm", -1)
-        gradient_low = summed(convolve(rounded_low, rounded_high, even, odd, True, group), "chan")
-        gradient_high = summed(convolve(rounded_high, following, even, odd, True, group), "chan")
+        following = shifted_by_pairs(rounded_low, "tm", -1)
+        gradient_low = summed(convolve(rounded_low, rounded_high, turned, True), "chan")
+        gradient_high = summed(convolve(rounded_high, following, turned, True), "chan")
         low = shrink(low, gradient_low)
         high = shrink(high, gradient_high)
     return from_blocks(low, high), from_blocks(misfit_low, misfit_high)[:chans]

time: 87 us -> 75.2 us (0.86)
  Pallas kernels: 46.2 us -> 31.2 us
  waiting for transfers between devices: 12.1 us -> 14.5 us
    pallas_call x8 -> x9, Pallas kernels: 35.5 us -> 23 us  [the longest x8 19.1 us: convolve(): pl.pallas_call(functools.partial(conv_kernel, transposed, steps), in_spec...]
    ppermute x0 -> x4, waiting for transfers between devices: none -> 4.66 us  [shifted_by_pairs(): part = lax.ppermute(value, axis, moves)]
    ppermute x0 -> x4, starting transfers between devices: none -> 4.31 us  [shifted_by_pairs(): part = lax.ppermute(value, axis, moves)]
    ppermute x4 -> x2, starting transfers between devices: 12.5 us -> 8.25 us  [shifted(): lax.ppermute(value, axis, [(i, i + steps) for i in range(first, last)])]
    pallas_call x1, Pallas kernels: 8.4 us -> 5.64 us  [bank_tiles(): pl.pallas_call(functools.partial(bank_kernel, rows), in_specs=[pl.BlockSp...]
    ppermute x12, waiting for transfers between devices: 12.1 us -> 9.8 us  [summed(): other = lax.ppermute(value, axis, [(i, i ^ step) for i in range(count)])]
  transfers between devices with their start and end apart: 16 -> 18, of which waited for: 6 -> 8; matrix products, arithmetic and copies ran while one was open for 0% -> 0% of each run, Pallas kernels for 52% -> 37%
where the time goes in v5:
time: 75.2 us; the launch traced here: 74.2 us
  Pallas kernels  31.2 us (41%)
  starting transfers between devices  22.9 us (30%)
  waiting for transfers between devices  14.5 us (19%)
  local copies, waits for them, and re-layouts  4.04 us (5%)
  between operations  0.95 us (1%)
    pallas_call x8, Pallas kernels, convolve(): pl.pallas_call(functools.partial(conv_kernel, transposed, steps), in_spec...  19.1 us
    ppermute x12, starting transfers between devices, summed(): other = lax.ppermute(value, axis, [(i, i ^ step) for i in range(count)])  10.4 us
    ppermute x12, waiting for transfers between devices, summed(): other = lax.ppermute(value, axis, [(i, i ^ step) for i in range(count)])  9.8 us
    ppermute x2, starting transfers between devices, shifted(): lax.ppermute(value, axis, [(i, i + steps) for i in range(first, last)])  8.25 us
    pallas_call x1, Pallas kernels, bank_tiles(): pl.pallas_call(functools.partial(bank_kernel, rows), in_specs=[pl.BlockSp...  5.64 us
    ppermute x4, waiting for transfers between devices, shifted_by_pairs(): part = lax.ppermute(value, axis, moves)  4.66 us
    ppermute x4, starting transfers between devices, shifted_by_pairs(): part = lax.ppermute(value, axis, moves)  4.31 us
    unnamed x10, local copies, waits for them, and re-layouts  4.04 us
  transfers between devices with their start and end apart: 18, of which 8 were waited for; matrix products, arithmetic and copies ran while one was open for 0% of the time, Pallas kernels for 37%

profile of v5, /device:TPU:0, one launch (start us, length us, event | category | flops | bytes accessed | tf_op | source)
XLA Modules:
  0.0 74.2 jit_solution(11015506379314480315)
XLA Ops:
  0.6 0.9 %copy-done.1 = f32[64,1024]{1,0:T(8,128)S(1)} copy-done((f32[64,1024]{1,0:T(8,128)S(1)}, f32[64,1024]{1,0:T(8,128)}, u32[]{:S(2)}) %copy-start.1) | copy-done | bytes 262168
  1.6 0.9 %copy-done.2 = bf16[64,1024]{1,0:T(8,128)(2,1)S(1)} copy-done((bf16[64,1024]{1,0:T(8,128)(2,1)S(1)}, bf16[64,1024]{1,0:T(8,128)(2,1)}, u32[]{:S(2)}) %copy-start.2) | copy-done | bytes 131096
  2.5 0.6 to_blocks.1
  3.1 4.9 %collective-permute-start = (bf16[8,16,256]{2,1,0:T(8,128)(2,1)S(1)}, bf16[8,16,256]{2,1,0:T(8,128)(2,1)S(1)}, u32[]{:S(2)}, u32[]{:S(2)}) collective-permute-start(bf16[8,16,256]{2,1,0:T(8,128)(2,1)S(1)} %convert_element_type.84.own_ref), channel_id=1, source_target_pairs={{0,8},{8,16},{16,24},{1,9},{9,17},{17,25},{2,10},{10,18},{18,26},{... | collective-permute-start | bytes 196616 | tf_op jit(solution)/shard_map/ppermute | solution.py:328
  8.1 0.0 copy-start
  8.1 2.2 %copy-done = bf16[64,64,512]{2,1,0:T(8,128)(2,1)S(1)} copy-done((bf16[64,64,512]{2,1,0:T(8,128)(2,1)S(1)}, bf16[64,64,512]{2,1,0:T(8,128)(2,1)}, u32[]{:S(2)}) %copy-start) | copy-done | bytes 4194328
  10.3 5.6 %bank_tiles.1 = (bf16[260,64,128]{2,1,0:T(8,128)(2,1)S(1)}, bf16[260,64,128]{2,1,0:T(8,128)(2,1)S(1)}) custom-call(bf16[64,64,512]{2,1,0:T(8,128)(2,1)S(1)} %copy-done), custom_call_target="tpu_custom_call" | custom-call | tf_op jit(solution)/shard_map/bank_tiles/pallas_call | solution.py:195
  15.9 3.9 %turn_tiles.1 = (bf16[260,64,128]{2,1,0:T(8,128)(2,1)S(1)}, bf16[260,64,128]{2,1,0:T(8,128)(2,1)S(1)}) custom-call(bf16[260,64,128]{2,1,0:T(8,128)(2,1)S(1)} %get-tuple-element.14.even.even_ref, bf16[260,64,128]{2,1,0:T(8,128)(2,1)S(1)} %get-tuple-element.15.odd.odd_ref), custom_call_target="tpu_custom_call" | custom-call | flops 2181038080 | bytes 17039360 | tf_op jit(solution)/shard_map/turn_tiles/pallas_call | solution.py:241
  19.8 0.1 fusion.4
  19.9 0.0 collective-permute-done.beside_ref
  19.9 2.4 %synthesize.4 = bf16[8,16,256]{2,1,0:T(8,128)(2,1)S(1)} custom-call(bf16[8,16,256]{2,1,0:T(8,128)(2,1)S(1)} %convert_element_type.85.own_ref.beside_ref, bf16[8,16,256]{2,1,0:T(8,128)(2,1)S(1)} %collective-permute-done.beside_ref, bf16[260,64,128]{2,1,0:T(8,128)(2,1)S(1)} %get-tuple-element.14.even.even_ref, ...), custom_call_target="tpu_custom_call" | custom-call | flops 2164260864 | bytes 8781824 | tf_op jit(solution)/shard_map/synthesize/pallas_call | solution.py:305
  22.3 1.6 %collective-permute-start.1 = (bf16[8,16,256]{2,1,0:T(8,128)(2,1)S(1)}, bf16[8,16,256]{2,1,0:T(8,128)(2,1)S(1)}, u32[]{:S(2)}, u32[]{:S(2)}) collective-permute-start(bf16[8,16,256]{2,1,0:T(8,128)(2,1)S(1)} %synthesize.4), channel_id=1, source_target_pairs={{0,4},{4,0},{1,5},{5,1},{2,6},{6,2},{3,7},{7,3},{8,12},{12,8},{9,1... | collective-permute-start | bytes 196616 | tf_op jit(solution)/shard_map/ppermute | solution.py:349
  23.8 2.4 %synthesize.5 = bf16[8,16,256]{2,1,0:T(8,128)(2,1)S(1)} custom-call(bf16[8,16,256]{2,1,0:T(8,128)(2,1)S(1)} %convert_element_type.84.own_ref, bf16[8,16,256]{2,1,0:T(8,128)(2,1)S(1)} %convert_element_type.85.own_ref.beside_ref, bf16[260,64,128]{2,1,0:T(8,128)(2,1)S(1)} %get-tuple-element.14.even.even_ref, bf16[260,64,128]{2,1,0:T(8,128)(2,1)S(1)} %get-tuple-element.15.odd.odd_ref), custom_call_target="tpu_custom_call" | custom-call | flops 2164260864 | bytes 8781824 | tf_op jit(solution)/shard_map/synthesize/pallas_call | solution.py:305
  26.2 0.6 collective-permute-start.2
  26.9 0.7 collective-permute-start.6
  27.5 1.5 %collective-permute-start.5 = (bf16[8,16,256]{2,1,0:T(8,128)(2,1)S(1)}, bf16[8,16,256]{2,1,0:T(8,128)(2,1)S(1)}, u32[]{:S(2)}, u32[]{:S(2)}) collective-permute-start(bf16[8,16,256]{2,1,0:T(8,128)(2,1)S(1)} %subtract_convert_fusion.1.own_ref), channel_id=1, source_target_pairs={{8,0},{24,16},{9,1},{25,17},{10,2},{26,18},{11,3},{27,19},{12,4},{... | collective-permute-start | bytes 196616 | tf_op jit(solution)/shard_map/ppermute | solution.py:338
  29.0 1.5 %collective-permute-done.2 = bf16[8,16,256]{2,1,0:T(8,128)(2,1)S(1)} collective-permute-done((bf16[8,16,256]{2,1,0:T(8,128)(2,1)S(1)}, bf16[8,16,256]{2,1,0:T(8,128)(2,1)S(1)}, u32[]{:S(2)}, u32[]{:S(2)}) %collective-permute-start.2) | collective-permute-done | bytes 65568 | tf_op jit(solution)/shard_map/ppermute | solution.py:349
  30.6 2.4 %correlate.4 = f32[8,16,256]{2,1,0:T(8,128)S(1)} custom-call(bf16[8,16,256]{2,1,0:T(8,128)(2,1)S(1)} %subtract_convert_fusion.1.own_ref, bf16[8,16,256]{2,1,0:T(8,128)(2,1)S(1)} %subtract_convert_fusion.beside_ref.own_ref, bf16[260,64,128]{2,1,0:T(8,128)(2,1)S(1)} %get-tuple-element.20.even, bf16[260,64,128]{2,1,0:T(8,128)(2,1)S(1)} %get-tuple-element.21.odd), custom_call_target="tpu_custom_call" | custom-call | flops 2164260864 | bytes 8781824 | tf_op jit(solution)/shard_map/correlate/pallas_call | solution.py:305
  33.0 0.1 collective-permute-start.3
  33.1 0.6 collective-permute-done.5
  33.7 2.4 %correlate.5 = f32[8,16,256]{2,1,0:T(8,128)S(1)} custom-call(bf16[8,16,256]{2,1,0:T(8,128)(2,1)S(1)} %subtract_convert_fusion.beside_ref.own_ref, bf16[8,16,256]{2,1,0:T(8,128)(2,1)S(1)} %add.46.beside_ref, bf16[260,64,128]{2,1,0:T(8,128)(2,1)S(1)} %get-tuple-element.20.even, bf16[260,64,128]{2,1,0:T(8,128)(2,1)S(1)} %get-tuple-element.21.odd), custom_call_target="tpu_custom_call" | custom-call | flops 2164260864 | bytes 8781824 | tf_op jit(solution)/shard_map/correlate/pallas_call | solution.py:305
  36.1 0.1 collective-permute-start.7
  36.2 1.6 %collective-permute-start.4 = (bf16[8,16,256]{2,1,0:T(8,128)(2,1)S(1)}, bf16[8,16,256]{2,1,0:T(8,128)(2,1)S(1)}, u32[]{:S(2)}, u32[]{:S(2)}) collective-permute-start(bf16[8,16,256]{2,1,0:T(8,128)(2,1)S(1)} %add_convert_fusion.3), channel_id=1, source_target_pairs={{0,2},{1,3},{2,0},{3,1},{4,6},{5,7},{6,4},{7,5},{8,10},{9,11},{10,... | collective-permute-start | bytes 196616 | tf_op jit(solution)/shard_map/ppermute | solution.py:349
  37.9 1.3 %collective-permute-start.8 = (bf16[8,16,256]{2,1,0:T(8,128)(2,1)S(1)}, bf16[8,16,256]{2,1,0:T(8,128)(2,1)S(1)}, u32[]{:S(2)}, u32[]{:S(2)}) collective-permute-start(bf16[8,16,256]{2,1,0:T(8,128)(2,1)S(1)} %add_convert_fusion.2), channel_id=1, source_target_pairs={{0,2},{1,3},{2,0},{3,1},{4,6},{5,7},{6,4},{7,5},{8,10},{9,11},{10,... | collective-permute-start | bytes 196616 | tf_op jit(solution)/shard_map/ppermute | solution.py:349
  39.2 0.1 pad_maximum_fusion
  39.2 1.6 %collective-permute-done.4 = bf16[8,16,256]{2,1,0:T(8,128)(2,1)S(1)} collective-permute-done((bf16[8,16,256]{2,1,0:T(8,128)(2,1)S(1)}, bf16[8,16,256]{2,1,0:T(8,128)(2,1)S(1)}, u32[]{:S(2)}, u32[]{:S(2)}) %collective-permute-start.4) | collective-permute-done | bytes 65568 | tf_op jit(solution)/shard_map/ppermute | solution.py:349
  40.9 1.3 %collective-permute-done.8 = bf16[8,16,256]{2,1,0:T(8,128)(2,1)S(1)} collective-permute-done((bf16[8,16,256]{2,1,0:T(8,128)(2,1)S(1)}, bf16[8,16,256]{2,1,0:T(8,128)(2,1)S(1)}, u32[]{:S(2)}, u32[]{:S(2)}) %collective-permute-start.8) | collective-permute-done | bytes 65568 | tf_op jit(solution)/shard_map/ppermute | solution.py:349
  42.2 0.1 fusion.1
  42.3 3.3 %collective-permute-start.9 = (bf16[8,16,256]{2,1,0:T(8,128)(2,1)S(1)}, bf16[8,16,256]{2,1,0:T(8,128)(2,1)S(1)}, u32[]{:S(2)}, u32[]{:S(2)}) collective-permute-start(bf16[8,16,256]{2,1,0:T(8,128)(2,1)S(1)} %get-tuple-element.30.own_ref), channel_id=1, source_target_pairs={{0,8},{8,16},{16,24},{1,9},{9,17},{17,25},{2,10},{10,18},{18,26},{... | collective-permute-start | bytes 196616 | tf_op jit(solution)/shard_map/ppermute | solution.py:328
  45.6 2.4 %synthesize.7 = bf16[8,16,256]{2,1,0:T(8,128)(2,1)S(1)} custom-call(bf16[8,16,256]{2,1,0:T(8,128)(2,1)S(1)} %get-tuple-element.30.own_ref, bf16[8,16,256]{2,1,0:T(8,128)(2,1)S(1)} %get-tuple-element.31.own_ref.beside_ref, bf16[260,64,128]{2,1,0:T(8,128)(2,1)S(1)} %get-tuple-element.14.even.even_ref, bf16[260,64,128]{2,1,0:T(8,128)(2,1)S(1)} %get-tuple-element.15.odd.odd_ref), custom_call_target="tpu_custom_call" | custom-call | flops 2164260864 | bytes 8781824 | tf_op jit(solution)/shard_map/synthesize/pallas_call | solution.py:305
  48.0 1.1 %collective-permute-start.11 = (bf16[8,16,256]{2,1,0:T(8,128)(2,1)S(1)}, bf16[8,16,256]{2,1,0:T(8,128)(2,1)S(1)}, u32[]{:S(2)}, u32[]{:S(2)}) collective-permute-start(bf16[8,16,256]{2,1,0:T(8,128)(2,1)S(1)} %synthesize.7), channel_id=1, source_target_pairs={{0,4},{4,0},{1,5},{5,1},{2,6},{6,2},{3,7},{7,3},{8,12},{12,8},{9,1... | collective-permute-start | bytes 196616 | tf_op jit(solution)/shard_map/ppermute | solution.py:349
  49.1 2.4 %synthesize.6 = bf16[8,16,256]{2,1,0:T(8,128)(2,1)S(1)} custom-call(bf16[8,16,256]{2,1,0:T(8,128)(2,1)S(1)} %get-tuple-element.31.own_ref.beside_ref, bf16[8,16,256]{2,1,0:T(8,128)(2,1)S(1)} %collective-permute-done.9.beside_ref, bf16[260,64,128]{2,1,0:T(8,128)(2,1)S(1)} %get-tuple-element.14.even.even_ref, ...), custom_call_target="tpu_custom_call" | custom-call | flops 2164260864 | bytes 8781824 | tf_op jit(solution)/shard_map/synthesize/pallas_call | solution.py:305
  51.5 1.1 %collective-permute-start.10 = (bf16[8,16,256]{2,1,0:T(8,128)(2,1)S(1)}, bf16[8,16,256]{2,1,0:T(8,128)(2,1)S(1)}, u32[]{:S(2)}, u32[]{:S(2)}) collective-permute-start(bf16[8,16,256]{2,1,0:T(8,128)(2,1)S(1)} %synthesize.6), channel_id=1, source_target_pairs={{0,4},{4,0},{1,5},{5,1},{2,6},{6,2},{3,7},{7,3},{8,12},{12,8},{9,1... | collective-permute-start | bytes 196616 | tf_op jit(solution)/shard_map/ppermute | solution.py:349
  52.6 3.2 %collective-permute-done.10 = bf16[8,16,256]{2,1,0:T(8,128)(2,1)S(1)} collective-permute-done((bf16[8,16,256]{2,1,0:T(8,128)(2,1)S(1)}, bf16[8,16,256]{2,1,0:T(8,128)(2,1)S(1)}, u32[]{:S(2)}, u32[]{:S(2)}) %collective-permute-start.10) | collective-permute-done | bytes 65568 | tf_op jit(solution)/shard_map/ppermute | solution.py:349
  55.9 0.7 collective-permute-start.15
  56.5 1.5 %collective-permute-start.14 = (bf16[8,16,256]{2,1,0:T(8,128)(2,1)S(1)}, bf16[8,16,256]{2,1,0:T(8,128)(2,1)S(1)}, u32[]{:S(2)}, u32[]{:S(2)}) collective-permute-start(bf16[8,16,256]{2,1,0:T(8,128)(2,1)S(1)} %get-tuple-element.24.own_ref), channel_id=1, source_target_pairs={{8,0},{24,16},{9,1},{25,17},{10,2},{26,18},{11,3},{27,19},{12,4},{... | collective-permute-start | bytes 196616 | tf_op jit(solution)/shard_map/ppermute | solution.py:338
  58.0 2.4 %correlate.6 = f32[8,16,256]{2,1,0:T(8,128)S(1)} custom-call(bf16[8,16,256]{2,1,0:T(8,128)(2,1)S(1)} %get-tuple-element.24.own_ref, bf16[8,16,256]{2,1,0:T(8,128)(2,1)S(1)} %get-tuple-element.22.beside_ref.own_ref, bf16[260,64,128]{2,1,0:T(8,128)(2,1)S(1)} %get-tuple-element.20.even, bf16[260,64,128]{2,1,0:T(8,128)(2,1)S(1)} %get-tuple-element.21.odd), custom_call_target="tpu_custom_call" | custom-call | flops 2164260864 | bytes 8781824 | tf_op jit(solution)/shard_map/correlate/pallas_call | solution.py:305
  60.4 0.1 collective-permute-start.12
  60.5 4.0 %collective-permute-done.14 = bf16[8,16,256]{2,1,0:T(8,128)(2,1)S(1)} collective-permute-done((bf16[8,16,256]{2,1,0:T(8,128)(2,1)S(1)}, bf16[8,16,256]{2,1,0:T(8,128)(2,1)S(1)}, u32[]{:S(2)}, u32[]{:S(2)}) %collective-permute-start.14) | collective-permute-done | bytes 65568 | tf_op jit(solution)/shard_map/ppermute | solution.py:338
  64.6 2.4 %correlate.7 = f32[8,16,256]{2,1,0:T(8,128)S(1)} custom-call(bf16[8,16,256]{2,1,0:T(8,128)(2,1)S(1)} %get-tuple-element.22.beside_ref.own_ref, bf16[8,16,256]{2,1,0:T(8,128)(2,1)S(1)} %add.53.beside_ref, bf16[260,64,128]{2,1,0:T(8,128)(2,1)S(1)} %get-tuple-element.20.even, bf16[260,64,128]{2,1,0:T(8,128)(2,1)S(1)} %get-tuple-element.21.odd), custom_call_target="tpu_custom_call" | custom-call | flops 2164260864 | bytes 8781824 | tf_op jit(solution)/shard_map/correlate/pallas_call | solution.py:305
  67.0 0.1 collective-permute-start.16
  67.1 1.6 %collective-permute-start.13 = (bf16[8,16,256]{2,1,0:T(8,128)(2,1)S(1)}, bf16[8,16,256]{2,1,0:T(8,128)(2,1)S(1)}, u32[]{:S(2)}, u32[]{:S(2)}) collective-permute-start(bf16[8,16,256]{2,1,0:T(8,128)(2,1)S(1)} %add_convert_fusion.1), channel_id=1, source_target_pairs={{0,2},{1,3},{2,0},{3,1},{4,6},{5,7},{6,4},{7,5},{8,10},{9,11},{10,... | collective-permute-start | bytes 196616 | tf_op jit(solution)/shard_map/ppermute | solution.py:349
  68.7 1.3 %collective-permute-start.17 = (bf16[8,16,256]{2,1,0:T(8,128)(2,1)S(1)}, bf16[8,16,256]{2,1,0:T(8,128)(2,1)S(1)}, u32[]{:S(2)}, u32[]{:S(2)}) collective-permute-start(bf16[8,16,256]{2,1,0:T(8,128)(2,1)S(1)} %add_convert_fusion), channel_id=1, source_target_pairs={{0,2},{1,3},{2,0},{3,1},{4,6},{5,7},{6,4},{7,5},{8,10},{9,11},{10,... | collective-permute-start | bytes 196616 | tf_op jit(solution)/shard_map/ppermute | solution.py:349
  70.0 1.0 %from_blocks.3 = f32[64,1024]{1,0:T(8,128)} custom-call(f32[8,16,256]{2,1,0:T(8,128)S(1)} %get-tuple-element.25.low_ref, f32[8,16,256]{2,1,0:T(8,128)S(1)} %get-tuple-element.23.high_ref), custom_call_target="tpu_custom_call" | custom-call | tf_op jit(solution)/shard_map/from_blocks/pallas_call | solution.py:87
  71.0 0.7 collective-permute-done.13
  71.7 1.3 %collective-permute-done.17 = bf16[8,16,256]{2,1,0:T(8,128)(2,1)S(1)} collective-permute-done((bf16[8,16,256]{2,1,0:T(8,128)(2,1)S(1)}, bf16[8,16,256]{2,1,0:T(8,128)(2,1)S(1)}, u32[]{:S(2)}, u32[]{:S(2)}) %collective-permute-start.17) | collective-permute-done | bytes 65568 | tf_op jit(solution)/shard_map/ppermute | solution.py:349
  73.1 0.1 minimum_subtract_fusion
  73.2 1.0 %from_blocks.2 = f32[64,1024]{1,0:T(8,128)} custom-call(f32[8,16,256]{2,1,0:T(8,128)S(1)} %get-tuple-element.29.low_ref, f32[8,16,256]{2,1,0:T(8,128)S(1)} %get-tuple-element.28.high_ref), custom_call_target="tpu_custom_call" | custom-call | tf_op jit(solution)/shard_map/from_blocks/pallas_call | solution.py:87
  (28 shorter events, 0.3 us)
Async XLA Ops:
  0.6 1.0 %copy-start.1 = (f32[64,1024]{1,0:T(8,128)S(1)}, f32[64,1024]{1,0:T(8,128)}, u32[]{:S(2)}) copy-start(f32[64,1024]{1,0:T(8,128)} %refs_0_.1) | copy-start | bytes 786436
  1.6 0.9 %copy-start.2 = (bf16[64,1024]{1,0:T(8,128)(2,1)S(1)}, bf16[64,1024]{1,0:T(8,128)(2,1)}, u32[]{:S(2)}) copy-start(bf16[64,1024]{1,0:T(8,128)(2,1)} %refs_1_.1) | copy-start | bytes 393220
  2.5 13.4 %copy-start.3 = (f32[64]{0:T(128)S(1)}, f32[64]{0:T(128)}, u32[]{:S(2)}) copy-start(f32[64]{0:T(128)} %param.9) | copy-start | bytes 772
  2.5 13.4 %copy-start.4 = (f32[64]{0:T(128)S(1)}, f32[64]{0:T(128)}, u32[]{:S(2)}) copy-start(f32[64]{0:T(128)} %param.8) | copy-start | bytes 772
  3.1 16.8 %collective-permute-start = (bf16[8,16,256]{2,1,0:T(8,128)(2,1)S(1)}, bf16[8,16,256]{2,1,0:T(8,128)(2,1)S(1)}, u32[]{:S(2)}, u32[]{:S(2)}) collective-permute-start(bf16[8,16,256]{2,1,0:T(8,128)(2,1)S(1)} %convert_element_type.84.own_ref), channel_id=1, source_target_pairs={{0,8},{8,16},{16,24},{1,9},{9,17},{17,25},{2,10},{10,18},{18,26},{... | collective-permute-start | bytes 196616 | tf_op jit(solution)/shard_map/ppermute | solution.py:328
  8.1 2.2 %copy-start = (bf16[64,64,512]{2,1,0:T(8,128)(2,1)S(1)}, bf16[64,64,512]{2,1,0:T(8,128)(2,1)}, u32[]{:S(2)}) copy-start(bf16[64,64,512]{2,1,0:T(8,128)(2,1)} %bank_hbm.1) | copy-start | bytes 12582916
  22.3 4.6 %collective-permute-start.1 = (bf16[8,16,256]{2,1,0:T(8,128)(2,1)S(1)}, bf16[8,16,256]{2,1,0:T(8,128)(2,1)S(1)}, u32[]{:S(2)}, u32[]{:S(2)}) collective-permute-start(bf16[8,16,256]{2,1,0:T(8,128)(2,1)S(1)} %synthesize.4), channel_id=1, source_target_pairs={{0,4},{4,0},{1,5},{5,1},{2,6},{6,2},{3,7},{7,3},{8,12},{12,8},{9,1... | collective-permute-start | bytes 196616 | tf_op jit(solution)/shard_map/ppermute | solution.py:349
  26.2 4.3 %collective-permute-start.2 = (bf16[8,16,256]{2,1,0:T(8,128)(2,1)S(1)}, bf16[8,16,256]{2,1,0:T(8,128)(2,1)S(1)}, u32[]{:S(2)}, u32[]{:S(2)}) collective-permute-start(bf16[8,16,256]{2,1,0:T(8,128)(2,1)S(1)} %synthesize.5), channel_id=1, source_target_pairs={{0,4},{4,0},{1,5},{5,1},{2,6},{6,2},{3,7},{7,3},{8,12},{12,8},{9,1... | collective-permute-start | bytes 196616 | tf_op jit(solution)/shard_map/ppermute | solution.py:349
  26.9 6.2 %collective-permute-start.6 = (bf16[8,16,256]{2,1,0:T(8,128)(2,1)S(1)}, bf16[8,16,256]{2,1,0:T(8,128)(2,1)S(1)}, u32[]{:S(2)}, u32[]{:S(2)}) collective-permute-start(bf16[8,16,256]{2,1,0:T(8,128)(2,1)S(1)} %subtract_convert_fusion.1.own_ref), channel_id=1, source_target_pairs={{16,8},{17,9},{18,10},{19,11},{20,12},{21,13},{22,14},{23,15}} | collective-permute-start | bytes 196616 | tf_op jit(solution)/shard_map/ppermute | solution.py:338
  27.5 6.2 %collective-permute-start.5 = (bf16[8,16,256]{2,1,0:T(8,128)(2,1)S(1)}, bf16[8,16,256]{2,1,0:T(8,128)(2,1)S(1)}, u32[]{:S(2)}, u32[]{:S(2)}) collective-permute-start(bf16[8,16,256]{2,1,0:T(8,128)(2,1)S(1)} %subtract_convert_fusion.1.own_ref), channel_id=1, source_target_pairs={{8,0},{24,16},{9,1},{25,17},{10,2},{26,18},{11,3},{27,19},{12,4},{... | collective-permute-start | bytes 196616 | tf_op jit(solution)/shard_map/ppermute | solution.py:338
  33.0 3.2 %collective-permute-start.3 = (f32[8,16,256]{2,1,0:T(8,128)S(1)}, f32[8,16,256]{2,1,0:T(8,128)S(1)}, u32[]{:S(2)}, u32[]{:S(2)}) collective-permute-start(f32[8,16,256]{2,1,0:T(8,128)S(1)} %correlate.4), channel_id=1, source_target_pairs={{0,1},{1,0},{2,3},{3,2},{4,5},{5,4},{6,7},{7,6},{8,9},{9,8},{10,11... | collective-permute-start | bytes 393224 | tf_op jit(solution)/shard_map/ppermute | solution.py:349
  36.1 1.7 %collective-permute-start.7 = (f32[8,16,256]{2,1,0:T(8,128)S(1)}, f32[8,16,256]{2,1,0:T(8,128)S(1)}, u32[]{:S(2)}, u32[]{:S(2)}) collective-permute-start(f32[8,16,256]{2,1,0:T(8,128)S(1)} %correlate.5), channel_id=1, source_target_pairs={{0,1},{1,0},{2,3},{3,2},{4,5},{5,4},{6,7},{7,6},{8,9},{9,8},{10,11... | collective-permute-start | bytes 393224 | tf_op jit(solution)/shard_map/ppermute | solution.py:349
  36.2 4.6 %collective-permute-start.4 = (bf16[8,16,256]{2,1,0:T(8,128)(2,1)S(1)}, bf16[8,16,256]{2,1,0:T(8,128)(2,1)S(1)}, u32[]{:S(2)}, u32[]{:S(2)}) collective-permute-start(bf16[8,16,256]{2,1,0:T(8,128)(2,1)S(1)} %add_convert_fusion.3), channel_id=1, source_target_pairs={{0,2},{1,3},{2,0},{3,1},{4,6},{5,7},{6,4},{7,5},{8,10},{9,11},{10,... | collective-permute-start | bytes 196616 | tf_op jit(solution)/shard_map/ppermute | solution.py:349
  37.9 4.3 %collective-permute-start.8 = (bf16[8,16,256]{2,1,0:T(8,128)(2,1)S(1)}, bf16[8,16,256]{2,1,0:T(8,128)(2,1)S(1)}, u32[]{:S(2)}, u32[]{:S(2)}) collective-permute-start(bf16[8,16,256]{2,1,0:T(8,128)(2,1)S(1)} %add_convert_fusion.2), channel_id=1, source_target_pairs={{0,2},{1,3},{2,0},{3,1},{4,6},{5,7},{6,4},{7,5},{8,10},{9,11},{10,... | collective-permute-start | bytes 196616 | tf_op jit(solution)/shard_map/ppermute | solution.py:349
  42.3 6.8 %collective-permute-start.9 = (bf16[8,16,256]{2,1,0:T(8,128)(2,1)S(1)}, bf16[8,16,256]{2,1,0:T(8,128)(2,1)S(1)}, u32[]{:S(2)}, u32[]{:S(2)}) collective-permute-start(bf16[8,16,256]{2,1,0:T(8,128)(2,1)S(1)} %get-tuple-element.30.own_ref), channel_id=1, source_target_pairs={{0,8},{8,16},{16,24},{1,9},{9,17},{17,25},{2,10},{10,18},{18,26},{... | collective-permute-start | bytes 196616 | tf_op jit(solution)/shard_map/ppermute | solution.py:328
  48.0 4.6 %collective-permute-start.11 = (bf16[8,16,256]{2,1,0:T(8,128)(2,1)S(1)}, bf16[8,16,256]{2,1,0:T(8,128)(2,1)S(1)}, u32[]{:S(2)}, u32[]{:S(2)}) collective-permute-start(bf16[8,16,256]{2,1,0:T(8,128)(2,1)S(1)} %synthesize.7), channel_id=1, source_target_pairs={{0,4},{4,0},{1,5},{5,1},{2,6},{6,2},{3,7},{7,3},{8,12},{12,8},{9,1... | collective-permute-start | bytes 196616 | tf_op jit(solution)/shard_map/ppermute | solution.py:349
  51.5 4.3 %collective-permute-start.10 = (bf16[8,16,256]{2,1,0:T(8,128)(2,1)S(1)}, bf16[8,16,256]{2,1,0:T(8,128)(2,1)S(1)}, u32[]{:S(2)}, u32[]{:S(2)}) collective-permute-start(bf16[8,16,256]{2,1,0:T(8,128)(2,1)S(1)} %synthesize.6), channel_id=1, source_target_pairs={{0,4},{4,0},{1,5},{5,1},{2,6},{6,2},{3,7},{7,3},{8,12},{12,8},{9,1... | collective-permute-start | bytes 196616 | tf_op jit(solution)/shard_map/ppermute | solution.py:349
  55.9 4.7 %collective-permute-start.15 = (bf16[8,16,256]{2,1,0:T(8,128)(2,1)S(1)}, bf16[8,16,256]{2,1,0:T(8,128)(2,1)S(1)}, u32[]{:S(2)}, u32[]{:S(2)}) collective-permute-start(bf16[8,16,256]{2,1,0:T(8,128)(2,1)S(1)} %get-tuple-element.24.own_ref), channel_id=1, source_target_pairs={{16,8},{17,9},{18,10},{19,11},{20,12},{21,13},{22,14},{23,15}} | collective-permute-start | bytes 196616 | tf_op jit(solution)/shard_map/ppermute | solution.py:338
  56.5 8.0 %collective-permute-start.14 = (bf16[8,16,256]{2,1,0:T(8,128)(2,1)S(1)}, bf16[8,16,256]{2,1,0:T(8,128)(2,1)S(1)}, u32[]{:S(2)}, u32[]{:S(2)}) collective-permute-start(bf16[8,16,256]{2,1,0:T(8,128)(2,1)S(1)} %get-tuple-element.24.own_ref), channel_id=1, source_target_pairs={{8,0},{24,16},{9,1},{25,17},{10,2},{26,18},{11,3},{27,19},{12,4},{... | collective-permute-start | bytes 196616 | tf_op jit(solution)/shard_map/ppermute | solution.py:338
  60.4 6.6 %collective-permute-start.12 = (f32[8,16,256]{2,1,0:T(8,128)S(1)}, f32[8,16,256]{2,1,0:T(8,128)S(1)}, u32[]{:S(2)}, u32[]{:S(2)}) collective-permute-start(f32[8,16,256]{2,1,0:T(8,128)S(1)} %correlate.6), channel_id=1, source_target_pairs={{0,1},{1,0},{2,3},{3,2},{4,5},{5,4},{6,7},{7,6},{8,9},{9,8},{10,11... | collective-permute-start | bytes 393224 | tf_op jit(solution)/shard_map/ppermute | solution.py:349
  67.0 1.7 %collective-permute-start.16 = (f32[8,16,256]{2,1,0:T(8,128)S(1)}, f32[8,16,256]{2,1,0:T(8,128)S(1)}, u32[]{:S(2)}, u32[]{:S(2)}) collective-permute-start(f32[8,16,256]{2,1,0:T(8,128)S(1)} %correlate.7), channel_id=1, source_target_pairs={{0,1},{1,0},{2,3},{3,2},{4,5},{5,4},{6,7},{7,6},{8,9},{9,8},{10,11... | collective-permute-start | bytes 393224 | tf_op jit(solution)/shard_map/ppermute | solution.py:349
  67.1 4.6 %collective-permute-start.13 = (bf16[8,16,256]{2,1,0:T(8,128)(2,1)S(1)}, bf16[8,16,256]{2,1,0:T(8,128)(2,1)S(1)}, u32[]{:S(2)}, u32[]{:S(2)}) collective-permute-start(bf16[8,16,256]{2,1,0:T(8,128)(2,1)S(1)} %add_convert_fusion.1), channel_id=1, source_target_pairs={{0,2},{1,3},{2,0},{3,1},{4,6},{5,7},{6,4},{7,5},{8,10},{9,11},{10,... | collective-permute-start | bytes 196616 | tf_op jit(solution)/shard_map/ppermute | solution.py:349
  68.7 4.3 %collective-permute-start.17 = (bf16[8,16,256]{2,1,0:T(8,128)(2,1)S(1)}, bf16[8,16,256]{2,1,0:T(8,128)(2,1)S(1)}, u32[]{:S(2)}, u32[]{:S(2)}) collective-permute-start(bf16[8,16,256]{2,1,0:T(8,128)(2,1)S(1)} %add_convert_fusion), channel_id=1, source_target_pairs={{0,2},{1,3},{2,0},{3,1},{4,6},{5,7},{6,4},{7,5},{8,10},{9,11},{10,... | collective-permute-start | bytes 196616 | tf_op jit(solution)/shard_map/ppermute | solution.py:349

commit v6 on v5

--- a/solution.py
+++ b/solution.py
@@ -60,7 +60,7 @@
         ],
         compiler_params=pltpu.CompilerParams(vmem_limit_bytes=VMEM),
         name="to_blocks",
-    )(*values)
+    )(*(pltpu.with_memory_space_constraint(value, pltpu.HBM) for value in values))
 
 
 def series_kernel(low_ref, high_ref, out_ref, flat):
@@ -204,31 +204,37 @@
         ],
         compiler_params=pltpu.CompilerParams(vmem_limit_bytes=24 * 1024 * 1024),
         name="bank_tiles",
-    )(atom_bank)
+    )(pltpu.with_memory_space_constraint(atom_bank, pltpu.HBM))
 
 
 def turn_kernel(even_ref, odd_ref, even_out, odd_out):
     tiles = even_ref.shape[0]
     rows = even_out.shape[1]
+    wide = 2 * LANES
     eye = (
-        lax.broadcasted_iota(jnp.int32, (LANES, LANES), 0)
-        == lax.broadcasted_iota(jnp.int32, (LANES, LANES), 1)
+        lax.broadcasted_iota(jnp.int32, (wide, wide), 0)
+        == lax.broadcasted_iota(jnp.int32, (wide, wide), 1)
     ).astype(jnp.bfloat16)
-    unroll = next(n for n in (26, 20, 10, 4, 2) if tiles % n == 0)
+    unroll = next(n for n in (52, 20, 4) if tiles % n == 0)
 
     def loop(turn, carry):
-        for inner in range(0, unroll, 2):
+        for inner in range(0, unroll, 4):
             tile = turn * unroll + inner
             stacked = jnp.concatenate(
-                [odd_ref[tile], even_ref[tile], odd_ref[tile + 1], even_ref[tile + 1]], axis=0
+                [
+                    jnp.concatenate([ref[tile + which], ref[tile + 2 + which]], axis=1)
+                    for which in range(2)
+                    for ref in (odd_ref, even_ref)
+                ],
+                axis=0,
             )
             turned = lax.dot_general(
                 eye, stacked, (((1,), (1,)), ((), ())), preferred_element_type=jnp.float32
             ).astype(jnp.bfloat16)
-            for which in range(2):
-                part = turned[:, which * LANES : (which + 1) * LANES]
+            for which in range(4):
+                part = turned[which // 2 * LANES :, which % 2 * LANES : (which % 2 + 1) * LANES]
                 odd_out[tile + which] = part[:rows]
-                even_out[tile + which] = part[rows:]
+                even_out[tile + which] = part[rows : 2 * rows]
         return carry
 
     lax.fori_loop(0, tiles // unroll, loop, 0)
@@ -328,28 +334,38 @@
     return lax.ppermute(value, axis, [(i, i + steps) for i in range(first, last)])
 
 
-def shifted_by_pairs(value, axis, steps):
-    count = lax.axis_size(axis)
-    total = None
-    for parity in range(2):
-        moves = [(i, i + steps) for i in range(count) if 0 <= i + steps < count]
-        moves = [move for move in moves if min(move) % 2 == parity]
-        if moves:
-            part = lax.ppermute(value, axis, moves)
-            total = part if total is None else total + part
-    return jnp.zeros_like(value) if total is None else total
-
-
-def summed(value, axis):
-    count = lax.axis_size(axis)
+def partner(value, axis, step):
+    return lax.ppermute(value, axis, [(i, i ^ step) for i in range(lax.axis_size(axis))])
+
+
+def after(value, *others):
+    return lax.optimization_barrier((value, *others))[0]
+
+
+def summed(value, axis, gate=None):
     step = 1
-    while step < count:
+    while step < lax.axis_size(axis):
         if step > 1:
             value = value.astype(jnp.bfloat16)
-        other = lax.ppermute(value, axis, [(i, i ^ step) for i in range(count)])
+        other = partner(value, axis, step)
+        step *= 2
+        if gate is not None and step >= lax.axis_size(axis):
+            other = after(other, gate)
         value = value.astype(jnp.float32) + other.astype(jnp.float32)
+    return value
+
+
+def summed_both(first, second, axis):
+    if lax.axis_size(axis) == 1:
+        return first, second
+    both = jnp.stack([first + partner(first, axis, 1), second + partner(second, axis, 1)])
+    step = 2
+    while step < lax.axis_size(axis):
+        both = both.astype(jnp.bfloat16)
+        other = partner(both, axis, step)
+        both = both.astype(jnp.float32) + other.astype(jnp.float32)
         step *= 2
-    return value
+    return both[0], both[1]
 
 
 def body(signal, codes_init, atom_bank, step_size, threshold):
@@ -368,27 +384,33 @@
         return moved - jnp.clip(moved, -bound, bound)
 
     turned = None
+    low16, high16 = low.astype(jnp.bfloat16), high.astype(jnp.bfloat16)
+    earlier = shifted(high16, "tm", 1)
     for sweep in range(ITERS):
-        low16, high16 = low.astype(jnp.bfloat16), high.astype(jnp.bfloat16)
-        earlier = shifted(high16, "tm", 1)
-        if sweep == 0:
-            recon_low = convolve(low16, earlier, tiles, False)
-            high16, recon_low = lax.optimization_barrier((high16, recon_low))
-            recon_high = convolve(high16, low16, tiles, False)
-            turned = turn_tiles(*tiles)
+        recon_low = convolve(low16, earlier, tiles, False)
+        recon_high = convolve(after(high16, recon_low), low16, tiles, False)
+        misfit_low = summed(recon_low, "atom") - heard_low
+        rounded_low = misfit_low.astype(jnp.bfloat16)
+        following = shifted(rounded_low, "tm", -1)
+        gate = None
+        if turned is None:
+            turned = turn_tiles(*(after(tile, rounded_low) for tile in tiles))
+            gate = turned[0]
+        misfit_high = summed(recon_high, "atom", gate) - heard_high
+        rounded_high = misfit_high.astype(jnp.bfloat16)
+        if sweep < ITERS - 1:
+            gradient_high = convolve(rounded_high, following, turned, True)
+            gradient_low = convolve(after(rounded_low, gradient_high), rounded_high, turned, True)
+            high = shrink(high, summed(gradient_high, "chan"))
+            high16 = high.astype(jnp.bfloat16)
+            earlier = shifted(high16, "tm", 1)
+            low = shrink(low, summed(gradient_low, "chan", earlier))
+            low16 = low.astype(jnp.bfloat16)
         else:
-            recon_high = convolve(high16, low16, tiles, False)
-            recon_low = convolve(low16, earlier, tiles, False)
-        recon_low, recon_high = summed(recon_low, "atom"), summed(recon_high, "atom")
-        misfit_low = recon_low - heard_low
-        misfit_high = recon_high - heard_high
-        rounded_low = misfit_low.astype(jnp.bfloat16)
-        rounded_high = misfit_high.astype(jnp.bfloat16)
-        following = shifted_by_pairs(rounded_low, "tm", -1)
-        gradient_low = summed(convolve(rounded_low, rounded_high, turned, True), "chan")
-        gradient_high = summed(convolve(rounded_high, following, turned, True), "chan")
-        low = shrink(low, gradient_low)
-        high = shrink(high, gradient_high)
+            gradient_low = convolve(rounded_low, rounded_high, turned, True)
+            gradient_high = convolve(rounded_high, following, turned, True)
+            gradient_low, gradient_high = summed_both(gradient_low, gradient_high, "chan")
+            low, high = shrink(low, gradient_low), shrink(high, gradient_high)
     return from_blocks(low, high), from_blocks(misfit_low, misfit_high)[:chans]
 
 

time: 75.2 us -> 67.8 us (0.902); the launches traced: 74.2 us -> 67.6 us
  local copies, waits for them, and re-layouts: 4.04 us -> 0.01 us
  starting transfers between devices: 22.9 us -> 20.6 us
  waiting for transfers between devices: 14.5 us -> 12.8 us
  Pallas kernels: 31.2 us -> 32.1 us
    ppermute x16 -> x11, waiting for transfers between devices: 14.5 us -> 8.69 us  [partner(): lax.ppermute(value, axis, [(i, i ^ step) for i in range(lax.axis_size(axi...]
    ppermute x16 -> x11, starting transfers between devices: 14.7 us -> 9.2 us  [partner(): lax.ppermute(value, axis, [(i, i ^ step) for i in range(lax.axis_size(axi...]
    ppermute x2 -> x4, waiting for transfers between devices: 0.01 us -> 4.06 us  [shifted(): lax.ppermute(value, axis, [(i, i + steps) for i in range(first, last)])]
    unnamed x10 -> x2, local copies, waits for them, and re-layouts: 4.04 us -> 0.01 us
    ppermute x2 -> x4, starting transfers between devices: 8.25 us -> 11.4 us  [shifted(): lax.ppermute(value, axis, [(i, i + steps) for i in range(first, last)])]
    pallas_call x1, Pallas kernels: 0.58 us -> 1.36 us  [to_blocks(): pl.pallas_call(functools.partial(blocks_kernel, len(values)), in_specs=[p...]
  transfers between devices with their start and end apart: 18 -> 15, of which waited for: 8 -> 8; matrix products, arithmetic and copies ran while one was open for 0% -> 2% of each run, Pallas kernels for 37% -> 33%
where the time goes in v6:
time: 67.8 us; the launch traced here: 67.6 us
  Pallas kernels  32.1 us (47%)
  starting transfers between devices  20.6 us (30%)
  waiting for transfers between devices  12.8 us (19%)
  other arithmetic  1.28 us (2%)
  between operations  0.89 us (1%)
    pallas_call x8, Pallas kernels, convolve(): pl.pallas_call(functools.partial(conv_kernel, transposed, steps), in_spec...  19.1 us
    ppermute x4, starting transfers between devices, shifted(): lax.ppermute(value, axis, [(i, i + steps) for i in range(first, last)])  11.4 us
    ppermute x11, starting transfers between devices, partner(): lax.ppermute(value, axis, [(i, i ^ step) for i in range(lax.axis_size(axi...  9.2 us
    ppermute x11, waiting for transfers between devices, partner(): lax.ppermute(value, axis, [(i, i ^ step) for i in range(lax.axis_size(axi...  8.69 us
    pallas_call x1, Pallas kernels, bank_tiles(): pl.pallas_call(functools.partial(bank_kernel, rows), in_specs=[pl.BlockSp...  6.36 us
    ppermute x4, waiting for transfers between devices, shifted(): lax.ppermute(value, axis, [(i, i + steps) for i in range(first, last)])  4.06 us
    pallas_call x1, Pallas kernels, turn_tiles(): pl.pallas_call(turn_kernel, in_specs=[spec, spec], out_specs=[spec, spec]...  3.24 us
    pallas_call x2, Pallas kernels, from_blocks(): pl.pallas_call(series_kernel, in_specs=[pl.BlockSpec(memory_space=pltpu.V...  2 us
  transfers between devices with their start and end apart: 15, of which 8 were waited for; matrix products, arithmetic and copies ran while one was open for 2% of the time, Pallas kernels for 33%

profile of v6, /device:TPU:0, one launch (start us, length us, event | category | flops | bytes accessed | tf_op | source)
XLA Modules:
  0.0 67.6 jit_solution(14912163809933796428)
XLA Ops:
  0.6 0.0 copy-start
  0.6 1.4 %to_blocks.1 = (f32[8,16,256]{2,1,0:T(8,128)S(1)}, f32[8,16,256]{2,1,0:T(8,128)S(1)}, f32[8,16,256]{2,1,0:T(8,128)S(1)}, f32[8,16,256]{2,1,0:T(8,128)S(1)}) custom-call(f32[64,1024]{1,0:T(8,128)} %refs_0_.1, bf16[64,1024]{1,0:T(8,128)(2,1)} %refs_1_.1), custom_call_target="tpu_custom_call" | custom-call | tf_op jit(solution)/shard_map/to_blocks/pallas_call | solution.py:51
  2.0 4.9 %collective-permute-start = (bf16[8,16,256]{2,1,0:T(8,128)(2,1)S(1)}, bf16[8,16,256]{2,1,0:T(8,128)(2,1)S(1)}, u32[]{:S(2)}, u32[]{:S(2)}) collective-permute-start(bf16[8,16,256]{2,1,0:T(8,128)(2,1)S(1)} %convert_element_type.74.own_ref), channel_id=1, source_target_pairs={{0,8},{8,16},{16,24},{1,9},{9,17},{17,25},{2,10},{10,18},{18,26},{... | collective-permute-start | bytes 196616 | tf_op jit(solution)/shard_map/ppermute | solution.py:334
  7.0 0.7 %mul.14 = f32[64]{0:T(128)S(1)} multiply(f32[64]{0:T(128)} %param.8, f32[64]{0:T(128)} %param.9) | non-fusion elementwise | flops 64 | bytes 768 | tf_op jit(solution)/shard_map/mul | solution.py:380
  7.6 0.1 fusion.10
  7.7 6.4 %bank_tiles.1 = (bf16[260,64,128]{2,1,0:T(8,128)(2,1)S(1)}, bf16[260,64,128]{2,1,0:T(8,128)(2,1)S(1)}) custom-call(bf16[64,64,512]{2,1,0:T(8,128)(2,1)} %bank_hbm.1), custom_call_target="tpu_custom_call" | custom-call | tf_op jit(solution)/shard_map/bank_tiles/pallas_call | solution.py:195
  14.1 0.1 pad_maximum_fusion.1
  14.2 0.0 collective-permute-done.beside_ref
  14.2 2.4 %synthesize.4 = bf16[8,16,256]{2,1,0:T(8,128)(2,1)S(1)} custom-call(bf16[8,16,256]{2,1,0:T(8,128)(2,1)S(1)} %convert_element_type.73.own_ref.beside_ref, bf16[8,16,256]{2,1,0:T(8,128)(2,1)S(1)} %collective-permute-done.beside_ref, bf16[260,64,128]{2,1,0:T(8,128)(2,1)S(1)} %get-tuple-element.23.even.even_ref, ...), custom_call_target="tpu_custom_call" | custom-call | flops 2164260864 | bytes 8781824 | tf_op jit(solution)/shard_map/synthesize/pallas_call | solution.py:311
  16.6 1.5 %collective-permute-start.1 = (bf16[8,16,256]{2,1,0:T(8,128)(2,1)S(1)}, bf16[8,16,256]{2,1,0:T(8,128)(2,1)S(1)}, u32[]{:S(2)}, u32[]{:S(2)}) collective-permute-start(bf16[8,16,256]{2,1,0:T(8,128)(2,1)S(1)} %synthesize.4), channel_id=1, source_target_pairs={{0,4},{4,0},{1,5},{5,1},{2,6},{6,2},{3,7},{7,3},{8,12},{12,8},{9,1... | collective-permute-start | bytes 196616 | tf_op jit(solution)/shard_map/ppermute | solution.py:338
  18.1 2.4 %synthesize.5 = bf16[8,16,256]{2,1,0:T(8,128)(2,1)S(1)} custom-call(bf16[8,16,256]{2,1,0:T(8,128)(2,1)S(1)} %convert_element_type.74.own_ref, bf16[8,16,256]{2,1,0:T(8,128)(2,1)S(1)} %convert_element_type.73.own_ref.beside_ref, bf16[260,64,128]{2,1,0:T(8,128)(2,1)S(1)} %get-tuple-element.23.even.even_ref, bf16[260,64,128]{2,1,0:T(8,128)(2,1)S(1)} %get-tuple-element.24.odd.odd_ref), custom_call_target="tpu_custom_call" | custom-call | flops 2164260864 | bytes 8781824 | tf_op jit(solution)/shard_map/synthesize/pallas_call | solution.py:311
  20.5 0.6 collective-permute-start.2
  21.1 0.0 collective-permute-done.1
  21.2 1.5 %collective-permute-start.3 = (bf16[8,16,256]{2,1,0:T(8,128)(2,1)S(1)}, bf16[8,16,256]{2,1,0:T(8,128)(2,1)S(1)}, u32[]{:S(2)}, u32[]{:S(2)}) collective-permute-start(bf16[8,16,256]{2,1,0:T(8,128)(2,1)S(1)} %subtract_convert_fusion.1.own_ref), channel_id=1, source_target_pairs={{8,0},{16,8},{24,16},{9,1},{17,9},{25,17},{10,2},{18,10},{26,18},{... | collective-permute-start | bytes 196616 | tf_op jit(solution)/shard_map/ppermute | solution.py:334
  22.7 3.2 %turn_tiles.1 = (bf16[260,64,128]{2,1,0:T(8,128)(2,1)S(1)}, bf16[260,64,128]{2,1,0:T(8,128)(2,1)S(1)}) custom-call(bf16[260,64,128]{2,1,0:T(8,128)(2,1)S(1)} %get-tuple-element.23.even.even_ref, bf16[260,64,128]{2,1,0:T(8,128)(2,1)S(1)} %get-tuple-element.24.odd.odd_ref), custom_call_target="tpu_custom_call" | custom-call | flops 2181038080 | bytes 17039360 | tf_op jit(solution)/shard_map/turn_tiles/pallas_call | solution.py:247
  25.9 0.0 collective-permute-done.2
  25.9 1.4 %collective-permute-done.3.beside_ref = bf16[8,16,256]{2,1,0:T(8,128)(2,1)S(1)} collective-permute-done((bf16[8,16,256]{2,1,0:T(8,128)(2,1)S(1)}, bf16[8,16,256]{2,1,0:T(8,128)(2,1)S(1)}, u32[]{:S(2)}, u32[]{:S(2)}) %collective-permute-start.3) | collective-permute-done | bytes 65568 | tf_op jit(solution)/shard_map/ppermute | solution.py:334
  27.3 2.4 %correlate.4 = f32[8,16,256]{2,1,0:T(8,128)S(1)} custom-call(bf16[8,16,256]{2,1,0:T(8,128)(2,1)S(1)} %subtract_convert_fusion.own_ref.beside_ref, bf16[8,16,256]{2,1,0:T(8,128)(2,1)S(1)} %collective-permute-done.3.beside_ref, bf16[260,64,128]{2,1,0:T(8,128)(2,1)S(1)} %get-tuple-element.25.even, bf16[260,64,128]{2,1,0:T(8,128)(2,1)S(1)} %get-tuple-element.28.odd), custom_call_target="tpu_custom_call" | custom-call | flops 2164260864 | bytes 8781824 | tf_op jit(solution)/shard_map/correlate/pallas_call | solution.py:311
  29.7 0.1 collective-permute-start.6
  29.8 2.4 %correlate.5 = f32[8,16,256]{2,1,0:T(8,128)S(1)} custom-call(bf16[8,16,256]{2,1,0:T(8,128)(2,1)S(1)} %subtract_convert_fusion.1.own_ref, bf16[8,16,256]{2,1,0:T(8,128)(2,1)S(1)} %subtract_convert_fusion.own_ref.beside_ref, bf16[260,64,128]{2,1,0:T(8,128)(2,1)S(1)} %get-tuple-element.25.even, bf16[260,64,128]{2,1,0:T(8,128)(2,1)S(1)} %get-tuple-element.28.odd), custom_call_target="tpu_custom_call" | custom-call | flops 2164260864 | bytes 8781824 | tf_op jit(solution)/shard_map/correlate/pallas_call | solution.py:311
  32.2 0.6 collective-permute-start.4
  32.8 0.0 collective-permute-done.6
  32.8 1.6 %collective-permute-start.7 = (bf16[8,16,256]{2,1,0:T(8,128)(2,1)S(1)}, bf16[8,16,256]{2,1,0:T(8,128)(2,1)S(1)}, u32[]{:S(2)}, u32[]{:S(2)}) collective-permute-start(bf16[8,16,256]{2,1,0:T(8,128)(2,1)S(1)} %add_convert_fusion.2), channel_id=1, source_target_pairs={{0,2},{1,3},{2,0},{3,1},{4,6},{5,7},{6,4},{7,5},{8,10},{9,11},{10,... | collective-permute-start | bytes 196616 | tf_op jit(solution)/shard_map/ppermute | solution.py:338
  34.4 0.0 collective-permute-done.4
  34.4 1.0 %collective-permute-start.5 = (bf16[8,16,256]{2,1,0:T(8,128)(2,1)S(1)}, bf16[8,16,256]{2,1,0:T(8,128)(2,1)S(1)}, u32[]{:S(2)}, u32[]{:S(2)}) collective-permute-start(bf16[8,16,256]{2,1,0:T(8,128)(2,1)S(1)} %add_convert_fusion.3), channel_id=1, source_target_pairs={{0,2},{1,3},{2,0},{3,1},{4,6},{5,7},{6,4},{7,5},{8,10},{9,11},{10,... | collective-permute-start | bytes 196616 | tf_op jit(solution)/shard_map/ppermute | solution.py:338
  35.4 2.2 %collective-permute-done.7 = bf16[8,16,256]{2,1,0:T(8,128)(2,1)S(1)} collective-permute-done((bf16[8,16,256]{2,1,0:T(8,128)(2,1)S(1)}, bf16[8,16,256]{2,1,0:T(8,128)(2,1)S(1)}, u32[]{:S(2)}, u32[]{:S(2)}) %collective-permute-start.7) | collective-permute-done | bytes 65568 | tf_op jit(solution)/shard_map/ppermute | solution.py:338
  37.6 3.5 %collective-permute-start.8 = (bf16[8,16,256]{2,1,0:T(8,128)(2,1)S(1)}, bf16[8,16,256]{2,1,0:T(8,128)(2,1)S(1)}, u32[]{:S(2)}, u32[]{:S(2)}) collective-permute-start(bf16[8,16,256]{2,1,0:T(8,128)(2,1)S(1)} %fusion.6.own_ref), channel_id=1, source_target_pairs={{0,8},{8,16},{16,24},{1,9},{9,17},{17,25},{2,10},{10,18},{18,26},{... | collective-permute-start | bytes 196616 | tf_op jit(solution)/shard_map/ppermute | solution.py:334
  41.1 0.0 collective-permute-done.5
  41.1 1.9 %collective-permute-done.8.beside_ref = bf16[8,16,256]{2,1,0:T(8,128)(2,1)S(1)} collective-permute-done((bf16[8,16,256]{2,1,0:T(8,128)(2,1)S(1)}, bf16[8,16,256]{2,1,0:T(8,128)(2,1)S(1)}, u32[]{:S(2)}, u32[]{:S(2)}) %collective-permute-start.8) | collective-permute-done | bytes 65568 | tf_op jit(solution)/shard_map/ppermute | solution.py:334
  43.0 2.4 %synthesize.6 = bf16[8,16,256]{2,1,0:T(8,128)(2,1)S(1)} custom-call(bf16[8,16,256]{2,1,0:T(8,128)(2,1)S(1)} %fusion.7.own_ref.beside_ref, bf16[8,16,256]{2,1,0:T(8,128)(2,1)S(1)} %collective-permute-done.8.beside_ref, bf16[260,64,128]{2,1,0:T(8,128)(2,1)S(1)} %get-tuple-element.23.even.even_ref, bf16[260,64,128]{2,1,0:T(8,128)(2,1)S(1)} %get-tuple-element.24.odd.odd_ref), custom_call_target="tpu_custom_call" | custom-call | flops 2164260864 | bytes 8781824 | tf_op jit(solution)/shard_map/synthesize/pallas_call | solution.py:311
  45.4 1.5 %collective-permute-start.9 = (bf16[8,16,256]{2,1,0:T(8,128)(2,1)S(1)}, bf16[8,16,256]{2,1,0:T(8,128)(2,1)S(1)}, u32[]{:S(2)}, u32[]{:S(2)}) collective-permute-start(bf16[8,16,256]{2,1,0:T(8,128)(2,1)S(1)} %synthesize.6), channel_id=1, source_target_pairs={{0,4},{4,0},{1,5},{5,1},{2,6},{6,2},{3,7},{7,3},{8,12},{12,8},{9,1... | collective-permute-start | bytes 196616 | tf_op jit(solution)/shard_map/ppermute | solution.py:338
  46.9 2.4 %synthesize.7 = bf16[8,16,256]{2,1,0:T(8,128)(2,1)S(1)} custom-call(bf16[8,16,256]{2,1,0:T(8,128)(2,1)S(1)} %fusion.6.own_ref, bf16[8,16,256]{2,1,0:T(8,128)(2,1)S(1)} %fusion.7.own_ref.beside_ref, bf16[260,64,128]{2,1,0:T(8,128)(2,1)S(1)} %get-tuple-element.23.even.even_ref, bf16[260,64,128]{2,1,0:T(8,128)(2,1)S(1)} %get-tuple-element.24.odd.odd_ref), custom_call_target="tpu_custom_call" | custom-call | flops 2164260864 | bytes 8781824 | tf_op jit(solution)/shard_map/synthesize/pallas_call | solution.py:311
  49.3 0.6 collective-permute-start.10
  49.9 0.2 collective-permute-done.9
  50.2 1.5 %collective-permute-start.12 = (bf16[8,16,256]{2,1,0:T(8,128)(2,1)S(1)}, bf16[8,16,256]{2,1,0:T(8,128)(2,1)S(1)}, u32[]{:S(2)}, u32[]{:S(2)}) collective-permute-start(bf16[8,16,256]{2,1,0:T(8,128)(2,1)S(1)} %get-tuple-element.32.own_ref), channel_id=1, source_target_pairs={{8,0},{16,8},{24,16},{9,1},{17,9},{25,17},{10,2},{18,10},{26,18},{... | collective-permute-start | bytes 196616 | tf_op jit(solution)/shard_map/ppermute | solution.py:334
  51.7 2.0 %collective-permute-done.10 = bf16[8,16,256]{2,1,0:T(8,128)(2,1)S(1)} collective-permute-done((bf16[8,16,256]{2,1,0:T(8,128)(2,1)S(1)}, bf16[8,16,256]{2,1,0:T(8,128)(2,1)S(1)}, u32[]{:S(2)}, u32[]{:S(2)}) %collective-permute-start.10) | collective-permute-done | bytes 65568 | tf_op jit(solution)/shard_map/ppermute | solution.py:338
  53.7 2.4 %correlate.6 = f32[8,16,256]{2,1,0:T(8,128)S(1)} custom-call(bf16[8,16,256]{2,1,0:T(8,128)(2,1)S(1)} %get-tuple-element.32.own_ref, bf16[8,16,256]{2,1,0:T(8,128)(2,1)S(1)} %get-tuple-element.34.beside_ref.own_ref, bf16[260,64,128]{2,1,0:T(8,128)(2,1)S(1)} %get-tuple-element.25.even, bf16[260,64,128]{2,1,0:T(8,128)(2,1)S(1)} %get-tuple-element.28.odd), custom_call_target="tpu_custom_call" | custom-call | flops 2164260864 | bytes 8781824 | tf_op jit(solution)/shard_map/correlate/pallas_call | solution.py:311
  56.1 0.1 collective-permute-start.11
  56.2 0.8 %collective-permute-done.12.beside_ref = bf16[8,16,256]{2,1,0:T(8,128)(2,1)S(1)} collective-permute-done((bf16[8,16,256]{2,1,0:T(8,128)(2,1)S(1)}, bf16[8,16,256]{2,1,0:T(8,128)(2,1)S(1)}, u32[]{:S(2)}, u32[]{:S(2)}) %collective-permute-start.12) | collective-permute-done | bytes 65568 | tf_op jit(solution)/shard_map/ppermute | solution.py:334
  57.0 2.4 %correlate.7 = f32[8,16,256]{2,1,0:T(8,128)S(1)} custom-call(bf16[8,16,256]{2,1,0:T(8,128)(2,1)S(1)} %get-tuple-element.34.beside_ref.own_ref, bf16[8,16,256]{2,1,0:T(8,128)(2,1)S(1)} %collective-permute-done.12.beside_ref, bf16[260,64,128]{2,1,0:T(8,128)(2,1)S(1)} %get-tuple-element.25.even, bf16[260,64,128]{2,1,0:T(8,128)(2,1)S(1)} %get-tuple-element.28.odd), custom_call_target="tpu_custom_call" | custom-call | flops 2164260864 | bytes 8781824 | tf_op jit(solution)/shard_map/correlate/pallas_call | solution.py:311
  59.4 0.1 collective-permute-start.13
  59.4 0.0 collective-permute-done.11
  59.5 1.3 %collective-permute-done.13 = f32[8,16,256]{2,1,0:T(8,128)S(1)} collective-permute-done((f32[8,16,256]{2,1,0:T(8,128)S(1)}, f32[8,16,256]{2,1,0:T(8,128)S(1)}, u32[]{:S(2)}, u32[]{:S(2)}) %collective-permute-start.13) | collective-permute-done | bytes 131104 | tf_op jit(solution)/shard_map/ppermute | solution.py:338
  60.8 1.6 %collective-permute-start.14 = (bf16[2,8,16,256]{3,2,1,0:T(8,128)(2,1)S(1)}, bf16[2,8,16,256]{3,2,1,0:T(8,128)(2,1)S(1)}, u32[]{:S(2)}, u32[]{:S(2)}) collective-permute-start(bf16[2,8,16,256]{3,2,1,0:T(8,128)(2,1)S(1)} %pad_maximum_fusion), channel_id=1, source_target_pairs={{0,2},{1,3},{2,0},{3,1},{4,6},{5,7},{6,4},{7,5},{8,10},{9,11},{10,... | collective-permute-start | bytes 393224 | tf_op jit(solution)/shard_map/ppermute | solution.py:338
  62.4 1.0 %from_blocks.3 = f32[64,1024]{1,0:T(8,128)} custom-call(f32[8,16,256]{2,1,0:T(8,128)S(1)} %get-tuple-element.33.low_ref, f32[8,16,256]{2,1,0:T(8,128)S(1)} %get-tuple-element.35.high_ref), custom_call_target="tpu_custom_call" | custom-call | tf_op jit(solution)/shard_map/from_blocks/pallas_call | solution.py:87
  63.4 3.0 %collective-permute-done.14 = bf16[2,8,16,256]{3,2,1,0:T(8,128)(2,1)S(1)} collective-permute-done((bf16[2,8,16,256]{3,2,1,0:T(8,128)(2,1)S(1)}, bf16[2,8,16,256]{3,2,1,0:T(8,128)(2,1)S(1)}, u32[]{:S(2)}, u32[]{:S(2)}) %collective-permute-start.14) | collective-permute-done | bytes 131104 | tf_op jit(solution)/shard_map/ppermute | solution.py:338
  66.5 0.1 minimum_subtract_fusion
  66.6 1.0 %from_blocks.2 = f32[64,1024]{1,0:T(8,128)} custom-call(f32[8,16,256]{2,1,0:T(8,128)S(1)} %get-tuple-element.39.low_ref, f32[8,16,256]{2,1,0:T(8,128)S(1)} %get-tuple-element.38.high_ref), custom_call_target="tpu_custom_call" | custom-call | tf_op jit(solution)/shard_map/from_blocks/pallas_call | solution.py:87
  (15 shorter events, 0.3 us)
Async XLA Ops:
  0.6 13.5 %copy-start = (f32[64]{0:T(128)S(1)}, f32[64]{0:T(128)}, u32[]{:S(2)}) copy-start(f32[64]{0:T(128)} %param.8) | copy-start | bytes 772
  2.0 12.2 %collective-permute-start = (bf16[8,16,256]{2,1,0:T(8,128)(2,1)S(1)}, bf16[8,16,256]{2,1,0:T(8,128)(2,1)S(1)}, u32[]{:S(2)}, u32[]{:S(2)}) collective-permute-start(bf16[8,16,256]{2,1,0:T(8,128)(2,1)S(1)} %convert_element_type.74.own_ref), channel_id=1, source_target_pairs={{0,8},{8,16},{16,24},{1,9},{9,17},{17,25},{2,10},{10,18},{18,26},{... | collective-permute-start | bytes 196616 | tf_op jit(solution)/shard_map/ppermute | solution.py:334
  16.6 4.6 %collective-permute-start.1 = (bf16[8,16,256]{2,1,0:T(8,128)(2,1)S(1)}, bf16[8,16,256]{2,1,0:T(8,128)(2,1)S(1)}, u32[]{:S(2)}, u32[]{:S(2)}) collective-permute-start(bf16[8,16,256]{2,1,0:T(8,128)(2,1)S(1)} %synthesize.4), channel_id=1, source_target_pairs={{0,4},{4,0},{1,5},{5,1},{2,6},{6,2},{3,7},{7,3},{8,12},{12,8},{9,1... | collective-permute-start | bytes 196616 | tf_op jit(solution)/shard_map/ppermute | solution.py:338
  20.5 5.4 %collective-permute-start.2 = (bf16[8,16,256]{2,1,0:T(8,128)(2,1)S(1)}, bf16[8,16,256]{2,1,0:T(8,128)(2,1)S(1)}, u32[]{:S(2)}, u32[]{:S(2)}) collective-permute-start(bf16[8,16,256]{2,1,0:T(8,128)(2,1)S(1)} %synthesize.5), channel_id=1, source_target_pairs={{0,4},{4,0},{1,5},{5,1},{2,6},{6,2},{3,7},{7,3},{8,12},{12,8},{9,1... | collective-permute-start | bytes 196616 | tf_op jit(solution)/shard_map/ppermute | solution.py:338
  21.2 6.2 %collective-permute-start.3 = (bf16[8,16,256]{2,1,0:T(8,128)(2,1)S(1)}, bf16[8,16,256]{2,1,0:T(8,128)(2,1)S(1)}, u32[]{:S(2)}, u32[]{:S(2)}) collective-permute-start(bf16[8,16,256]{2,1,0:T(8,128)(2,1)S(1)} %subtract_convert_fusion.1.own_ref), channel_id=1, source_target_pairs={{8,0},{16,8},{24,16},{9,1},{17,9},{25,17},{10,2},{18,10},{26,18},{... | collective-permute-start | bytes 196616 | tf_op jit(solution)/shard_map/ppermute | solution.py:334
  29.7 3.0 %collective-permute-start.6 = (f32[8,16,256]{2,1,0:T(8,128)S(1)}, f32[8,16,256]{2,1,0:T(8,128)S(1)}, u32[]{:S(2)}, u32[]{:S(2)}) collective-permute-start(f32[8,16,256]{2,1,0:T(8,128)S(1)} %correlate.4), channel_id=1, source_target_pairs={{0,1},{1,0},{2,3},{3,2},{4,5},{5,4},{6,7},{7,6},{8,9},{9,8},{10,11... | collective-permute-start | bytes 393224 | tf_op jit(solution)/shard_map/ppermute | solution.py:338
  32.2 2.2 %collective-permute-start.4 = (f32[8,16,256]{2,1,0:T(8,128)S(1)}, f32[8,16,256]{2,1,0:T(8,128)S(1)}, u32[]{:S(2)}, u32[]{:S(2)}) collective-permute-start(f32[8,16,256]{2,1,0:T(8,128)S(1)} %correlate.5), channel_id=1, source_target_pairs={{0,1},{1,0},{2,3},{3,2},{4,5},{5,4},{6,7},{7,6},{8,9},{9,8},{10,11... | collective-permute-start | bytes 393224 | tf_op jit(solution)/shard_map/ppermute | solution.py:338
  32.8 4.7 %collective-permute-start.7 = (bf16[8,16,256]{2,1,0:T(8,128)(2,1)S(1)}, bf16[8,16,256]{2,1,0:T(8,128)(2,1)S(1)}, u32[]{:S(2)}, u32[]{:S(2)}) collective-permute-start(bf16[8,16,256]{2,1,0:T(8,128)(2,1)S(1)} %add_convert_fusion.2), channel_id=1, source_target_pairs={{0,2},{1,3},{2,0},{3,1},{4,6},{5,7},{6,4},{7,5},{8,10},{9,11},{10,... | collective-permute-start | bytes 196616 | tf_op jit(solution)/shard_map/ppermute | solution.py:338
  34.4 6.7 %collective-permute-start.5 = (bf16[8,16,256]{2,1,0:T(8,128)(2,1)S(1)}, bf16[8,16,256]{2,1,0:T(8,128)(2,1)S(1)}, u32[]{:S(2)}, u32[]{:S(2)}) collective-permute-start(bf16[8,16,256]{2,1,0:T(8,128)(2,1)S(1)} %add_convert_fusion.3), channel_id=1, source_target_pairs={{0,2},{1,3},{2,0},{3,1},{4,6},{5,7},{6,4},{7,5},{8,10},{9,11},{10,... | collective-permute-start | bytes 196616 | tf_op jit(solution)/shard_map/ppermute | solution.py:338
  37.6 5.4 %collective-permute-start.8 = (bf16[8,16,256]{2,1,0:T(8,128)(2,1)S(1)}, bf16[8,16,256]{2,1,0:T(8,128)(2,1)S(1)}, u32[]{:S(2)}, u32[]{:S(2)}) collective-permute-start(bf16[8,16,256]{2,1,0:T(8,128)(2,1)S(1)} %fusion.6.own_ref), channel_id=1, source_target_pairs={{0,8},{8,16},{16,24},{1,9},{9,17},{17,25},{2,10},{10,18},{18,26},{... | collective-permute-start | bytes 196616 | tf_op jit(solution)/shard_map/ppermute | solution.py:334
  45.4 4.7 %collective-permute-start.9 = (bf16[8,16,256]{2,1,0:T(8,128)(2,1)S(1)}, bf16[8,16,256]{2,1,0:T(8,128)(2,1)S(1)}, u32[]{:S(2)}, u32[]{:S(2)}) collective-permute-start(bf16[8,16,256]{2,1,0:T(8,128)(2,1)S(1)} %synthesize.6), channel_id=1, source_target_pairs={{0,4},{4,0},{1,5},{5,1},{2,6},{6,2},{3,7},{7,3},{8,12},{12,8},{9,1... | collective-permute-start | bytes 196616 | tf_op jit(solution)/shard_map/ppermute | solution.py:338
  49.3 4.3 %collective-permute-start.10 = (bf16[8,16,256]{2,1,0:T(8,128)(2,1)S(1)}, bf16[8,16,256]{2,1,0:T(8,128)(2,1)S(1)}, u32[]{:S(2)}, u32[]{:S(2)}) collective-permute-start(bf16[8,16,256]{2,1,0:T(8,128)(2,1)S(1)} %synthesize.7), channel_id=1, source_target_pairs={{0,4},{4,0},{1,5},{5,1},{2,6},{6,2},{3,7},{7,3},{8,12},{12,8},{9,1... | collective-permute-start | bytes 196616 | tf_op jit(solution)/shard_map/ppermute | solution.py:338
  50.2 6.8 %collective-permute-start.12 = (bf16[8,16,256]{2,1,0:T(8,128)(2,1)S(1)}, bf16[8,16,256]{2,1,0:T(8,128)(2,1)S(1)}, u32[]{:S(2)}, u32[]{:S(2)}) collective-permute-start(bf16[8,16,256]{2,1,0:T(8,128)(2,1)S(1)} %get-tuple-element.32.own_ref), channel_id=1, source_target_pairs={{8,0},{16,8},{24,16},{9,1},{17,9},{25,17},{10,2},{18,10},{26,18},{... | collective-permute-start | bytes 196616 | tf_op jit(solution)/shard_map/ppermute | solution.py:334
  56.1 3.4 %collective-permute-start.11 = (f32[8,16,256]{2,1,0:T(8,128)S(1)}, f32[8,16,256]{2,1,0:T(8,128)S(1)}, u32[]{:S(2)}, u32[]{:S(2)}) collective-permute-start(f32[8,16,256]{2,1,0:T(8,128)S(1)} %correlate.6), channel_id=1, source_target_pairs={{0,1},{1,0},{2,3},{3,2},{4,5},{5,4},{6,7},{7,6},{8,9},{9,8},{10,11... | collective-permute-start | bytes 393224 | tf_op jit(solution)/shard_map/ppermute | solution.py:338
  59.4 1.4 %collective-permute-start.13 = (f32[8,16,256]{2,1,0:T(8,128)S(1)}, f32[8,16,256]{2,1,0:T(8,128)S(1)}, u32[]{:S(2)}, u32[]{:S(2)}) collective-permute-start(f32[8,16,256]{2,1,0:T(8,128)S(1)} %correlate.7), channel_id=1, source_target_pairs={{0,1},{1,0},{2,3},{3,2},{4,5},{5,4},{6,7},{7,6},{8,9},{9,8},{10,11... | collective-permute-start | bytes 393224 | tf_op jit(solution)/shard_map/ppermute | solution.py:338
  60.8 5.6 %collective-permute-start.14 = (bf16[2,8,16,256]{3,2,1,0:T(8,128)(2,1)S(1)}, bf16[2,8,16,256]{3,2,1,0:T(8,128)(2,1)S(1)}, u32[]{:S(2)}, u32[]{:S(2)}) collective-permute-start(bf16[2,8,16,256]{3,2,1,0:T(8,128)(2,1)S(1)} %pad_maximum_fusion), channel_id=1, source_target_pairs={{0,2},{1,3},{2,0},{3,1},{4,6},{5,7},{6,4},{7,5},{8,10},{9,11},{10,... | collective-permute-start | bytes 393224 | tf_op jit(solution)/shard_map/ppermute | solution.py:338

commit v7 on v6

--- a/solution.py
+++ b/solution.py
@@ -15,15 +15,17 @@
 
 
 def blocks_kernel(count, *refs):
-    values, outs = refs[:count], refs[count : 3 * count]
-    held, flat, sems = refs[3 * count : 4 * count], refs[-2], refs[-1]
+    values, vectors = refs[:count], refs[count : count + 2]
+    outs, vector_outs = refs[count + 2 : 3 * count + 2], refs[3 * count + 2 : 3 * count + 4]
+    held = refs[3 * count + 4 : 4 * count + 6]
+    flat, sems = refs[-2:]
     copies = [
         pltpu.make_async_copy(value, place, sems.at[index])
-        for index, (value, place) in enumerate(zip(values, held))
+        for index, (value, place) in enumerate(zip(values + vectors, held))
     ]
     for copy in copies:
         copy.start()
-    for index, value_ref in enumerate(held):
+    for index, value_ref in enumerate(held[:count]):
         copies[index].wait()
         halves = outs[2 * index : 2 * index + 2]
         rows, slab = value_ref.shape
@@ -42,25 +44,32 @@
                 out[q] = jnp.concatenate(
                     [jnp.where(low, phases[s], phases[s + 1]) for s in range(0, PHASES, 2)], axis=1
                 )
-
-
-def to_blocks(taps, *values):
+    for copy in copies[count:]:
+        copy.wait()
+    step, threshold = held[count][...], held[count + 1][...]
+    vector_outs[0][...] = jnp.concatenate([step] * PHASES, axis=1)
+    vector_outs[1][...] = jnp.concatenate([step * threshold] * PHASES, axis=1)
+
+
+def to_blocks(taps, values, vectors):
     run = taps // (PHASES * PARTS)
-    half = jax.ShapeDtypeStruct((run, PARTS, PHASES * LANES // 2), jnp.float32)
+    width = PHASES * LANES // 2
+    half = jax.ShapeDtypeStruct((run, PARTS, width), jnp.float32)
     slab = values[0].shape[1]
+    args = [*values, *(vector[None] for vector in vectors)]
     return pl.pallas_call(
         functools.partial(blocks_kernel, len(values)),
-        in_specs=[pl.BlockSpec(memory_space=pltpu.HBM)] * len(values),
-        out_specs=[pl.BlockSpec(memory_space=pltpu.VMEM)] * (2 * len(values)),
-        out_shape=[half] * (2 * len(values)),
-        scratch_shapes=[pltpu.VMEM(value.shape, value.dtype) for value in values]
+        in_specs=[pl.BlockSpec(memory_space=pltpu.HBM)] * len(args),
+        out_specs=[pl.BlockSpec(memory_space=pltpu.VMEM)] * (2 * len(values) + 2),
+        out_shape=[half] * (2 * len(values)) + [jax.ShapeDtypeStruct((1, width), jnp.float32)] * 2,
+        scratch_shapes=[pltpu.VMEM(value.shape, value.dtype) for value in args]
         + [
             pltpu.VMEM((slab + slab // (run * PHASES) + 7, LANES), jnp.float32),
-            pltpu.SemaphoreType.DMA((len(values),)),
+            pltpu.SemaphoreType.DMA((len(args),)),
         ],
         compiler_params=pltpu.CompilerParams(vmem_limit_bytes=VMEM),
         name="to_blocks",
-    )(*(pltpu.with_memory_space_constraint(value, pltpu.HBM) for value in values))
+    )(*(pltpu.with_memory_space_constraint(value, pltpu.HBM) for value in args))
 
 
 def series_kernel(low_ref, high_ref, out_ref, flat):
@@ -131,47 +140,60 @@
             for copy in piece:
                 copy.start()
 
-    def tap(index):
-        value = flat[pl.ds(index + margin, block, stride=rows), :]
-        return value, pltpu.roll(value, chans, 1)
-
-    for group in range(turns):
-        def turn(pair, carry):
-            first = group * block + 2 * pair
-            stacked = jnp.concatenate(
-                [bank[first], bank[half + first], bank[first + 1], bank[half + first + 1]], axis=0
+    def turn(group, pair):
+        first = group * block + 2 * pair
+        stacked = jnp.concatenate(
+            [bank[first], bank[half + first], bank[first + 1], bank[half + first + 1]], axis=0
+        )
+        place = flat.at[group % 2]
+        for which in range(2):
+            base = (2 * pair + which) * rows
+            place[pl.ds(base, margin), :] = zeros
+            place[pl.ds(base + margin + taps, margin), :] = zeros
+        for part in range(taps // step):
+            turned = lax.dot_general(
+                eye,
+                stacked[:, part * step : (part + 1) * step],
+                (((1,), (1,)), ((), ())),
+                preferred_element_type=jnp.float32,
             )
             for which in range(2):
-                base = (2 * pair + which) * rows
-                flat[pl.ds(base, margin), :] = zeros
-                flat[pl.ds(base + margin + taps, margin), :] = zeros
-            for part in range(taps // step):
-                turned = lax.dot_general(
-                    eye,
-                    stacked[:, part * step : (part + 1) * step],
-                    (((1,), (1,)), ((), ())),
-                    preferred_element_type=jnp.float32,
-                )
-                for which in range(2):
-                    base = (2 * pair + which) * rows + margin + part * step
-                    flat[pl.ds(base, step), :] = turned[:, which * LANES : (which + 1) * LANES]
-            return carry
-
-        for piece in range(pieces):
-            for copy in copies[group][piece]:
-                copy.wait()
-            for pair in range(piece * size // 2, (piece + 1) * size // 2):
-                turn(pair, 0)
+                base = (2 * pair + which) * rows + margin + part * step
+                place[pl.ds(base, step), :] = turned[:, which * LANES : (which + 1) * LANES]
+
+    pairs = block // 2
+    loops = next(n for n in (4, 2, 1) if tiles % n == 0 and pairs % n == 0)
+    unroll, beside = tiles // loops, pairs // loops
+
+    for piece in range(pieces):
+        for copy in copies[0][piece]:
+            copy.wait()
+        for pair in range(piece * size // 2, (piece + 1) * size // 2):
+            turn(0, pair)
+
+    for group in range(turns):
+        place = flat.at[group % 2]
+        start = group * block
+
+        def tap(index):
+            value = place[pl.ds(index + margin, block, stride=rows), :]
+            return value, pltpu.roll(value, chans, 1)
 
         def store(ref, tile, early, late):
-            start = group * block
             ref[tile, start : start + block] = jnp.where(low, early[0], late[1]).astype(jnp.bfloat16)
-            start += half
-            ref[tile, start : start + block] = jnp.where(low, early[1], late[0]).astype(jnp.bfloat16)
-
-        unroll = next(n for n in (65, 20, 13, 8, 5, 4, 2, 1) if tiles % n == 0)
+            ref[tile, half + start : half + start + block] = jnp.where(
+                low, early[1], late[0]
+            ).astype(jnp.bfloat16)
+
+        if group + 1 < turns:
+            for piece in copies[group + 1]:
+                for copy in piece:
+                    copy.wait()
 
         def merge(turn_index, carry):
+            if group + 1 < turns:
+                for inner in range(beside):
+                    turn(group + 1, turn_index * beside + inner)
             for inner in range(unroll):
                 tile = turn_index * unroll + inner
                 middle = tap(2 * tile - 3)
@@ -181,7 +203,7 @@
                 carry = later
             return carry
 
-        lax.fori_loop(0, tiles // unroll, merge, tap(-4))
+        lax.fori_loop(0, loops, merge, tap(-4))
 
 
 def bank_tiles(atom_bank):
@@ -199,7 +221,7 @@
         out_shape=[shape, shape],
         scratch_shapes=[
             pltpu.VMEM(atom_bank.shape, jnp.bfloat16),
-            pltpu.VMEM((block * rows, LANES), jnp.float32),
+            pltpu.VMEM((2, block * rows, LANES), jnp.float32),
             pltpu.SemaphoreType.DMA((turns, 4, 2)),
         ],
         compiler_params=pltpu.CompilerParams(vmem_limit_bytes=24 * 1024 * 1024),
@@ -328,10 +350,21 @@
     )(own, beside, even, odd)
 
 
-def shifted(value, axis, steps):
+def shifted(value, axis, steps, closed):
     count = lax.axis_size(axis)
-    first, last = max(0, -steps), min(count, count - steps)
-    return lax.ppermute(value, axis, [(i, i + steps) for i in range(first, last)])
+    if count == 1:
+        return jnp.zeros_like(value)
+    swaps = [(i, i ^ 1) for i in range(count)]
+    inner = [(i, i + 1) for i in range(1, count - 1, 2)]
+    inner += [(j, i) for i, j in inner]
+    if closed and count > 2:
+        inner += [(0, count - 1), (count - 1, 0)]
+    first = lax.ppermute(value, axis, swaps)
+    second = lax.ppermute(value, axis, inner) if inner else jnp.zeros_like(value)
+    place = lax.axis_index(axis)
+    source = place - steps
+    second = jnp.where((source >= 0) & (source < count), second, 0)
+    return jnp.where(source == (place ^ 1), first, second)
 
 
 def partner(value, axis, step):
@@ -355,29 +388,16 @@
     return value
 
 
-def summed_both(first, second, axis):
-    if lax.axis_size(axis) == 1:
-        return first, second
-    both = jnp.stack([first + partner(first, axis, 1), second + partner(second, axis, 1)])
-    step = 2
-    while step < lax.axis_size(axis):
-        both = both.astype(jnp.bfloat16)
-        other = partner(both, axis, step)
-        both = both.astype(jnp.float32) + other.astype(jnp.float32)
-        step *= 2
-    return both[0], both[1]
-
-
 def body(signal, codes_init, atom_bank, step_size, threshold):
     atoms, chans, taps = atom_bank.shape
     held = LANES // 2
     if chans < held:
         atom_bank = jnp.pad(atom_bank, ((0, 0), (0, held - chans), (0, 0)))
         signal = jnp.pad(signal, ((0, held - chans), (0, 0)))
-    low, high, heard_low, heard_high = to_blocks(taps, codes_init, signal)
+    low, high, heard_low, heard_high, step, bound = to_blocks(
+        taps, (codes_init, signal), (step_size, threshold)
+    )
     tiles = bank_tiles(atom_bank)
-    step = jnp.concatenate([step_size] * PHASES)
-    bound = jnp.concatenate([step_size * threshold] * PHASES)
 
     def shrink(current, gradient):
         moved = current - step * gradient
@@ -385,13 +405,13 @@
 
     turned = None
     low16, high16 = low.astype(jnp.bfloat16), high.astype(jnp.bfloat16)
-    earlier = shifted(high16, "tm", 1)
+    earlier = shifted(high16, "tm", 1, False)
     for sweep in range(ITERS):
         recon_low = convolve(low16, earlier, tiles, False)
         recon_high = convolve(after(high16, recon_low), low16, tiles, False)
         misfit_low = summed(recon_low, "atom") - heard_low
         rounded_low = misfit_low.astype(jnp.bfloat16)
-        following = shifted(rounded_low, "tm", -1)
+        following = shifted(rounded_low, "tm", -1, True)
         gate = None
         if turned is None:
             turned = turn_tiles(*(after(tile, rounded_low) for tile in tiles))
@@ -403,14 +423,14 @@
             gradient_low = convolve(after(rounded_low, gradient_high), rounded_high, turned, True)
             high = shrink(high, summed(gradient_high, "chan"))
             high16 = high.astype(jnp.bfloat16)
-            earlier = shifted(high16, "tm", 1)
+            earlier = shifted(high16, "tm", 1, False)
             low = shrink(low, summed(gradient_low, "chan", earlier))
             low16 = low.astype(jnp.bfloat16)
         else:
             gradient_low = convolve(rounded_low, rounded_high, turned, True)
             gradient_high = convolve(rounded_high, following, turned, True)
-            gradient_low, gradient_high = summed_both(gradient_low, gradient_high, "chan")
-            low, high = shrink(low, gradient_low), shrink(high, gradient_high)
+            low = shrink(low, summed(gradient_low, "chan"))
+            high = shrink(high, summed(gradient_high, "chan"))
     return from_blocks(low, high), from_blocks(misfit_low, misfit_high)[:chans]
 
 

time: 67.8 us -> 77.4 us (1.14)
  local copies, waits for them, and re-layouts: 0.01 us -> 8.45 us
  starting transfers between devices: 20.6 us -> 24.2 us
  waiting for transfers between devices: 12.8 us -> 10.8 us
  other arithmetic: 1.28 us -> 0.46 us
    unnamed x2 -> x16, local copies, waits for them, and re-layouts: 0.01 us -> 8.45 us
    ppermute x4 -> x8, starting transfers between devices: 11.4 us -> 13.5 us  [the longest x4 9.17 us: shifted(): first = lax.ppermute(value, axis, swaps)]
    ppermute x4 -> x8, waiting for transfers between devices: 4.06 us -> 2.5 us  [the longest x4 1.56 us: shifted(): lax.ppermute(value, axis, inner)]
    ppermute x11 -> x12, starting transfers between devices: 9.2 us -> 10.6 us  [partner(): lax.ppermute(value, axis, [(i, i ^ step) for i in range(lax.axis_size(axi...]
    ppermute x11 -> x12, waiting for transfers between devices: 8.69 us -> 8.35 us  [partner(): lax.ppermute(value, axis, [(i, i ^ step) for i in range(lax.axis_size(axi...]
  transfers between devices with their start and end apart: 15 -> 20, of which waited for: 8 -> 10; matrix products, arithmetic and copies ran while one was open for 2% -> 0% of each run, Pallas kernels for 33% -> 29%
where the time goes in v7:
time: 77.4 us; the launch traced here: 77.1 us
  Pallas kernels  32.3 us (42%)
  starting transfers between devices  24.2 us (31%)
  waiting for transfers between devices  10.8 us (14%)
  local copies, waits for them, and re-layouts  8.45 us (11%)
  between operations  0.94 us (1%)
    pallas_call x8, Pallas kernels, convolve(): pl.pallas_call(functools.partial(conv_kernel, transposed, steps), in_spec...  19.1 us
    ppermute x12, starting transfers between devices, partner(): lax.ppermute(value, axis, [(i, i ^ step) for i in range(lax.axis_size(axi...  10.6 us
    ppermute x4, starting transfers between devices, shifted(): first = lax.ppermute(value, axis, swaps)  9.17 us
    unnamed x16, local copies, waits for them, and re-layouts  8.45 us
    ppermute x12, waiting for transfers between devices, partner(): lax.ppermute(value, axis, [(i, i ^ step) for i in range(lax.axis_size(axi...  8.35 us
    pallas_call x1, Pallas kernels, bank_tiles(): pl.pallas_call(functools.partial(bank_kernel, rows), in_specs=[pl.BlockSp...  6.49 us
    ppermute x4, starting transfers between devices, shifted(): lax.ppermute(value, axis, inner)  4.34 us
    pallas_call x1, Pallas kernels, turn_tiles(): pl.pallas_call(turn_kernel, in_specs=[spec, spec], out_specs=[spec, spec]...  3.24 us
  transfers between devices with their start and end apart: 20, of which 10 were waited for; matrix products, arithmetic and copies ran while one was open for 0% of the time, Pallas kernels for 29%

profile of v7, /device:TPU:0, one launch (start us, length us, event | category | flops | bytes accessed | tf_op | source)
XLA Modules:
  0.0 77.1 jit_solution(13789167587396574250)
XLA Ops:
  0.6 1.4 %to_blocks.1 = (f32[8,16,256]{2,1,0:T(8,128)S(1)}, f32[8,16,256]{2,1,0:T(8,128)S(1)}, f32[8,16,256]{2,1,0:T(8,128)S(1)}, f32[8,16,256]{2,1,0:T(8,128)S(1)}, f32[1,256]{1,0:T(1,128)S(1)}, /*index=5*/f32[1,256]{1,0:T(1,128)S(1)}) custom-call(f32[64,1024]{1,0:T(8,128)} %refs_0_.1, bf16[64,1024]{1,0:T(8,128)(2,1)} %refs_1_.1, f32[1,64]{1,0:T(1,128)} %bitcast.18, ...), custom_call_target="tpu_custom_call" | custom-call | tf_op jit(solution)/shard_map/to_blocks/pallas_call | solution.py:60
  2.1 0.7 collective-permute-start.1
  2.8 5.9 %collective-permute-start = (bf16[8,16,256]{2,1,0:T(8,128)(2,1)S(1)}, bf16[8,16,256]{2,1,0:T(8,128)(2,1)S(1)}, u32[]{:S(2)}, u32[]{:S(2)}) collective-permute-start(bf16[8,16,256]{2,1,0:T(8,128)(2,1)S(1)} %convert_element_type.90.own_ref), channel_id=1, source_target_pairs={{0,8},{8,0},{16,24},{24,16},{1,9},{9,1},{17,25},{25,17},{2,10},{10... | collective-permute-start | bytes 196616 | tf_op jit(solution)/shard_map/ppermute | solution.py:362
  8.7 6.5 %bank_tiles.1 = (bf16[260,64,128]{2,1,0:T(8,128)(2,1)S(1)}, bf16[260,64,128]{2,1,0:T(8,128)(2,1)S(1)}) custom-call(bf16[64,64,512]{2,1,0:T(8,128)(2,1)} %bank_hbm.1), custom_call_target="tpu_custom_call" | custom-call | tf_op jit(solution)/shard_map/bank_tiles/pallas_call | solution.py:217
  15.2 2.0 %copy-done = bf16[260,64,128]{2,1,0:T(8,128)(2,1)} copy-done((bf16[260,64,128]{2,1,0:T(8,128)(2,1)}, bf16[260,64,128]{2,1,0:T(8,128)(2,1)S(1)}, u32[]{:S(2)}) %copy-start) | copy-done | bytes 4259864
  17.2 2.0 %copy-done.2 = bf16[260,64,128]{2,1,0:T(8,128)(2,1)} copy-done((bf16[260,64,128]{2,1,0:T(8,128)(2,1)}, bf16[260,64,128]{2,1,0:T(8,128)(2,1)S(1)}, u32[]{:S(2)}) %copy-start.2) | copy-done | bytes 4259864
  19.3 2.2 %copy-done.1 = bf16[260,64,128]{2,1,0:T(8,128)(2,1)S(1)} copy-done((bf16[260,64,128]{2,1,0:T(8,128)(2,1)S(1)}, bf16[260,64,128]{2,1,0:T(8,128)(2,1)}, u32[]{:S(2)}) %copy-start.1) | copy-done | bytes 4259864
  21.5 2.2 %copy-done.3 = bf16[260,64,128]{2,1,0:T(8,128)(2,1)S(1)} copy-done((bf16[260,64,128]{2,1,0:T(8,128)(2,1)S(1)}, bf16[260,64,128]{2,1,0:T(8,128)(2,1)}, u32[]{:S(2)}) %copy-start.3) | copy-done | bytes 4259864
  23.7 2.4 %synthesize.4 = bf16[8,16,256]{2,1,0:T(8,128)(2,1)S(1)} custom-call(bf16[8,16,256]{2,1,0:T(8,128)(2,1)S(1)} %convert_element_type.89.own_ref.beside_ref, bf16[8,16,256]{2,1,0:T(8,128)(2,1)S(1)} %select_select_fusion.3.beside_ref, bf16[260,64,128]{2,1,0:T(8,128)(2,1)S(1)} %copy-done.1, bf16[260,64,128]{2,1,0:T(8,128)(2,1)S(1)} %copy-done.3), custom_call_target="tpu_custom_call" | custom-call | flops 2164260864 | bytes 8781824 | tf_op jit(solution)/shard_map/synthesize/pallas_call | solution.py:333
  26.1 1.6 %collective-permute-start.2 = (bf16[8,16,256]{2,1,0:T(8,128)(2,1)S(1)}, bf16[8,16,256]{2,1,0:T(8,128)(2,1)S(1)}, u32[]{:S(2)}, u32[]{:S(2)}) collective-permute-start(bf16[8,16,256]{2,1,0:T(8,128)(2,1)S(1)} %synthesize.4), channel_id=1, source_target_pairs={{0,4},{4,0},{1,5},{5,1},{2,6},{6,2},{3,7},{7,3},{8,12},{12,8},{9,1... | collective-permute-start | bytes 196616 | tf_op jit(solution)/shard_map/ppermute | solution.py:371
  27.6 2.4 %synthesize.5 = bf16[8,16,256]{2,1,0:T(8,128)(2,1)S(1)} custom-call(bf16[8,16,256]{2,1,0:T(8,128)(2,1)S(1)} %convert_element_type.90.own_ref, bf16[8,16,256]{2,1,0:T(8,128)(2,1)S(1)} %convert_element_type.89.own_ref.beside_ref, bf16[260,64,128]{2,1,0:T(8,128)(2,1)S(1)} %copy-done.1, bf16[260,64,128]{2,1,0:T(8,128)(2,1)S(1)} %copy-done.3), custom_call_target="tpu_custom_call" | custom-call | flops 2164260864 | bytes 8781824 | tf_op jit(solution)/shard_map/synthesize/pallas_call | solution.py:333
  30.0 0.6 collective-permute-start.3
  30.6 1.4 %collective-permute-start.5 = (bf16[8,16,256]{2,1,0:T(8,128)(2,1)S(1)}, bf16[8,16,256]{2,1,0:T(8,128)(2,1)S(1)}, u32[]{:S(2)}, u32[]{:S(2)}) collective-permute-start(bf16[8,16,256]{2,1,0:T(8,128)(2,1)S(1)} %subtract_convert_fusion.1.own_ref), channel_id=1, source_target_pairs={{8,16},{16,8},{0,24},{24,0},{9,17},{17,9},{1,25},{25,1},{10,18},{1... | collective-permute-start | bytes 196616 | tf_op jit(solution)/shard_map/ppermute | solution.py:363
  32.1 3.2 %turn_tiles.1 = (bf16[260,64,128]{2,1,0:T(8,128)(2,1)S(1)}, bf16[260,64,128]{2,1,0:T(8,128)(2,1)S(1)}) custom-call(bf16[260,64,128]{2,1,0:T(8,128)(2,1)S(1)} %copy-done.1, bf16[260,64,128]{2,1,0:T(8,128)(2,1)S(1)} %copy-done.3), custom_call_target="tpu_custom_call" | custom-call | flops 2181038080 | bytes 17039360 | tf_op jit(solution)/shard_map/turn_tiles/pallas_call | solution.py:269
  35.3 0.0 collective-permute-done.3
  35.3 1.5 %collective-permute-done.5 = bf16[8,16,256]{2,1,0:T(8,128)(2,1)S(1)} collective-permute-done((bf16[8,16,256]{2,1,0:T(8,128)(2,1)S(1)}, bf16[8,16,256]{2,1,0:T(8,128)(2,1)S(1)}, u32[]{:S(2)}, u32[]{:S(2)}) %collective-permute-start.5) | collective-permute-done | bytes 65568 | tf_op jit(solution)/shard_map/ppermute | solution.py:363
  36.9 0.1 collective-permute-done.4
  37.0 2.4 %correlate.4 = f32[8,16,256]{2,1,0:T(8,128)S(1)} custom-call(bf16[8,16,256]{2,1,0:T(8,128)(2,1)S(1)} %subtract_convert_fusion.own_ref.beside_ref, bf16[8,16,256]{2,1,0:T(8,128)(2,1)S(1)} %select_select_fusion.2.beside_ref, bf16[260,64,128]{2,1,0:T(8,128)(2,1)S(1)} %get-tuple-element.28.even, bf16[260,64,128]{2,1,0:T(8,128)(2,1)S(1)} %get-tuple-element.31.odd), custom_call_target="tpu_custom_call" | custom-call | flops 2164260864 | bytes 8781824 | tf_op jit(solution)/shard_map/correlate/pallas_call | solution.py:333
  39.4 0.1 collective-permute-start.8
  39.5 1.3 %collective-permute-done.8 = f32[8,16,256]{2,1,0:T(8,128)S(1)} collective-permute-done((f32[8,16,256]{2,1,0:T(8,128)S(1)}, f32[8,16,256]{2,1,0:T(8,128)S(1)}, u32[]{:S(2)}, u32[]{:S(2)}) %collective-permute-start.8) | collective-permute-done | bytes 131104 | tf_op jit(solution)/shard_map/ppermute | solution.py:371
  40.9 1.6 %collective-permute-start.9 = (bf16[8,16,256]{2,1,0:T(8,128)(2,1)S(1)}, bf16[8,16,256]{2,1,0:T(8,128)(2,1)S(1)}, u32[]{:S(2)}, u32[]{:S(2)}) collective-permute-start(bf16[8,16,256]{2,1,0:T(8,128)(2,1)S(1)} %add_convert_fusion.2), channel_id=1, source_target_pairs={{0,2},{1,3},{2,0},{3,1},{4,6},{5,7},{6,4},{7,5},{8,10},{9,11},{10,... | collective-permute-start | bytes 196616 | tf_op jit(solution)/shard_map/ppermute | solution.py:371
  42.5 2.4 %correlate.5 = f32[8,16,256]{2,1,0:T(8,128)S(1)} custom-call(bf16[8,16,256]{2,1,0:T(8,128)(2,1)S(1)} %subtract_convert_fusion.1.own_ref, bf16[8,16,256]{2,1,0:T(8,128)(2,1)S(1)} %subtract_convert_fusion.own_ref.beside_ref, bf16[260,64,128]{2,1,0:T(8,128)(2,1)S(1)} %get-tuple-element.28.even, bf16[260,64,128]{2,1,0:T(8,128)(2,1)S(1)} %get-tuple-element.31.odd), custom_call_target="tpu_custom_call" | custom-call | flops 2164260864 | bytes 8781824 | tf_op jit(solution)/shard_map/correlate/pallas_call | solution.py:333
  44.9 0.1 collective-permute-start.6
  45.0 0.3 collective-permute-done.9
  45.3 0.8 %collective-permute-start.11 = (bf16[8,16,256]{2,1,0:T(8,128)(2,1)S(1)}, bf16[8,16,256]{2,1,0:T(8,128)(2,1)S(1)}, u32[]{:S(2)}, u32[]{:S(2)}) collective-permute-start(bf16[8,16,256]{2,1,0:T(8,128)(2,1)S(1)} %fusion.own_ref), channel_id=1, source_target_pairs={{8,16},{16,8},{9,17},{17,9},{10,18},{18,10},{11,19},{19,11},{12,20... | collective-permute-start | bytes 196616 | tf_op jit(solution)/shard_map/ppermute | solution.py:363
  46.1 3.3 %collective-permute-start.10 = (bf16[8,16,256]{2,1,0:T(8,128)(2,1)S(1)}, bf16[8,16,256]{2,1,0:T(8,128)(2,1)S(1)}, u32[]{:S(2)}, u32[]{:S(2)}) collective-permute-start(bf16[8,16,256]{2,1,0:T(8,128)(2,1)S(1)} %fusion.own_ref), channel_id=1, source_target_pairs={{0,8},{8,0},{16,24},{24,16},{1,9},{9,1},{17,25},{25,17},{2,10},{10... | collective-permute-start | bytes 196616 | tf_op jit(solution)/shard_map/ppermute | solution.py:362
  49.4 1.6 %collective-permute-start.7 = (bf16[8,16,256]{2,1,0:T(8,128)(2,1)S(1)}, bf16[8,16,256]{2,1,0:T(8,128)(2,1)S(1)}, u32[]{:S(2)}, u32[]{:S(2)}) collective-permute-start(bf16[8,16,256]{2,1,0:T(8,128)(2,1)S(1)} %add_convert_fusion.3), channel_id=1, source_target_pairs={{0,2},{1,3},{2,0},{3,1},{4,6},{5,7},{6,4},{7,5},{8,10},{9,11},{10,... | collective-permute-start | bytes 196616 | tf_op jit(solution)/shard_map/ppermute | solution.py:371
  51.0 0.6 collective-permute-done.10
  51.6 2.1 %collective-permute-done.7 = bf16[8,16,256]{2,1,0:T(8,128)(2,1)S(1)} collective-permute-done((bf16[8,16,256]{2,1,0:T(8,128)(2,1)S(1)}, bf16[8,16,256]{2,1,0:T(8,128)(2,1)S(1)}, u32[]{:S(2)}, u32[]{:S(2)}) %collective-permute-start.7) | collective-permute-done | bytes 65568 | tf_op jit(solution)/shard_map/ppermute | solution.py:371
  53.8 2.4 %synthesize.6 = bf16[8,16,256]{2,1,0:T(8,128)(2,1)S(1)} custom-call(bf16[8,16,256]{2,1,0:T(8,128)(2,1)S(1)} %fusion.1.own_ref.beside_ref, bf16[8,16,256]{2,1,0:T(8,128)(2,1)S(1)} %select_select_fusion.1.beside_ref, bf16[260,64,128]{2,1,0:T(8,128)(2,1)S(1)} %bitcast.6, bf16[260,64,128]{2,1,0:T(8,128)(2,1)S(1)} %bitcast.8), custom_call_target="tpu_custom_call" | custom-call | flops 2164260864 | bytes 8781824 | tf_op jit(solution)/shard_map/synthesize/pallas_call | solution.py:333
  56.2 1.6 %collective-permute-start.12 = (bf16[8,16,256]{2,1,0:T(8,128)(2,1)S(1)}, bf16[8,16,256]{2,1,0:T(8,128)(2,1)S(1)}, u32[]{:S(2)}, u32[]{:S(2)}) collective-permute-start(bf16[8,16,256]{2,1,0:T(8,128)(2,1)S(1)} %synthesize.6), channel_id=1, source_target_pairs={{0,4},{4,0},{1,5},{5,1},{2,6},{6,2},{3,7},{7,3},{8,12},{12,8},{9,1... | collective-permute-start | bytes 196616 | tf_op jit(solution)/shard_map/ppermute | solution.py:371
  57.8 2.4 %synthesize.7 = bf16[8,16,256]{2,1,0:T(8,128)(2,1)S(1)} custom-call(bf16[8,16,256]{2,1,0:T(8,128)(2,1)S(1)} %fusion.own_ref, bf16[8,16,256]{2,1,0:T(8,128)(2,1)S(1)} %fusion.1.own_ref.beside_ref, bf16[260,64,128]{2,1,0:T(8,128)(2,1)S(1)} %bitcast.6, bf16[260,64,128]{2,1,0:T(8,128)(2,1)S(1)} %bitcast.8), custom_call_target="tpu_custom_call" | custom-call | flops 2164260864 | bytes 8781824 | tf_op jit(solution)/shard_map/synthesize/pallas_call | solution.py:333
  60.2 0.6 collective-permute-start.13
  60.8 1.4 %collective-permute-start.17 = (bf16[8,16,256]{2,1,0:T(8,128)(2,1)S(1)}, bf16[8,16,256]{2,1,0:T(8,128)(2,1)S(1)}, u32[]{:S(2)}, u32[]{:S(2)}) collective-permute-start(bf16[8,16,256]{2,1,0:T(8,128)(2,1)S(1)} %get-tuple-element.38.own_ref), channel_id=1, source_target_pairs={{8,16},{16,8},{0,24},{24,0},{9,17},{17,9},{1,25},{25,1},{10,18},{1... | collective-permute-start | bytes 196616 | tf_op jit(solution)/shard_map/ppermute | solution.py:363
  62.2 2.3 %collective-permute-done.13 = bf16[8,16,256]{2,1,0:T(8,128)(2,1)S(1)} collective-permute-done((bf16[8,16,256]{2,1,0:T(8,128)(2,1)S(1)}, bf16[8,16,256]{2,1,0:T(8,128)(2,1)S(1)}, u32[]{:S(2)}, u32[]{:S(2)}) %collective-permute-start.13) | collective-permute-done | bytes 65568 | tf_op jit(solution)/shard_map/ppermute | solution.py:371
  64.6 2.4 %correlate.6 = f32[8,16,256]{2,1,0:T(8,128)S(1)} custom-call(bf16[8,16,256]{2,1,0:T(8,128)(2,1)S(1)} %get-tuple-element.38.own_ref, bf16[8,16,256]{2,1,0:T(8,128)(2,1)S(1)} %get-tuple-element.36.beside_ref.own_ref, bf16[260,64,128]{2,1,0:T(8,128)(2,1)S(1)} %get-tuple-element.28.even, bf16[260,64,128]{2,1,0:T(8,128)(2,1)S(1)} %get-tuple-element.31.odd), custom_call_target="tpu_custom_call" | custom-call | flops 2164260864 | bytes 8781824 | tf_op jit(solution)/shard_map/correlate/pallas_call | solution.py:333
  67.0 0.1 collective-permute-start.14
  67.0 0.0 collective-permute-done.17
  67.1 0.1 collective-permute-done.16
  67.2 2.4 %correlate.7 = f32[8,16,256]{2,1,0:T(8,128)S(1)} custom-call(bf16[8,16,256]{2,1,0:T(8,128)(2,1)S(1)} %get-tuple-element.36.beside_ref.own_ref, bf16[8,16,256]{2,1,0:T(8,128)(2,1)S(1)} %select_select_fusion.beside_ref, bf16[260,64,128]{2,1,0:T(8,128)(2,1)S(1)} %get-tuple-element.28.even, bf16[260,64,128]{2,1,0:T(8,128)(2,1)S(1)} %get-tuple-element.31.odd), custom_call_target="tpu_custom_call" | custom-call | flops 2164260864 | bytes 8781824 | tf_op jit(solution)/shard_map/correlate/pallas_call | solution.py:333
  69.6 0.4 collective-permute-start.18
  70.0 1.6 %collective-permute-start.15 = (bf16[8,16,256]{2,1,0:T(8,128)(2,1)S(1)}, bf16[8,16,256]{2,1,0:T(8,128)(2,1)S(1)}, u32[]{:S(2)}, u32[]{:S(2)}) collective-permute-start(bf16[8,16,256]{2,1,0:T(8,128)(2,1)S(1)} %add_convert_fusion.1), channel_id=1, source_target_pairs={{0,2},{1,3},{2,0},{3,1},{4,6},{5,7},{6,4},{7,5},{8,10},{9,11},{10,... | collective-permute-start | bytes 196616 | tf_op jit(solution)/shard_map/ppermute | solution.py:371
  71.6 1.0 %collective-permute-start.19 = (bf16[8,16,256]{2,1,0:T(8,128)(2,1)S(1)}, bf16[8,16,256]{2,1,0:T(8,128)(2,1)S(1)}, u32[]{:S(2)}, u32[]{:S(2)}) collective-permute-start(bf16[8,16,256]{2,1,0:T(8,128)(2,1)S(1)} %add_convert_fusion), channel_id=1, source_target_pairs={{0,2},{1,3},{2,0},{3,1},{4,6},{5,7},{6,4},{7,5},{8,10},{9,11},{10,... | collective-permute-start | bytes 196616 | tf_op jit(solution)/shard_map/ppermute | solution.py:371
  72.6 1.0 %from_blocks.3 = f32[64,1024]{1,0:T(8,128)} custom-call(f32[8,16,256]{2,1,0:T(8,128)S(1)} %get-tuple-element.39.low_ref, f32[8,16,256]{2,1,0:T(8,128)S(1)} %get-tuple-element.37.high_ref), custom_call_target="tpu_custom_call" | custom-call | tf_op jit(solution)/shard_map/from_blocks/pallas_call | solution.py:96
  73.6 1.0 %collective-permute-done.15 = bf16[8,16,256]{2,1,0:T(8,128)(2,1)S(1)} collective-permute-done((bf16[8,16,256]{2,1,0:T(8,128)(2,1)S(1)}, bf16[8,16,256]{2,1,0:T(8,128)(2,1)S(1)}, u32[]{:S(2)}, u32[]{:S(2)}) %collective-permute-start.15) | collective-permute-done | bytes 65568 | tf_op jit(solution)/shard_map/ppermute | solution.py:371
  74.6 1.4 %collective-permute-done.19 = bf16[8,16,256]{2,1,0:T(8,128)(2,1)S(1)} collective-permute-done((bf16[8,16,256]{2,1,0:T(8,128)(2,1)S(1)}, bf16[8,16,256]{2,1,0:T(8,128)(2,1)S(1)}, u32[]{:S(2)}, u32[]{:S(2)}) %collective-permute-start.19) | collective-permute-done | bytes 65568 | tf_op jit(solution)/shard_map/ppermute | solution.py:371
  76.0 0.1 minimum_subtract_fusion
  76.1 1.0 %from_blocks.2 = f32[64,1024]{1,0:T(8,128)} custom-call(f32[8,16,256]{2,1,0:T(8,128)S(1)} %get-tuple-element.41.low_ref, f32[8,16,256]{2,1,0:T(8,128)S(1)} %get-tuple-element.40.high_ref), custom_call_target="tpu_custom_call" | custom-call | tf_op jit(solution)/shard_map/from_blocks/pallas_call | solution.py:96
  (41 shorter events, 0.4 us)
Async XLA Ops:
  2.1 17.1 %collective-permute-start.1 = (bf16[8,16,256]{2,1,0:T(8,128)(2,1)S(1)}, bf16[8,16,256]{2,1,0:T(8,128)(2,1)S(1)}, u32[]{:S(2)}, u32[]{:S(2)}) collective-permute-start(bf16[8,16,256]{2,1,0:T(8,128)(2,1)S(1)} %convert_element_type.90.own_ref), channel_id=1, source_target_pairs={{8,16},{16,8},{9,17},{17,9},{10,18},{18,10},{11,19},{19,11},{12,20... | collective-permute-start | bytes 196616 | tf_op jit(solution)/shard_map/ppermute | solution.py:363
  2.8 16.5 %collective-permute-start = (bf16[8,16,256]{2,1,0:T(8,128)(2,1)S(1)}, bf16[8,16,256]{2,1,0:T(8,128)(2,1)S(1)}, u32[]{:S(2)}, u32[]{:S(2)}) collective-permute-start(bf16[8,16,256]{2,1,0:T(8,128)(2,1)S(1)} %convert_element_type.90.own_ref), channel_id=1, source_target_pairs={{0,8},{8,0},{16,24},{24,16},{1,9},{9,1},{17,25},{25,17},{2,10},{10... | collective-permute-start | bytes 196616 | tf_op jit(solution)/shard_map/ppermute | solution.py:362
  15.2 2.0 %copy-start = (bf16[260,64,128]{2,1,0:T(8,128)(2,1)}, bf16[260,64,128]{2,1,0:T(8,128)(2,1)S(1)}, u32[]{:S(2)}) copy-start(bf16[260,64,128]{2,1,0:T(8,128)(2,1)S(1)} %get-tuple-element.26.even.even_ref) | copy-start | bytes 12779524
  17.2 2.0 %copy-start.2 = (bf16[260,64,128]{2,1,0:T(8,128)(2,1)}, bf16[260,64,128]{2,1,0:T(8,128)(2,1)S(1)}, u32[]{:S(2)}) copy-start(bf16[260,64,128]{2,1,0:T(8,128)(2,1)S(1)} %get-tuple-element.27.odd.odd_ref) | copy-start | bytes 12779524
  19.3 2.2 %copy-start.1 = (bf16[260,64,128]{2,1,0:T(8,128)(2,1)S(1)}, bf16[260,64,128]{2,1,0:T(8,128)(2,1)}, u32[]{:S(2)}) copy-start(bf16[260,64,128]{2,1,0:T(8,128)(2,1)} %copy-done) | copy-start | bytes 12779524
  21.5 2.2 %copy-start.3 = (bf16[260,64,128]{2,1,0:T(8,128)(2,1)S(1)}, bf16[260,64,128]{2,1,0:T(8,128)(2,1)}, u32[]{:S(2)}) copy-start(bf16[260,64,128]{2,1,0:T(8,128)(2,1)} %copy-done.2) | copy-start | bytes 12779524
  26.1 4.6 %collective-permute-start.2 = (bf16[8,16,256]{2,1,0:T(8,128)(2,1)S(1)}, bf16[8,16,256]{2,1,0:T(8,128)(2,1)S(1)}, u32[]{:S(2)}, u32[]{:S(2)}) collective-permute-start(bf16[8,16,256]{2,1,0:T(8,128)(2,1)S(1)} %synthesize.4), channel_id=1, source_target_pairs={{0,4},{4,0},{1,5},{5,1},{2,6},{6,2},{3,7},{7,3},{8,12},{12,8},{9,1... | collective-permute-start | bytes 196616 | tf_op jit(solution)/shard_map/ppermute | solution.py:371
  30.0 5.3 %collective-permute-start.3 = (bf16[8,16,256]{2,1,0:T(8,128)(2,1)S(1)}, bf16[8,16,256]{2,1,0:T(8,128)(2,1)S(1)}, u32[]{:S(2)}, u32[]{:S(2)}) collective-permute-start(bf16[8,16,256]{2,1,0:T(8,128)(2,1)S(1)} %synthesize.5), channel_id=1, source_target_pairs={{0,4},{4,0},{1,5},{5,1},{2,6},{6,2},{3,7},{7,3},{8,12},{12,8},{9,1... | collective-permute-start | bytes 196616 | tf_op jit(solution)/shard_map/ppermute | solution.py:371
  30.6 6.2 %collective-permute-start.5 = (bf16[8,16,256]{2,1,0:T(8,128)(2,1)S(1)}, bf16[8,16,256]{2,1,0:T(8,128)(2,1)S(1)}, u32[]{:S(2)}, u32[]{:S(2)}) collective-permute-start(bf16[8,16,256]{2,1,0:T(8,128)(2,1)S(1)} %subtract_convert_fusion.1.own_ref), channel_id=1, source_target_pairs={{8,16},{16,8},{0,24},{24,0},{9,17},{17,9},{1,25},{25,1},{10,18},{1... | collective-permute-start | bytes 196616 | tf_op jit(solution)/shard_map/ppermute | solution.py:363
  32.1 5.0 %collective-permute-start.4 = (bf16[8,16,256]{2,1,0:T(8,128)(2,1)S(1)}, bf16[8,16,256]{2,1,0:T(8,128)(2,1)S(1)}, u32[]{:S(2)}, u32[]{:S(2)}) collective-permute-start(bf16[8,16,256]{2,1,0:T(8,128)(2,1)S(1)} %subtract_convert_fusion.1.own_ref), channel_id=1, source_target_pairs={{0,8},{8,0},{16,24},{24,16},{1,9},{9,1},{17,25},{25,17},{2,10},{10... | collective-permute-start | bytes 196616 | tf_op jit(solution)/shard_map/ppermute | solution.py:362
  32.1 21.7 %slice-start.2 = ((s8[4259840]{0:T(1024)(128)(4,1)}), s8[65536]{0:T(1024)(128)(4,1)S(1)}, s32[]{:S(2)}) async-start(s8[4259840]{0:T(1024)(128)(4,1)} %bitcast.7), calls=%async_computation.2 | async-start | bytes 131072
  37.0 16.8 %slice-start.3 = ((s8[4259840]{0:T(1024)(128)(4,1)}), s8[4194304]{0:T(1024)(128)(4,1)S(1)}, s32[]{:S(2)}) async-start(s8[4259840]{0:T(1024)(128)(4,1)} %bitcast.7), calls=%async_computation.3 | async-start | bytes 8388608
  39.4 1.4 %collective-permute-start.8 = (f32[8,16,256]{2,1,0:T(8,128)S(1)}, f32[8,16,256]{2,1,0:T(8,128)S(1)}, u32[]{:S(2)}, u32[]{:S(2)}) collective-permute-start(f32[8,16,256]{2,1,0:T(8,128)S(1)} %correlate.4), channel_id=1, source_target_pairs={{0,1},{1,0},{2,3},{3,2},{4,5},{5,4},{6,7},{7,6},{8,9},{9,8},{10,11... | collective-permute-start | bytes 393224 | tf_op jit(solution)/shard_map/ppermute | solution.py:371
  40.9 12.9 %slice-start = ((s8[4259840]{0:T(1024)(128)(4,1)}), s8[4194304]{0:T(1024)(128)(4,1)S(1)}, s32[]{:S(2)}) async-start(s8[4259840]{0:T(1024)(128)(4,1)} %bitcast.5), calls=%async_computation | async-start | bytes 8388608
  40.9 12.9 %slice-start.1 = ((s8[4259840]{0:T(1024)(128)(4,1)}), s8[65536]{0:T(1024)(128)(4,1)S(1)}, s32[]{:S(2)}) async-start(s8[4259840]{0:T(1024)(128)(4,1)} %bitcast.5), calls=%async_computation.1 | async-start | bytes 131072
  40.9 4.3 %collective-permute-start.9 = (bf16[8,16,256]{2,1,0:T(8,128)(2,1)S(1)}, bf16[8,16,256]{2,1,0:T(8,128)(2,1)S(1)}, u32[]{:S(2)}, u32[]{:S(2)}) collective-permute-start(bf16[8,16,256]{2,1,0:T(8,128)(2,1)S(1)} %add_convert_fusion.2), channel_id=1, source_target_pairs={{0,2},{1,3},{2,0},{3,1},{4,6},{5,7},{6,4},{7,5},{8,10},{9,11},{10,... | collective-permute-start | bytes 196616 | tf_op jit(solution)/shard_map/ppermute | solution.py:371
  44.9 4.5 %collective-permute-start.6 = (f32[8,16,256]{2,1,0:T(8,128)S(1)}, f32[8,16,256]{2,1,0:T(8,128)S(1)}, u32[]{:S(2)}, u32[]{:S(2)}) collective-permute-start(f32[8,16,256]{2,1,0:T(8,128)S(1)} %correlate.5), channel_id=1, source_target_pairs={{0,1},{1,0},{2,3},{3,2},{4,5},{5,4},{6,7},{7,6},{8,9},{9,8},{10,11... | collective-permute-start | bytes 393224 | tf_op jit(solution)/shard_map/ppermute | solution.py:371
  45.3 5.7 %collective-permute-start.11 = (bf16[8,16,256]{2,1,0:T(8,128)(2,1)S(1)}, bf16[8,16,256]{2,1,0:T(8,128)(2,1)S(1)}, u32[]{:S(2)}, u32[]{:S(2)}) collective-permute-start(bf16[8,16,256]{2,1,0:T(8,128)(2,1)S(1)} %fusion.own_ref), channel_id=1, source_target_pairs={{8,16},{16,8},{9,17},{17,9},{10,18},{18,10},{11,19},{19,11},{12,20... | collective-permute-start | bytes 196616 | tf_op jit(solution)/shard_map/ppermute | solution.py:363
  46.1 5.5 %collective-permute-start.10 = (bf16[8,16,256]{2,1,0:T(8,128)(2,1)S(1)}, bf16[8,16,256]{2,1,0:T(8,128)(2,1)S(1)}, u32[]{:S(2)}, u32[]{:S(2)}) collective-permute-start(bf16[8,16,256]{2,1,0:T(8,128)(2,1)S(1)} %fusion.own_ref), channel_id=1, source_target_pairs={{0,8},{8,0},{16,24},{24,16},{1,9},{9,1},{17,25},{25,17},{2,10},{10... | collective-permute-start | bytes 196616 | tf_op jit(solution)/shard_map/ppermute | solution.py:362
  49.4 4.3 %collective-permute-start.7 = (bf16[8,16,256]{2,1,0:T(8,128)(2,1)S(1)}, bf16[8,16,256]{2,1,0:T(8,128)(2,1)S(1)}, u32[]{:S(2)}, u32[]{:S(2)}) collective-permute-start(bf16[8,16,256]{2,1,0:T(8,128)(2,1)S(1)} %add_convert_fusion.3), channel_id=1, source_target_pairs={{0,2},{1,3},{2,0},{3,1},{4,6},{5,7},{6,4},{7,5},{8,10},{9,11},{10,... | collective-permute-start | bytes 196616 | tf_op jit(solution)/shard_map/ppermute | solution.py:371
  56.2 4.6 %collective-permute-start.12 = (bf16[8,16,256]{2,1,0:T(8,128)(2,1)S(1)}, bf16[8,16,256]{2,1,0:T(8,128)(2,1)S(1)}, u32[]{:S(2)}, u32[]{:S(2)}) collective-permute-start(bf16[8,16,256]{2,1,0:T(8,128)(2,1)S(1)} %synthesize.6), channel_id=1, source_target_pairs={{0,4},{4,0},{1,5},{5,1},{2,6},{6,2},{3,7},{7,3},{8,12},{12,8},{9,1... | collective-permute-start | bytes 196616 | tf_op jit(solution)/shard_map/ppermute | solution.py:371
  60.2 4.3 %collective-permute-start.13 = (bf16[8,16,256]{2,1,0:T(8,128)(2,1)S(1)}, bf16[8,16,256]{2,1,0:T(8,128)(2,1)S(1)}, u32[]{:S(2)}, u32[]{:S(2)}) collective-permute-start(bf16[8,16,256]{2,1,0:T(8,128)(2,1)S(1)} %synthesize.7), channel_id=1, source_target_pairs={{0,4},{4,0},{1,5},{5,1},{2,6},{6,2},{3,7},{7,3},{8,12},{12,8},{9,1... | collective-permute-start | bytes 196616 | tf_op jit(solution)/shard_map/ppermute | solution.py:371
  60.8 6.2 %collective-permute-start.17 = (bf16[8,16,256]{2,1,0:T(8,128)(2,1)S(1)}, bf16[8,16,256]{2,1,0:T(8,128)(2,1)S(1)}, u32[]{:S(2)}, u32[]{:S(2)}) collective-permute-start(bf16[8,16,256]{2,1,0:T(8,128)(2,1)S(1)} %get-tuple-element.38.own_ref), channel_id=1, source_target_pairs={{8,16},{16,8},{0,24},{24,0},{9,17},{17,9},{1,25},{25,1},{10,18},{1... | collective-permute-start | bytes 196616 | tf_op jit(solution)/shard_map/ppermute | solution.py:363
  62.2 5.0 %collective-permute-start.16 = (bf16[8,16,256]{2,1,0:T(8,128)(2,1)S(1)}, bf16[8,16,256]{2,1,0:T(8,128)(2,1)S(1)}, u32[]{:S(2)}, u32[]{:S(2)}) collective-permute-start(bf16[8,16,256]{2,1,0:T(8,128)(2,1)S(1)} %get-tuple-element.38.own_ref), channel_id=1, source_target_pairs={{0,8},{8,0},{16,24},{24,16},{1,9},{9,1},{17,25},{25,17},{2,10},{10... | collective-permute-start | bytes 196616 | tf_op jit(solution)/shard_map/ppermute | solution.py:362
  67.0 3.1 %collective-permute-start.14 = (f32[8,16,256]{2,1,0:T(8,128)S(1)}, f32[8,16,256]{2,1,0:T(8,128)S(1)}, u32[]{:S(2)}, u32[]{:S(2)}) collective-permute-start(f32[8,16,256]{2,1,0:T(8,128)S(1)} %correlate.6), channel_id=1, source_target_pairs={{0,1},{1,0},{2,3},{3,2},{4,5},{5,4},{6,7},{7,6},{8,9},{9,8},{10,11... | collective-permute-start | bytes 393224 | tf_op jit(solution)/shard_map/ppermute | solution.py:371
  69.6 2.0 %collective-permute-start.18 = (f32[8,16,256]{2,1,0:T(8,128)S(1)}, f32[8,16,256]{2,1,0:T(8,128)S(1)}, u32[]{:S(2)}, u32[]{:S(2)}) collective-permute-start(f32[8,16,256]{2,1,0:T(8,128)S(1)} %correlate.7), channel_id=1, source_target_pairs={{0,1},{1,0},{2,3},{3,2},{4,5},{5,4},{6,7},{7,6},{8,9},{9,8},{10,11... | collective-permute-start | bytes 393224 | tf_op jit(solution)/shard_map/ppermute | solution.py:371
  70.0 4.6 %collective-permute-start.15 = (bf16[8,16,256]{2,1,0:T(8,128)(2,1)S(1)}, bf16[8,16,256]{2,1,0:T(8,128)(2,1)S(1)}, u32[]{:S(2)}, u32[]{:S(2)}) collective-permute-start(bf16[8,16,256]{2,1,0:T(8,128)(2,1)S(1)} %add_convert_fusion.1), channel_id=1, source_target_pairs={{0,2},{1,3},{2,0},{3,1},{4,6},{5,7},{6,4},{7,5},{8,10},{9,11},{10,... | collective-permute-start | bytes 196616 | tf_op jit(solution)/shard_map/ppermute | solution.py:371
  71.6 4.3 %collective-permute-start.19 = (bf16[8,16,256]{2,1,0:T(8,128)(2,1)S(1)}, bf16[8,16,256]{2,1,0:T(8,128)(2,1)S(1)}, u32[]{:S(2)}, u32[]{:S(2)}) collective-permute-start(bf16[8,16,256]{2,1,0:T(8,128)(2,1)S(1)} %add_convert_fusion), channel_id=1, source_target_pairs={{0,2},{1,3},{2,0},{3,1},{4,6},{5,7},{6,4},{7,5},{8,10},{9,11},{10,... | collective-permute-start | bytes 196616 | tf_op jit(solution)/shard_map/ppermute | solution.py:371

commit v8 on v7

--- a/solution.py
+++ b/solution.py
@@ -162,9 +162,6 @@
                 place[pl.ds(base, step), :] = turned[:, which * LANES : (which + 1) * LANES]
 
     pairs = block // 2
-    loops = next(n for n in (4, 2, 1) if tiles % n == 0 and pairs % n == 0)
-    unroll, beside = tiles // loops, pairs // loops
-
     for piece in range(pieces):
         for copy in copies[0][piece]:
             copy.wait()
@@ -190,20 +187,15 @@
                 for copy in piece:
                     copy.wait()
 
-        def merge(turn_index, carry):
-            if group + 1 < turns:
-                for inner in range(beside):
-                    turn(group + 1, turn_index * beside + inner)
-            for inner in range(unroll):
-                tile = turn_index * unroll + inner
-                middle = tap(2 * tile - 3)
-                later = tap(2 * tile - 2)
-                store(even_ref, tile, carry, middle)
-                store(odd_ref, tile, middle, later)
-                carry = later
-            return carry
-
-        lax.fori_loop(0, loops, merge, tap(-4))
+        early = tap(-4)
+        for tile in range(tiles):
+            if group + 1 < turns and tile % (tiles // pairs) == 0 and tile // (tiles // pairs) < pairs:
+                turn(group + 1, tile // (tiles // pairs))
+            middle = tap(2 * tile - 3)
+            late = tap(2 * tile - 2)
+            store(even_ref, tile, early, middle)
+            store(odd_ref, tile, middle, late)
+            early = late
 
 
 def bank_tiles(atom_bank):
@@ -237,7 +229,7 @@
         lax.broadcasted_iota(jnp.int32, (wide, wide), 0)
         == lax.broadcasted_iota(jnp.int32, (wide, wide), 1)
     ).astype(jnp.bfloat16)
-    unroll = next(n for n in (52, 20, 4) if tiles % n == 0)
+    unroll = next(n for n in (260, 52, 20, 4) if tiles % n == 0)
 
     def loop(turn, carry):
         for inner in range(0, unroll, 4):
@@ -279,13 +271,17 @@
     )(even, odd)
 
 
-def conv_kernel(transposed, steps, own_ref, beside_ref, even, odd, out_ref, base, spread, total):
+def conv_kernel(transposed, edge, own_ref, beside_ref, even, odd, out_ref, base, spread, total):
     run, parts, width = own_ref.shape
     lanes = width // LANES
 
-    first, second = (own_ref, beside_ref) if transposed else (beside_ref, own_ref)
-    base[:, :parts] = first[...].astype(jnp.float32)
-    base[:, parts:] = second[...].astype(jnp.float32)
+    beside = beside_ref[...].astype(jnp.float32)
+    if edge is not None:
+        axis, last = edge
+        beside = jnp.where(lax.axis_index(axis) == last, 0.0, beside)
+    own_start = 0 if transposed else parts
+    base[:, own_start : own_start + parts] = own_ref[...].astype(jnp.float32)
+    base[:, parts - own_start : 2 * parts - own_start] = beside
 
     def fill(shift):
         window = base[:, shift : shift + parts].astype(jnp.bfloat16)
@@ -318,25 +314,24 @@
     fill(order[0])
     total[0] = product(0, 1)
     total[1] = jnp.zeros_like(total[1])
-    for turn in range(parts):
+    for turn in range(0, parts, 2):
         fill(order[turn + 1])
-        total[turn % 2] += product(1 + turn * run, run)
+        fill(order[turn + 2])
+        total[turn // 2 % 2] += product(1 + turn * run, 2 * run)
     out_ref[...] = (total[0] + total[1]).reshape(out_ref.shape).astype(out_ref.dtype)
 
 
-def convolve(own, beside, tiles, transposed):
+def convolve(own, beside, tiles, transposed, edge=None):
     run, parts, width = own.shape
     even, odd = tiles
     steps = run * parts + 1
     out_width = PHASES * LANES // 2
     flops = 2 * run * parts * width * out_width * steps
     return pl.pallas_call(
-        functools.partial(conv_kernel, transposed, steps),
+        functools.partial(conv_kernel, transposed, edge),
         in_specs=[pl.BlockSpec(memory_space=pltpu.VMEM)] * 4,
         out_specs=pl.BlockSpec(memory_space=pltpu.VMEM),
-        out_shape=jax.ShapeDtypeStruct(
-            (run, parts, out_width), jnp.float32 if transposed else jnp.bfloat16
-        ),
+        out_shape=jax.ShapeDtypeStruct((run, parts, out_width), jnp.bfloat16),
         scratch_shapes=[
             pltpu.VMEM((run, 2 * parts, width), jnp.float32),
             pltpu.VMEM((width // LANES, (parts + 1) * run, parts, LANES), jnp.bfloat16),
@@ -350,21 +345,11 @@
     )(own, beside, even, odd)
 
 
-def shifted(value, axis, steps, closed):
+def shifted(value, axis, steps):
     count = lax.axis_size(axis)
     if count == 1:
         return jnp.zeros_like(value)
-    swaps = [(i, i ^ 1) for i in range(count)]
-    inner = [(i, i + 1) for i in range(1, count - 1, 2)]
-    inner += [(j, i) for i, j in inner]
-    if closed and count > 2:
-        inner += [(0, count - 1), (count - 1, 0)]
-    first = lax.ppermute(value, axis, swaps)
-    second = lax.ppermute(value, axis, inner) if inner else jnp.zeros_like(value)
-    place = lax.axis_index(axis)
-    source = place - steps
-    second = jnp.where((source >= 0) & (source < count), second, 0)
-    return jnp.where(source == (place ^ 1), first, second)
+    return lax.ppermute(value, axis, [(i, (i + steps) % count) for i in range(count)])
 
 
 def partner(value, axis, step):
@@ -376,13 +361,13 @@
 
 
 def summed(value, axis, gate=None):
-    step = 1
-    while step < lax.axis_size(axis):
+    step = lax.axis_size(axis) // 2
+    while step:
         if step > 1:
             value = value.astype(jnp.bfloat16)
         other = partner(value, axis, step)
-        step *= 2
-        if gate is not None and step >= lax.axis_size(axis):
+        step //= 2
+        if gate is not None and not step:
             other = after(other, gate)
         value = value.astype(jnp.float32) + other.astype(jnp.float32)
     return value
@@ -403,15 +388,16 @@
         moved = current - step * gradient
         return moved - jnp.clip(moved, -bound, bound)
 
+    last = lax.axis_size("tm") - 1
     turned = None
     low16, high16 = low.astype(jnp.bfloat16), high.astype(jnp.bfloat16)
-    earlier = shifted(high16, "tm", 1, False)
+    earlier = shifted(high16, "tm", 1)
     for sweep in range(ITERS):
-        recon_low = convolve(low16, earlier, tiles, False)
+        recon_low = convolve(low16, earlier, tiles, False, ("tm", 0))
         recon_high = convolve(after(high16, recon_low), low16, tiles, False)
         misfit_low = summed(recon_low, "atom") - heard_low
         rounded_low = misfit_low.astype(jnp.bfloat16)
-        following = shifted(rounded_low, "tm", -1, True)
+        following = shifted(rounded_low, "tm", -1)
         gate = None
         if turned is None:
             turned = turn_tiles(*(after(tile, rounded_low) for tile in tiles))
@@ -419,16 +405,16 @@
         misfit_high = summed(recon_high, "atom", gate) - heard_high
         rounded_high = misfit_high.astype(jnp.bfloat16)
         if sweep < ITERS - 1:
-            gradient_high = convolve(rounded_high, following, turned, True)
+            gradient_high = convolve(rounded_high, following, turned, True, ("tm", last))
             gradient_low = convolve(after(rounded_low, gradient_high), rounded_high, turned, True)
             high = shrink(high, summed(gradient_high, "chan"))
             high16 = high.astype(jnp.bfloat16)
-            earlier = shifted(high16, "tm", 1, False)
+            earlier = shifted(high16, "tm", 1)
             low = shrink(low, summed(gradient_low, "chan", earlier))
             low16 = low.astype(jnp.bfloat16)
         else:
             gradient_low = convolve(rounded_low, rounded_high, turned, True)
-            gradient_high = convolve(rounded_high, following, turned, True)
+            gradient_high = convolve(rounded_high, following, turned, True, ("tm", last))
             low = shrink(low, summed(gradient_low, "chan"))
             high = shrink(high, summed(gradient_high, "chan"))
     return from_blocks(low, high), from_blocks(misfit_low, misfit_high)[:chans]

time: 77.4 us -> 62.9 us (0.81)
  local copies, waits for them, and re-layouts: 8.45 us -> 0 us
  starting transfers between devices: 24.2 us -> 17.4 us
  waiting for transfers between devices: 10.8 us -> 14 us
  Pallas kernels: 32.3 us -> 30 us
    unnamed x16 -> x0, local copies, waits for them, and re-layouts: 8.45 us -> none
    ppermute x8 -> x4, starting transfers between devices: 13.5 us -> 8.53 us  [shifted(): lax.ppermute(value, axis, [(i, (i + steps) % count) for i in range(count)])]
    ppermute x8 -> x4, waiting for transfers between devices: 2.5 us -> 5.24 us  [shifted(): lax.ppermute(value, axis, [(i, (i + steps) % count) for i in range(count)])]
    ppermute x12, starting transfers between devices: 10.6 us -> 8.91 us  [partner(): lax.ppermute(value, axis, [(i, i ^ step) for i in range(lax.axis_size(axi...]
    pallas_call x1, Pallas kernels: 6.49 us -> 5 us  [bank_tiles(): pl.pallas_call(functools.partial(bank_kernel, rows), in_specs=[pl.BlockSp...]
    pallas_call x1, Pallas kernels: 3.24 us -> 2.41 us  [turn_tiles(): pl.pallas_call(turn_kernel, in_specs=[spec, spec], out_specs=[spec, spec]...]
  transfers between devices with their start and end apart: 20 -> 16, of which waited for: 10 -> 6; matrix products, arithmetic and copies ran while one was open for 0% -> 0% of each run, Pallas kernels for 29% -> 32%
where the time goes in v8:
time: 62.9 us; the launch traced here: 62.7 us
  Pallas kernels  30 us (48%)
  starting transfers between devices  17.4 us (28%)
  waiting for transfers between devices  14 us (22%)
  between operations  0.84 us (1%)
    pallas_call x8, Pallas kernels, convolve(): pl.pallas_call(functools.partial(conv_kernel, transposed, edge), in_specs...  19.1 us
    ppermute x12, starting transfers between devices, partner(): lax.ppermute(value, axis, [(i, i ^ step) for i in range(lax.axis_size(axi...  8.91 us
    ppermute x12, waiting for transfers between devices, partner(): lax.ppermute(value, axis, [(i, i ^ step) for i in range(lax.axis_size(axi...  8.76 us
    ppermute x4, starting transfers between devices, shifted(): lax.ppermute(value, axis, [(i, (i + steps) % count) for i in range(count)])  8.53 us
    ppermute x4, waiting for transfers between devices, shifted(): lax.ppermute(value, axis, [(i, (i + steps) % count) for i in range(count)])  5.24 us
    pallas_call x1, Pallas kernels, bank_tiles(): pl.pallas_call(functools.partial(bank_kernel, rows), in_specs=[pl.BlockSp...  5 us
    pallas_call x1, Pallas kernels, turn_tiles(): pl.pallas_call(turn_kernel, in_specs=[spec, spec], out_specs=[spec, spec]...  2.41 us
    pallas_call x2, Pallas kernels, from_blocks(): pl.pallas_call(series_kernel, in_specs=[pl.BlockSpec(memory_space=pltpu.V...  2 us
  transfers between devices with their start and end apart: 16, of which 6 were waited for; matrix products, arithmetic and copies ran while one was open for 0% of the time, Pallas kernels for 32%

profile of v8, /device:TPU:0, one launch (start us, length us, event | category | flops | bytes accessed | tf_op | source)
XLA Modules:
  0.0 62.7 jit_solution(1476394371581430217)
XLA Ops:
  0.6 1.4 %to_blocks.1 = (f32[8,16,256]{2,1,0:T(8,128)S(1)}, f32[8,16,256]{2,1,0:T(8,128)S(1)}, f32[8,16,256]{2,1,0:T(8,128)S(1)}, f32[8,16,256]{2,1,0:T(8,128)S(1)}, f32[1,256]{1,0:T(1,128)S(1)}, /*index=5*/f32[1,256]{1,0:T(1,128)S(1)}) custom-call(f32[64,1024]{1,0:T(8,128)} %refs_0_.1, bf16[64,1024]{1,0:T(8,128)(2,1)} %refs_1_.1, f32[1,64]{1,0:T(1,128)} %bitcast.14, ...), custom_call_target="tpu_custom_call" | custom-call | tf_op jit(solution)/shard_map/to_blocks/pallas_call | solution.py:60
  2.1 3.1 %collective-permute-start = (bf16[8,16,256]{2,1,0:T(8,128)(2,1)S(1)}, bf16[8,16,256]{2,1,0:T(8,128)(2,1)S(1)}, u32[]{:S(2)}, u32[]{:S(2)}) collective-permute-start(bf16[8,16,256]{2,1,0:T(8,128)(2,1)S(1)} %convert_element_type.73.own_ref), channel_id=1, source_target_pairs={{0,8},{8,16},{16,24},{24,0},{1,9},{9,17},{17,25},{25,1},{2,10},{10... | collective-permute-start | bytes 196616 | tf_op jit(solution)/shard_map/ppermute | solution.py:352
  5.2 5.0 %bank_tiles.1 = (bf16[260,64,128]{2,1,0:T(8,128)(2,1)S(1)}, bf16[260,64,128]{2,1,0:T(8,128)(2,1)S(1)}) custom-call(bf16[64,64,512]{2,1,0:T(8,128)(2,1)} %bank_hbm.1), custom_call_target="tpu_custom_call" | custom-call | tf_op jit(solution)/shard_map/bank_tiles/pallas_call | solution.py:209
  10.2 0.0 collective-permute-done.beside_ref
  10.2 2.4 %synthesize.4 = bf16[8,16,256]{2,1,0:T(8,128)(2,1)S(1)} custom-call(bf16[8,16,256]{2,1,0:T(8,128)(2,1)S(1)} %convert_element_type.72.own_ref.beside_ref, bf16[8,16,256]{2,1,0:T(8,128)(2,1)S(1)} %collective-permute-done.beside_ref, bf16[260,64,128]{2,1,0:T(8,128)(2,1)S(1)} %get-tuple-element.26.even.even_ref, ...), custom_call_target="tpu_custom_call" | custom-call | flops 2164260864 | bytes 8781824 | tf_op jit(solution)/shard_map/synthesize/pallas_call | solution.py:330
  12.6 1.6 %collective-permute-start.1 = (bf16[8,16,256]{2,1,0:T(8,128)(2,1)S(1)}, bf16[8,16,256]{2,1,0:T(8,128)(2,1)S(1)}, u32[]{:S(2)}, u32[]{:S(2)}) collective-permute-start(bf16[8,16,256]{2,1,0:T(8,128)(2,1)S(1)} %synthesize.4), channel_id=1, source_target_pairs={{0,4},{4,0},{1,5},{5,1},{2,6},{6,2},{3,7},{7,3},{8,12},{12,8},{9,1... | collective-permute-start | bytes 196616 | tf_op jit(solution)/shard_map/ppermute | solution.py:356
  14.2 2.4 %synthesize.5 = bf16[8,16,256]{2,1,0:T(8,128)(2,1)S(1)} custom-call(bf16[8,16,256]{2,1,0:T(8,128)(2,1)S(1)} %convert_element_type.73.own_ref, bf16[8,16,256]{2,1,0:T(8,128)(2,1)S(1)} %convert_element_type.72.own_ref.beside_ref, bf16[260,64,128]{2,1,0:T(8,128)(2,1)S(1)} %get-tuple-element.26.even.even_ref, bf16[260,64,128]{2,1,0:T(8,128)(2,1)S(1)} %get-tuple-element.27.odd.odd_ref), custom_call_target="tpu_custom_call" | custom-call | flops 2164260864 | bytes 8781824 | tf_op jit(solution)/shard_map/synthesize/pallas_call | solution.py:330
  16.6 0.6 collective-permute-start.2
  17.2 0.0 collective-permute-done.1
  17.2 2.3 %collective-permute-start.3 = (bf16[8,16,256]{2,1,0:T(8,128)(2,1)S(1)}, bf16[8,16,256]{2,1,0:T(8,128)(2,1)S(1)}, u32[]{:S(2)}, u32[]{:S(2)}) collective-permute-start(bf16[8,16,256]{2,1,0:T(8,128)(2,1)S(1)} %subtract_convert_fusion.1.own_ref), channel_id=1, source_target_pairs={{0,24},{8,0},{16,8},{24,16},{1,25},{9,1},{17,9},{25,17},{2,26},{10... | collective-permute-start | bytes 196616 | tf_op jit(solution)/shard_map/ppermute | solution.py:352
  19.5 2.4 %turn_tiles.1 = (bf16[260,64,128]{2,1,0:T(8,128)(2,1)S(1)}, bf16[260,64,128]{2,1,0:T(8,128)(2,1)S(1)}) custom-call(bf16[260,64,128]{2,1,0:T(8,128)(2,1)S(1)} %get-tuple-element.26.even.even_ref, bf16[260,64,128]{2,1,0:T(8,128)(2,1)S(1)} %get-tuple-element.27.odd.odd_ref), custom_call_target="tpu_custom_call" | custom-call | flops 2181038080 | bytes 17039360 | tf_op jit(solution)/shard_map/turn_tiles/pallas_call | solution.py:261
  21.9 0.0 collective-permute-done.2
  21.9 0.0 collective-permute-done.3.beside_ref
  22.0 2.4 %correlate.4 = bf16[8,16,256]{2,1,0:T(8,128)(2,1)S(1)} custom-call(bf16[8,16,256]{2,1,0:T(8,128)(2,1)S(1)} %subtract_convert_fusion.own_ref.beside_ref, bf16[8,16,256]{2,1,0:T(8,128)(2,1)S(1)} %collective-permute-done.3.beside_ref, bf16[260,64,128]{2,1,0:T(8,128)(2,1)S(1)} %get-tuple-element.28.even, bf16[260,64,128]{2,1,0:T(8,128)(2,1)S(1)} %get-tuple-element.31.odd), custom_call_target="tpu_custom_call" | custom-call | flops 2164260864 | bytes 8781824 | tf_op jit(solution)/shard_map/correlate/pallas_call | solution.py:330
  24.4 1.8 %collective-permute-start.6 = (bf16[8,16,256]{2,1,0:T(8,128)(2,1)S(1)}, bf16[8,16,256]{2,1,0:T(8,128)(2,1)S(1)}, u32[]{:S(2)}, u32[]{:S(2)}) collective-permute-start(bf16[8,16,256]{2,1,0:T(8,128)(2,1)S(1)} %correlate.4), channel_id=1, source_target_pairs={{0,2},{1,3},{2,0},{3,1},{4,6},{5,7},{6,4},{7,5},{8,10},{9,11},{10,... | collective-permute-start | bytes 196616 | tf_op jit(solution)/shard_map/ppermute | solution.py:356
  26.1 2.4 %correlate.5 = bf16[8,16,256]{2,1,0:T(8,128)(2,1)S(1)} custom-call(bf16[8,16,256]{2,1,0:T(8,128)(2,1)S(1)} %subtract_convert_fusion.1.own_ref, bf16[8,16,256]{2,1,0:T(8,128)(2,1)S(1)} %subtract_convert_fusion.own_ref.beside_ref, bf16[260,64,128]{2,1,0:T(8,128)(2,1)S(1)} %get-tuple-element.28.even, bf16[260,64,128]{2,1,0:T(8,128)(2,1)S(1)} %get-tuple-element.31.odd), custom_call_target="tpu_custom_call" | custom-call | flops 2164260864 | bytes 8781824 | tf_op jit(solution)/shard_map/correlate/pallas_call | solution.py:330
  28.5 0.4 collective-permute-start.4
  28.9 0.0 collective-permute-done.6
  28.9 0.1 collective-permute-start.7
  29.0 3.9 %collective-permute-done.4 = bf16[8,16,256]{2,1,0:T(8,128)(2,1)S(1)} collective-permute-done((bf16[8,16,256]{2,1,0:T(8,128)(2,1)S(1)}, bf16[8,16,256]{2,1,0:T(8,128)(2,1)S(1)}, u32[]{:S(2)}, u32[]{:S(2)}) %collective-permute-start.4) | collective-permute-done | bytes 65568 | tf_op jit(solution)/shard_map/ppermute | solution.py:356
  32.9 0.1 collective-permute-start.5
  33.0 0.0 collective-permute-done.7
  33.0 0.1 fusion.own_ref
  33.0 1.4 %collective-permute-start.8 = (bf16[8,16,256]{2,1,0:T(8,128)(2,1)S(1)}, bf16[8,16,256]{2,1,0:T(8,128)(2,1)S(1)}, u32[]{:S(2)}, u32[]{:S(2)}) collective-permute-start(bf16[8,16,256]{2,1,0:T(8,128)(2,1)S(1)} %fusion.own_ref), channel_id=1, source_target_pairs={{0,8},{8,16},{16,24},{24,0},{1,9},{9,17},{17,25},{25,1},{2,10},{10... | collective-permute-start | bytes 196616 | tf_op jit(solution)/shard_map/ppermute | solution.py:352
  34.4 0.0 collective-permute-done.5
  34.4 5.2 %collective-permute-done.8.beside_ref = bf16[8,16,256]{2,1,0:T(8,128)(2,1)S(1)} collective-permute-done((bf16[8,16,256]{2,1,0:T(8,128)(2,1)S(1)}, bf16[8,16,256]{2,1,0:T(8,128)(2,1)S(1)}, u32[]{:S(2)}, u32[]{:S(2)}) %collective-permute-start.8) | collective-permute-done | bytes 65568 | tf_op jit(solution)/shard_map/ppermute | solution.py:352
  39.6 0.1 fusion.1.own_ref.beside_ref
  39.7 2.4 %synthesize.6 = bf16[8,16,256]{2,1,0:T(8,128)(2,1)S(1)} custom-call(bf16[8,16,256]{2,1,0:T(8,128)(2,1)S(1)} %fusion.1.own_ref.beside_ref, bf16[8,16,256]{2,1,0:T(8,128)(2,1)S(1)} %collective-permute-done.8.beside_ref, bf16[260,64,128]{2,1,0:T(8,128)(2,1)S(1)} %get-tuple-element.26.even.even_ref, bf16[260,64,128]{2,1,0:T(8,128)(2,1)S(1)} %get-tuple-element.27.odd.odd_ref), custom_call_target="tpu_custom_call" | custom-call | flops 2164260864 | bytes 8781824 | tf_op jit(solution)/shard_map/synthesize/pallas_call | solution.py:330
  42.1 1.5 %collective-permute-start.9 = (bf16[8,16,256]{2,1,0:T(8,128)(2,1)S(1)}, bf16[8,16,256]{2,1,0:T(8,128)(2,1)S(1)}, u32[]{:S(2)}, u32[]{:S(2)}) collective-permute-start(bf16[8,16,256]{2,1,0:T(8,128)(2,1)S(1)} %synthesize.6), channel_id=1, source_target_pairs={{0,4},{4,0},{1,5},{5,1},{2,6},{6,2},{3,7},{7,3},{8,12},{12,8},{9,1... | collective-permute-start | bytes 196616 | tf_op jit(solution)/shard_map/ppermute | solution.py:356
  43.7 2.4 %synthesize.7 = bf16[8,16,256]{2,1,0:T(8,128)(2,1)S(1)} custom-call(bf16[8,16,256]{2,1,0:T(8,128)(2,1)S(1)} %fusion.own_ref, bf16[8,16,256]{2,1,0:T(8,128)(2,1)S(1)} %fusion.1.own_ref.beside_ref, bf16[260,64,128]{2,1,0:T(8,128)(2,1)S(1)} %get-tuple-element.26.even.even_ref, bf16[260,64,128]{2,1,0:T(8,128)(2,1)S(1)} %get-tuple-element.27.odd.odd_ref), custom_call_target="tpu_custom_call" | custom-call | flops 2164260864 | bytes 8781824 | tf_op jit(solution)/shard_map/synthesize/pallas_call | solution.py:330
  46.0 0.6 collective-permute-start.10
  46.7 0.0 collective-permute-done.9
  46.7 1.8 %collective-permute-start.13 = (bf16[8,16,256]{2,1,0:T(8,128)(2,1)S(1)}, bf16[8,16,256]{2,1,0:T(8,128)(2,1)S(1)}, u32[]{:S(2)}, u32[]{:S(2)}) collective-permute-start(bf16[8,16,256]{2,1,0:T(8,128)(2,1)S(1)} %get-tuple-element.38.own_ref), channel_id=1, source_target_pairs={{0,24},{8,0},{16,8},{24,16},{1,25},{9,1},{17,9},{25,17},{2,26},{10... | collective-permute-start | bytes 196616 | tf_op jit(solution)/shard_map/ppermute | solution.py:352
  48.5 1.9 %collective-permute-done.10 = bf16[8,16,256]{2,1,0:T(8,128)(2,1)S(1)} collective-permute-done((bf16[8,16,256]{2,1,0:T(8,128)(2,1)S(1)}, bf16[8,16,256]{2,1,0:T(8,128)(2,1)S(1)}, u32[]{:S(2)}, u32[]{:S(2)}) %collective-permute-start.10) | collective-permute-done | bytes 65568 | tf_op jit(solution)/shard_map/ppermute | solution.py:356
  50.4 2.4 %correlate.6 = bf16[8,16,256]{2,1,0:T(8,128)(2,1)S(1)} custom-call(bf16[8,16,256]{2,1,0:T(8,128)(2,1)S(1)} %get-tuple-element.38.own_ref, bf16[8,16,256]{2,1,0:T(8,128)(2,1)S(1)} %get-tuple-element.36.beside_ref.own_ref, bf16[260,64,128]{2,1,0:T(8,128)(2,1)S(1)} %get-tuple-element.28.even, bf16[260,64,128]{2,1,0:T(8,128)(2,1)S(1)} %get-tuple-element.31.odd), custom_call_target="tpu_custom_call" | custom-call | flops 2164260864 | bytes 8781824 | tf_op jit(solution)/shard_map/correlate/pallas_call | solution.py:330
  52.8 0.6 collective-permute-start.11
  53.4 0.0 collective-permute-done.13.beside_ref
  53.4 2.4 %correlate.7 = bf16[8,16,256]{2,1,0:T(8,128)(2,1)S(1)} custom-call(bf16[8,16,256]{2,1,0:T(8,128)(2,1)S(1)} %get-tuple-element.36.beside_ref.own_ref, bf16[8,16,256]{2,1,0:T(8,128)(2,1)S(1)} %collective-permute-done.13.beside_ref, bf16[260,64,128]{2,1,0:T(8,128)(2,1)S(1)} %get-tuple-element.28.even, bf16[260,64,128]{2,1,0:T(8,128)(2,1)S(1)} %get-tuple-element.31.odd), custom_call_target="tpu_custom_call" | custom-call | flops 2164260864 | bytes 8781824 | tf_op jit(solution)/shard_map/correlate/pallas_call | solution.py:330
  55.8 1.6 %collective-permute-start.14 = (bf16[8,16,256]{2,1,0:T(8,128)(2,1)S(1)}, bf16[8,16,256]{2,1,0:T(8,128)(2,1)S(1)}, u32[]{:S(2)}, u32[]{:S(2)}) collective-permute-start(bf16[8,16,256]{2,1,0:T(8,128)(2,1)S(1)} %correlate.7), channel_id=1, source_target_pairs={{0,2},{1,3},{2,0},{3,1},{4,6},{5,7},{6,4},{7,5},{8,10},{9,11},{10,... | collective-permute-start | bytes 196616 | tf_op jit(solution)/shard_map/ppermute | solution.py:356
  57.4 0.4 collective-permute-done.11
  57.8 0.1 collective-permute-start.12
  57.9 2.2 %collective-permute-done.14 = bf16[8,16,256]{2,1,0:T(8,128)(2,1)S(1)} collective-permute-done((bf16[8,16,256]{2,1,0:T(8,128)(2,1)S(1)}, bf16[8,16,256]{2,1,0:T(8,128)(2,1)S(1)}, u32[]{:S(2)}, u32[]{:S(2)}) %collective-permute-start.14) | collective-permute-done | bytes 65568 | tf_op jit(solution)/shard_map/ppermute | solution.py:356
  60.1 0.1 collective-permute-start.15
  60.2 1.0 %from_blocks.3 = f32[64,1024]{1,0:T(8,128)} custom-call(f32[8,16,256]{2,1,0:T(8,128)S(1)} %get-tuple-element.39.low_ref, f32[8,16,256]{2,1,0:T(8,128)S(1)} %get-tuple-element.37.high_ref), custom_call_target="tpu_custom_call" | custom-call | tf_op jit(solution)/shard_map/from_blocks/pallas_call | solution.py:96
  61.2 0.0 collective-permute-done.12
  61.2 0.3 collective-permute-done.15
  61.5 0.2 minimum_subtract_fusion
  61.7 1.0 %from_blocks.2 = f32[64,1024]{1,0:T(8,128)} custom-call(f32[8,16,256]{2,1,0:T(8,128)S(1)} %get-tuple-element.41.low_ref, f32[8,16,256]{2,1,0:T(8,128)S(1)} %get-tuple-element.40.high_ref), custom_call_target="tpu_custom_call" | custom-call | tf_op jit(solution)/shard_map/from_blocks/pallas_call | solution.py:96
  (11 shorter events, 0.2 us)
Async XLA Ops:
  2.1 8.1 %collective-permute-start = (bf16[8,16,256]{2,1,0:T(8,128)(2,1)S(1)}, bf16[8,16,256]{2,1,0:T(8,128)(2,1)S(1)}, u32[]{:S(2)}, u32[]{:S(2)}) collective-permute-start(bf16[8,16,256]{2,1,0:T(8,128)(2,1)S(1)} %convert_element_type.73.own_ref), channel_id=1, source_target_pairs={{0,8},{8,16},{16,24},{24,0},{1,9},{9,17},{17,25},{25,1},{2,10},{10... | collective-permute-start | bytes 196616 | tf_op jit(solution)/shard_map/ppermute | solution.py:352
  12.6 4.6 %collective-permute-start.1 = (bf16[8,16,256]{2,1,0:T(8,128)(2,1)S(1)}, bf16[8,16,256]{2,1,0:T(8,128)(2,1)S(1)}, u32[]{:S(2)}, u32[]{:S(2)}) collective-permute-start(bf16[8,16,256]{2,1,0:T(8,128)(2,1)S(1)} %synthesize.4), channel_id=1, source_target_pairs={{0,4},{4,0},{1,5},{5,1},{2,6},{6,2},{3,7},{7,3},{8,12},{12,8},{9,1... | collective-permute-start | bytes 196616 | tf_op jit(solution)/shard_map/ppermute | solution.py:356
  16.6 5.3 %collective-permute-start.2 = (bf16[8,16,256]{2,1,0:T(8,128)(2,1)S(1)}, bf16[8,16,256]{2,1,0:T(8,128)(2,1)S(1)}, u32[]{:S(2)}, u32[]{:S(2)}) collective-permute-start(bf16[8,16,256]{2,1,0:T(8,128)(2,1)S(1)} %synthesize.5), channel_id=1, source_target_pairs={{0,4},{4,0},{1,5},{5,1},{2,6},{6,2},{3,7},{7,3},{8,12},{12,8},{9,1... | collective-permute-start | bytes 196616 | tf_op jit(solution)/shard_map/ppermute | solution.py:356
  17.2 4.8 %collective-permute-start.3 = (bf16[8,16,256]{2,1,0:T(8,128)(2,1)S(1)}, bf16[8,16,256]{2,1,0:T(8,128)(2,1)S(1)}, u32[]{:S(2)}, u32[]{:S(2)}) collective-permute-start(bf16[8,16,256]{2,1,0:T(8,128)(2,1)S(1)} %subtract_convert_fusion.1.own_ref), channel_id=1, source_target_pairs={{0,24},{8,0},{16,8},{24,16},{1,25},{9,1},{17,9},{25,17},{2,26},{10... | collective-permute-start | bytes 196616 | tf_op jit(solution)/shard_map/ppermute | solution.py:352
  24.4 4.6 %collective-permute-start.6 = (bf16[8,16,256]{2,1,0:T(8,128)(2,1)S(1)}, bf16[8,16,256]{2,1,0:T(8,128)(2,1)S(1)}, u32[]{:S(2)}, u32[]{:S(2)}) collective-permute-start(bf16[8,16,256]{2,1,0:T(8,128)(2,1)S(1)} %correlate.4), channel_id=1, source_target_pairs={{0,2},{1,3},{2,0},{3,1},{4,6},{5,7},{6,4},{7,5},{8,10},{9,11},{10,... | collective-permute-start | bytes 196616 | tf_op jit(solution)/shard_map/ppermute | solution.py:356
  28.5 4.3 %collective-permute-start.4 = (bf16[8,16,256]{2,1,0:T(8,128)(2,1)S(1)}, bf16[8,16,256]{2,1,0:T(8,128)(2,1)S(1)}, u32[]{:S(2)}, u32[]{:S(2)}) collective-permute-start(bf16[8,16,256]{2,1,0:T(8,128)(2,1)S(1)} %correlate.5), channel_id=1, source_target_pairs={{0,2},{1,3},{2,0},{3,1},{4,6},{5,7},{6,4},{7,5},{8,10},{9,11},{10,... | collective-permute-start | bytes 196616 | tf_op jit(solution)/shard_map/ppermute | solution.py:356
  28.9 4.0 %collective-permute-start.7 = (f32[8,16,256]{2,1,0:T(8,128)S(1)}, f32[8,16,256]{2,1,0:T(8,128)S(1)}, u32[]{:S(2)}, u32[]{:S(2)}) collective-permute-start(f32[8,16,256]{2,1,0:T(8,128)S(1)} %convert_add_fusion.2), channel_id=1, source_target_pairs={{0,1},{1,0},{2,3},{3,2},{4,5},{5,4},{6,7},{7,6},{8,9},{9,8},{10,11... | collective-permute-start | bytes 393224 | tf_op jit(solution)/shard_map/ppermute | solution.py:356
  32.9 1.5 %collective-permute-start.5 = (f32[8,16,256]{2,1,0:T(8,128)S(1)}, f32[8,16,256]{2,1,0:T(8,128)S(1)}, u32[]{:S(2)}, u32[]{:S(2)}) collective-permute-start(f32[8,16,256]{2,1,0:T(8,128)S(1)} %convert_add_fusion.3), channel_id=1, source_target_pairs={{0,1},{1,0},{2,3},{3,2},{4,5},{5,4},{6,7},{7,6},{8,9},{9,8},{10,11... | collective-permute-start | bytes 393224 | tf_op jit(solution)/shard_map/ppermute | solution.py:356
  33.0 6.6 %collective-permute-start.8 = (bf16[8,16,256]{2,1,0:T(8,128)(2,1)S(1)}, bf16[8,16,256]{2,1,0:T(8,128)(2,1)S(1)}, u32[]{:S(2)}, u32[]{:S(2)}) collective-permute-start(bf16[8,16,256]{2,1,0:T(8,128)(2,1)S(1)} %fusion.own_ref), channel_id=1, source_target_pairs={{0,8},{8,16},{16,24},{24,0},{1,9},{9,17},{17,25},{25,1},{2,10},{10... | collective-permute-start | bytes 196616 | tf_op jit(solution)/shard_map/ppermute | solution.py:352
  42.1 4.6 %collective-permute-start.9 = (bf16[8,16,256]{2,1,0:T(8,128)(2,1)S(1)}, bf16[8,16,256]{2,1,0:T(8,128)(2,1)S(1)}, u32[]{:S(2)}, u32[]{:S(2)}) collective-permute-start(bf16[8,16,256]{2,1,0:T(8,128)(2,1)S(1)} %synthesize.6), channel_id=1, source_target_pairs={{0,4},{4,0},{1,5},{5,1},{2,6},{6,2},{3,7},{7,3},{8,12},{12,8},{9,1... | collective-permute-start | bytes 196616 | tf_op jit(solution)/shard_map/ppermute | solution.py:356
  46.0 4.3 %collective-permute-start.10 = (bf16[8,16,256]{2,1,0:T(8,128)(2,1)S(1)}, bf16[8,16,256]{2,1,0:T(8,128)(2,1)S(1)}, u32[]{:S(2)}, u32[]{:S(2)}) collective-permute-start(bf16[8,16,256]{2,1,0:T(8,128)(2,1)S(1)} %synthesize.7), channel_id=1, source_target_pairs={{0,4},{4,0},{1,5},{5,1},{2,6},{6,2},{3,7},{7,3},{8,12},{12,8},{9,1... | collective-permute-start | bytes 196616 | tf_op jit(solution)/shard_map/ppermute | solution.py:356
  46.7 6.7 %collective-permute-start.13 = (bf16[8,16,256]{2,1,0:T(8,128)(2,1)S(1)}, bf16[8,16,256]{2,1,0:T(8,128)(2,1)S(1)}, u32[]{:S(2)}, u32[]{:S(2)}) collective-permute-start(bf16[8,16,256]{2,1,0:T(8,128)(2,1)S(1)} %get-tuple-element.38.own_ref), channel_id=1, source_target_pairs={{0,24},{8,0},{16,8},{24,16},{1,25},{9,1},{17,9},{25,17},{2,26},{10... | collective-permute-start | bytes 196616 | tf_op jit(solution)/shard_map/ppermute | solution.py:352
  52.8 5.0 %collective-permute-start.11 = (bf16[8,16,256]{2,1,0:T(8,128)(2,1)S(1)}, bf16[8,16,256]{2,1,0:T(8,128)(2,1)S(1)}, u32[]{:S(2)}, u32[]{:S(2)}) collective-permute-start(bf16[8,16,256]{2,1,0:T(8,128)(2,1)S(1)} %correlate.6), channel_id=1, source_target_pairs={{0,2},{1,3},{2,0},{3,1},{4,6},{5,7},{6,4},{7,5},{8,10},{9,11},{10,... | collective-permute-start | bytes 196616 | tf_op jit(solution)/shard_map/ppermute | solution.py:356
  55.8 4.3 %collective-permute-start.14 = (bf16[8,16,256]{2,1,0:T(8,128)(2,1)S(1)}, bf16[8,16,256]{2,1,0:T(8,128)(2,1)S(1)}, u32[]{:S(2)}, u32[]{:S(2)}) collective-permute-start(bf16[8,16,256]{2,1,0:T(8,128)(2,1)S(1)} %correlate.7), channel_id=1, source_target_pairs={{0,2},{1,3},{2,0},{3,1},{4,6},{5,7},{6,4},{7,5},{8,10},{9,11},{10,... | collective-permute-start | bytes 196616 | tf_op jit(solution)/shard_map/ppermute | solution.py:356
  57.8 3.4 %collective-permute-start.12 = (f32[8,16,256]{2,1,0:T(8,128)S(1)}, f32[8,16,256]{2,1,0:T(8,128)S(1)}, u32[]{:S(2)}, u32[]{:S(2)}) collective-permute-start(f32[8,16,256]{2,1,0:T(8,128)S(1)} %convert_add_fusion.1), channel_id=1, source_target_pairs={{0,1},{1,0},{2,3},{3,2},{4,5},{5,4},{6,7},{7,6},{8,9},{9,8},{10,11... | collective-permute-start | bytes 393224 | tf_op jit(solution)/shard_map/ppermute | solution.py:356
  60.1 1.4 %collective-permute-start.15 = (f32[8,16,256]{2,1,0:T(8,128)S(1)}, f32[8,16,256]{2,1,0:T(8,128)S(1)}, u32[]{:S(2)}, u32[]{:S(2)}) collective-permute-start(f32[8,16,256]{2,1,0:T(8,128)S(1)} %convert_add_fusion), channel_id=1, source_target_pairs={{0,1},{1,0},{2,3},{3,2},{4,5},{5,4},{6,7},{7,6},{8,9},{9,8},{10,11... | collective-permute-start | bytes 393224 | tf_op jit(solution)/shard_map/ppermute | solution.py:356

commit v9 on v8

--- a/solution.py
+++ b/solution.py
@@ -360,12 +360,15 @@
     return lax.optimization_barrier((value, *others))[0]
 
 
-def summed(value, axis, gate=None):
+def summed(value, axis, gate=None, early_gate=None):
     step = lax.axis_size(axis) // 2
+    first = step
     while step:
         if step > 1:
             value = value.astype(jnp.bfloat16)
         other = partner(value, axis, step)
+        if early_gate is not None and step == first:
+            other = after(other, early_gate)
         step //= 2
         if gate is not None and not step:
             other = after(other, gate)
@@ -407,10 +410,10 @@
         if sweep < ITERS - 1:
             gradient_high = convolve(rounded_high, following, turned, True, ("tm", last))
             gradient_low = convolve(after(rounded_low, gradient_high), rounded_high, turned, True)
-            high = shrink(high, summed(gradient_high, "chan"))
+            high = shrink(high, summed(gradient_high, "chan", None, gradient_low))
             high16 = high.astype(jnp.bfloat16)
             earlier = shifted(high16, "tm", 1)
-            low = shrink(low, summed(gradient_low, "chan", earlier))
+            low = shrink(low, summed(gradient_low, "chan", None, earlier))
             low16 = low.astype(jnp.bfloat16)
         else:
             gradient_low = convolve(rounded_low, rounded_high, turned, True)

time: 62.9 us -> 62.4 us (level)
  waiting for transfers between devices: 14 us -> 12 us
  starting transfers between devices: 17.4 us -> 18.9 us
    ppermute x4, waiting for transfers between devices: 5.24 us -> 3.68 us  [shifted(): lax.ppermute(value, axis, [(i, (i + steps) % count) for i in range(count)])]
    ppermute x12, starting transfers between devices: 8.91 us -> 10.3 us  [partner(): lax.ppermute(value, axis, [(i, i ^ step) for i in range(lax.axis_size(axi...]
  transfers between devices with their start and end apart: 16 -> 16, of which waited for: 6 -> 7; matrix products, arithmetic and copies ran while one was open for 0% -> 0% of each run, Pallas kernels for 32% -> 33%
where the time goes in v9:
time: 62.4 us; the launch traced here: 62.2 us
  Pallas kernels  30 us (48%)
  starting transfers between devices  18.9 us (30%)
  waiting for transfers between devices  12 us (19%)
  between operations  0.84 us (1%)
    pallas_call x8, Pallas kernels, convolve(): pl.pallas_call(functools.partial(conv_kernel, transposed, edge), in_specs...  19.1 us
    ppermute x12, starting transfers between devices, partner(): lax.ppermute(value, axis, [(i, i ^ step) for i in range(lax.axis_size(axi...  10.3 us
    ppermute x4, starting transfers between devices, shifted(): lax.ppermute(value, axis, [(i, (i + steps) % count) for i in range(count)])  8.6 us
    ppermute x12, waiting for transfers between devices, partner(): lax.ppermute(value, axis, [(i, i ^ step) for i in range(lax.axis_size(axi...  8.36 us
    pallas_call x1, Pallas kernels, bank_tiles(): pl.pallas_call(functools.partial(bank_kernel, rows), in_specs=[pl.BlockSp...  5 us
    ppermute x4, waiting for transfers between devices, shifted(): lax.ppermute(value, axis, [(i, (i + steps) % count) for i in range(count)])  3.68 us
    pallas_call x1, Pallas kernels, turn_tiles(): pl.pallas_call(turn_kernel, in_specs=[spec, spec], out_specs=[spec, spec]...  2.41 us
    pallas_call x2, Pallas kernels, from_blocks(): pl.pallas_call(series_kernel, in_specs=[pl.BlockSpec(memory_space=pltpu.V...  2 us
  transfers between devices with their start and end apart: 16, of which 7 were waited for; matrix products, arithmetic and copies ran while one was open for 0% of the time, Pallas kernels for 33%

profile of v9, /device:TPU:0, one launch (start us, length us, event | category | flops | bytes accessed | tf_op | source)
XLA Modules:
  0.0 62.2 jit_solution(14559193171381608726)
XLA Ops:
  0.6 1.4 %to_blocks.1 = (f32[8,16,256]{2,1,0:T(8,128)S(1)}, f32[8,16,256]{2,1,0:T(8,128)S(1)}, f32[8,16,256]{2,1,0:T(8,128)S(1)}, f32[8,16,256]{2,1,0:T(8,128)S(1)}, f32[1,256]{1,0:T(1,128)S(1)}, /*index=5*/f32[1,256]{1,0:T(1,128)S(1)}) custom-call(f32[64,1024]{1,0:T(8,128)} %refs_0_.1, bf16[64,1024]{1,0:T(8,128)(2,1)} %refs_1_.1, f32[1,64]{1,0:T(1,128)} %bitcast.14, ...), custom_call_target="tpu_custom_call" | custom-call | tf_op jit(solution)/shard_map/to_blocks/pallas_call | solution.py:60
  2.1 3.1 %collective-permute-start = (bf16[8,16,256]{2,1,0:T(8,128)(2,1)S(1)}, bf16[8,16,256]{2,1,0:T(8,128)(2,1)S(1)}, u32[]{:S(2)}, u32[]{:S(2)}) collective-permute-start(bf16[8,16,256]{2,1,0:T(8,128)(2,1)S(1)} %convert_element_type.73.own_ref), channel_id=1, source_target_pairs={{0,8},{8,16},{16,24},{24,0},{1,9},{9,17},{17,25},{25,1},{2,10},{10... | collective-permute-start | bytes 196616 | tf_op jit(solution)/shard_map/ppermute | solution.py:352
  5.2 5.0 %bank_tiles.1 = (bf16[260,64,128]{2,1,0:T(8,128)(2,1)S(1)}, bf16[260,64,128]{2,1,0:T(8,128)(2,1)S(1)}) custom-call(bf16[64,64,512]{2,1,0:T(8,128)(2,1)} %bank_hbm.1), custom_call_target="tpu_custom_call" | custom-call | tf_op jit(solution)/shard_map/bank_tiles/pallas_call | solution.py:209
  10.2 0.0 collective-permute-done.beside_ref
  10.2 2.4 %synthesize.4 = bf16[8,16,256]{2,1,0:T(8,128)(2,1)S(1)} custom-call(bf16[8,16,256]{2,1,0:T(8,128)(2,1)S(1)} %convert_element_type.72.own_ref.beside_ref, bf16[8,16,256]{2,1,0:T(8,128)(2,1)S(1)} %collective-permute-done.beside_ref, bf16[260,64,128]{2,1,0:T(8,128)(2,1)S(1)} %get-tuple-element.27.even.even_ref, ...), custom_call_target="tpu_custom_call" | custom-call | flops 2164260864 | bytes 8781824 | tf_op jit(solution)/shard_map/synthesize/pallas_call | solution.py:330
  12.6 1.6 %collective-permute-start.1 = (bf16[8,16,256]{2,1,0:T(8,128)(2,1)S(1)}, bf16[8,16,256]{2,1,0:T(8,128)(2,1)S(1)}, u32[]{:S(2)}, u32[]{:S(2)}) collective-permute-start(bf16[8,16,256]{2,1,0:T(8,128)(2,1)S(1)} %synthesize.4), channel_id=1, source_target_pairs={{0,4},{4,0},{1,5},{5,1},{2,6},{6,2},{3,7},{7,3},{8,12},{12,8},{9,1... | collective-permute-start | bytes 196616 | tf_op jit(solution)/shard_map/ppermute | solution.py:356
  14.2 2.4 %synthesize.5 = bf16[8,16,256]{2,1,0:T(8,128)(2,1)S(1)} custom-call(bf16[8,16,256]{2,1,0:T(8,128)(2,1)S(1)} %convert_element_type.73.own_ref, bf16[8,16,256]{2,1,0:T(8,128)(2,1)S(1)} %convert_element_type.72.own_ref.beside_ref, bf16[260,64,128]{2,1,0:T(8,128)(2,1)S(1)} %get-tuple-element.27.even.even_ref, bf16[260,64,128]{2,1,0:T(8,128)(2,1)S(1)} %get-tuple-element.28.odd.odd_ref), custom_call_target="tpu_custom_call" | custom-call | flops 2164260864 | bytes 8781824 | tf_op jit(solution)/shard_map/synthesize/pallas_call | solution.py:330
  16.6 0.6 collective-permute-start.2
  17.2 0.0 collective-permute-done.1
  17.2 2.3 %collective-permute-start.3 = (bf16[8,16,256]{2,1,0:T(8,128)(2,1)S(1)}, bf16[8,16,256]{2,1,0:T(8,128)(2,1)S(1)}, u32[]{:S(2)}, u32[]{:S(2)}) collective-permute-start(bf16[8,16,256]{2,1,0:T(8,128)(2,1)S(1)} %subtract_convert_fusion.1.own_ref), channel_id=1, source_target_pairs={{0,24},{8,0},{16,8},{24,16},{1,25},{9,1},{17,9},{25,17},{2,26},{10... | collective-permute-start | bytes 196616 | tf_op jit(solution)/shard_map/ppermute | solution.py:352
  19.5 2.4 %turn_tiles.1 = (bf16[260,64,128]{2,1,0:T(8,128)(2,1)S(1)}, bf16[260,64,128]{2,1,0:T(8,128)(2,1)S(1)}) custom-call(bf16[260,64,128]{2,1,0:T(8,128)(2,1)S(1)} %get-tuple-element.27.even.even_ref, bf16[260,64,128]{2,1,0:T(8,128)(2,1)S(1)} %get-tuple-element.28.odd.odd_ref), custom_call_target="tpu_custom_call" | custom-call | flops 2181038080 | bytes 17039360 | tf_op jit(solution)/shard_map/turn_tiles/pallas_call | solution.py:261
  21.9 0.0 collective-permute-done.2
  21.9 0.0 collective-permute-done.3.beside_ref
  22.0 2.4 %correlate.4 = bf16[8,16,256]{2,1,0:T(8,128)(2,1)S(1)} custom-call(bf16[8,16,256]{2,1,0:T(8,128)(2,1)S(1)} %subtract_convert_fusion.own_ref.beside_ref, bf16[8,16,256]{2,1,0:T(8,128)(2,1)S(1)} %collective-permute-done.3.beside_ref, bf16[260,64,128]{2,1,0:T(8,128)(2,1)S(1)} %get-tuple-element.29.even, bf16[260,64,128]{2,1,0:T(8,128)(2,1)S(1)} %get-tuple-element.32.odd), custom_call_target="tpu_custom_call" | custom-call | flops 2164260864 | bytes 8781824 | tf_op jit(solution)/shard_map/correlate/pallas_call | solution.py:330
  24.3 1.8 %collective-permute-start.5 = (bf16[8,16,256]{2,1,0:T(8,128)(2,1)S(1)}, bf16[8,16,256]{2,1,0:T(8,128)(2,1)S(1)}, u32[]{:S(2)}, u32[]{:S(2)}) collective-permute-start(bf16[8,16,256]{2,1,0:T(8,128)(2,1)S(1)} %correlate.4), channel_id=1, source_target_pairs={{0,2},{1,3},{2,0},{3,1},{4,6},{5,7},{6,4},{7,5},{8,10},{9,11},{10,... | collective-permute-start | bytes 196616 | tf_op jit(solution)/shard_map/ppermute | solution.py:356
  26.1 2.4 %correlate.5 = bf16[8,16,256]{2,1,0:T(8,128)(2,1)S(1)} custom-call(bf16[8,16,256]{2,1,0:T(8,128)(2,1)S(1)} %subtract_convert_fusion.1.own_ref, bf16[8,16,256]{2,1,0:T(8,128)(2,1)S(1)} %subtract_convert_fusion.own_ref.beside_ref, bf16[260,64,128]{2,1,0:T(8,128)(2,1)S(1)} %get-tuple-element.29.even, bf16[260,64,128]{2,1,0:T(8,128)(2,1)S(1)} %get-tuple-element.32.odd), custom_call_target="tpu_custom_call" | custom-call | flops 2164260864 | bytes 8781824 | tf_op jit(solution)/shard_map/correlate/pallas_call | solution.py:330
  28.5 0.2 collective-permute-done.5
  28.7 0.1 collective-permute-start.6
  28.8 1.8 %collective-permute-start.4 = (bf16[8,16,256]{2,1,0:T(8,128)(2,1)S(1)}, bf16[8,16,256]{2,1,0:T(8,128)(2,1)S(1)}, u32[]{:S(2)}, u32[]{:S(2)}) collective-permute-start(bf16[8,16,256]{2,1,0:T(8,128)(2,1)S(1)} %correlate.5), channel_id=1, source_target_pairs={{0,2},{1,3},{2,0},{3,1},{4,6},{5,7},{6,4},{7,5},{8,10},{9,11},{10,... | collective-permute-start | bytes 196616 | tf_op jit(solution)/shard_map/ppermute | solution.py:356
  30.6 0.0 collective-permute-done.6
  30.6 0.1 fusion.own_ref
  30.6 1.4 %collective-permute-start.7 = (bf16[8,16,256]{2,1,0:T(8,128)(2,1)S(1)}, bf16[8,16,256]{2,1,0:T(8,128)(2,1)S(1)}, u32[]{:S(2)}, u32[]{:S(2)}) collective-permute-start(bf16[8,16,256]{2,1,0:T(8,128)(2,1)S(1)} %fusion.own_ref), channel_id=1, source_target_pairs={{0,8},{8,16},{16,24},{24,0},{1,9},{9,17},{17,25},{25,1},{2,10},{10... | collective-permute-start | bytes 196616 | tf_op jit(solution)/shard_map/ppermute | solution.py:352
  32.0 1.3 %collective-permute-done.4 = bf16[8,16,256]{2,1,0:T(8,128)(2,1)S(1)} collective-permute-done((bf16[8,16,256]{2,1,0:T(8,128)(2,1)S(1)}, bf16[8,16,256]{2,1,0:T(8,128)(2,1)S(1)}, u32[]{:S(2)}, u32[]{:S(2)}) %collective-permute-start.4) | collective-permute-done | bytes 65568 | tf_op jit(solution)/shard_map/ppermute | solution.py:356
  33.3 3.7 %collective-permute-done.7.beside_ref = bf16[8,16,256]{2,1,0:T(8,128)(2,1)S(1)} collective-permute-done((bf16[8,16,256]{2,1,0:T(8,128)(2,1)S(1)}, bf16[8,16,256]{2,1,0:T(8,128)(2,1)S(1)}, u32[]{:S(2)}, u32[]{:S(2)}) %collective-permute-start.7) | collective-permute-done | bytes 65568 | tf_op jit(solution)/shard_map/ppermute | solution.py:352
  37.0 0.1 collective-permute-start.8
  37.1 1.3 %collective-permute-done.8 = f32[8,16,256]{2,1,0:T(8,128)S(1)} collective-permute-done((f32[8,16,256]{2,1,0:T(8,128)S(1)}, f32[8,16,256]{2,1,0:T(8,128)S(1)}, u32[]{:S(2)}, u32[]{:S(2)}) %collective-permute-start.8) | collective-permute-done | bytes 131104 | tf_op jit(solution)/shard_map/ppermute | solution.py:356
  38.4 0.1 fusion.1.own_ref.beside_ref
  38.4 2.4 %synthesize.6 = bf16[8,16,256]{2,1,0:T(8,128)(2,1)S(1)} custom-call(bf16[8,16,256]{2,1,0:T(8,128)(2,1)S(1)} %fusion.1.own_ref.beside_ref, bf16[8,16,256]{2,1,0:T(8,128)(2,1)S(1)} %collective-permute-done.7.beside_ref, bf16[260,64,128]{2,1,0:T(8,128)(2,1)S(1)} %get-tuple-element.27.even.even_ref, bf16[260,64,128]{2,1,0:T(8,128)(2,1)S(1)} %get-tuple-element.28.odd.odd_ref), custom_call_target="tpu_custom_call" | custom-call | flops 2164260864 | bytes 8781824 | tf_op jit(solution)/shard_map/synthesize/pallas_call | solution.py:330
  40.9 1.6 %collective-permute-start.9 = (bf16[8,16,256]{2,1,0:T(8,128)(2,1)S(1)}, bf16[8,16,256]{2,1,0:T(8,128)(2,1)S(1)}, u32[]{:S(2)}, u32[]{:S(2)}) collective-permute-start(bf16[8,16,256]{2,1,0:T(8,128)(2,1)S(1)} %synthesize.6), channel_id=1, source_target_pairs={{0,4},{4,0},{1,5},{5,1},{2,6},{6,2},{3,7},{7,3},{8,12},{12,8},{9,1... | collective-permute-start | bytes 196616 | tf_op jit(solution)/shard_map/ppermute | solution.py:356
  42.4 2.4 %synthesize.7 = bf16[8,16,256]{2,1,0:T(8,128)(2,1)S(1)} custom-call(bf16[8,16,256]{2,1,0:T(8,128)(2,1)S(1)} %fusion.own_ref, bf16[8,16,256]{2,1,0:T(8,128)(2,1)S(1)} %fusion.1.own_ref.beside_ref, bf16[260,64,128]{2,1,0:T(8,128)(2,1)S(1)} %get-tuple-element.27.even.even_ref, bf16[260,64,128]{2,1,0:T(8,128)(2,1)S(1)} %get-tuple-element.28.odd.odd_ref), custom_call_target="tpu_custom_call" | custom-call | flops 2164260864 | bytes 8781824 | tf_op jit(solution)/shard_map/synthesize/pallas_call | solution.py:330
  44.8 0.6 collective-permute-start.10
  45.4 0.0 collective-permute-done.9
  45.4 1.8 %collective-permute-start.13 = (bf16[8,16,256]{2,1,0:T(8,128)(2,1)S(1)}, bf16[8,16,256]{2,1,0:T(8,128)(2,1)S(1)}, u32[]{:S(2)}, u32[]{:S(2)}) collective-permute-start(bf16[8,16,256]{2,1,0:T(8,128)(2,1)S(1)} %get-tuple-element.40.own_ref), channel_id=1, source_target_pairs={{0,24},{8,0},{16,8},{24,16},{1,25},{9,1},{17,9},{25,17},{2,26},{10... | collective-permute-start | bytes 196616 | tf_op jit(solution)/shard_map/ppermute | solution.py:352
  47.3 1.9 %collective-permute-done.10 = bf16[8,16,256]{2,1,0:T(8,128)(2,1)S(1)} collective-permute-done((bf16[8,16,256]{2,1,0:T(8,128)(2,1)S(1)}, bf16[8,16,256]{2,1,0:T(8,128)(2,1)S(1)}, u32[]{:S(2)}, u32[]{:S(2)}) %collective-permute-start.10) | collective-permute-done | bytes 65568 | tf_op jit(solution)/shard_map/ppermute | solution.py:356
  49.2 2.4 %correlate.6 = bf16[8,16,256]{2,1,0:T(8,128)(2,1)S(1)} custom-call(bf16[8,16,256]{2,1,0:T(8,128)(2,1)S(1)} %get-tuple-element.40.own_ref, bf16[8,16,256]{2,1,0:T(8,128)(2,1)S(1)} %get-tuple-element.38.beside_ref.own_ref, bf16[260,64,128]{2,1,0:T(8,128)(2,1)S(1)} %get-tuple-element.29.even, bf16[260,64,128]{2,1,0:T(8,128)(2,1)S(1)} %get-tuple-element.32.odd), custom_call_target="tpu_custom_call" | custom-call | flops 2164260864 | bytes 8781824 | tf_op jit(solution)/shard_map/correlate/pallas_call | solution.py:330
  51.6 1.3 %collective-permute-start.11 = (bf16[8,16,256]{2,1,0:T(8,128)(2,1)S(1)}, bf16[8,16,256]{2,1,0:T(8,128)(2,1)S(1)}, u32[]{:S(2)}, u32[]{:S(2)}) collective-permute-start(bf16[8,16,256]{2,1,0:T(8,128)(2,1)S(1)} %correlate.6), channel_id=1, source_target_pairs={{0,2},{1,3},{2,0},{3,1},{4,6},{5,7},{6,4},{7,5},{8,10},{9,11},{10,... | collective-permute-start | bytes 196616 | tf_op jit(solution)/shard_map/ppermute | solution.py:356
  52.9 0.0 collective-permute-done.13.beside_ref
  52.9 2.4 %correlate.7 = bf16[8,16,256]{2,1,0:T(8,128)(2,1)S(1)} custom-call(bf16[8,16,256]{2,1,0:T(8,128)(2,1)S(1)} %get-tuple-element.38.beside_ref.own_ref, bf16[8,16,256]{2,1,0:T(8,128)(2,1)S(1)} %collective-permute-done.13.beside_ref, bf16[260,64,128]{2,1,0:T(8,128)(2,1)S(1)} %get-tuple-element.29.even, bf16[260,64,128]{2,1,0:T(8,128)(2,1)S(1)} %get-tuple-element.32.odd), custom_call_target="tpu_custom_call" | custom-call | flops 2164260864 | bytes 8781824 | tf_op jit(solution)/shard_map/correlate/pallas_call | solution.py:330
  55.3 0.8 %collective-permute-start.14 = (bf16[8,16,256]{2,1,0:T(8,128)(2,1)S(1)}, bf16[8,16,256]{2,1,0:T(8,128)(2,1)S(1)}, u32[]{:S(2)}, u32[]{:S(2)}) collective-permute-start(bf16[8,16,256]{2,1,0:T(8,128)(2,1)S(1)} %correlate.7), channel_id=1, source_target_pairs={{0,2},{1,3},{2,0},{3,1},{4,6},{5,7},{6,4},{7,5},{8,10},{9,11},{10,... | collective-permute-start | bytes 196616 | tf_op jit(solution)/shard_map/ppermute | solution.py:356
  56.1 0.0 collective-permute-done.11
  56.1 0.1 collective-permute-start.12
  56.2 3.4 %collective-permute-done.14 = bf16[8,16,256]{2,1,0:T(8,128)(2,1)S(1)} collective-permute-done((bf16[8,16,256]{2,1,0:T(8,128)(2,1)S(1)}, bf16[8,16,256]{2,1,0:T(8,128)(2,1)S(1)}, u32[]{:S(2)}, u32[]{:S(2)}) %collective-permute-start.14) | collective-permute-done | bytes 65568 | tf_op jit(solution)/shard_map/ppermute | solution.py:356
  59.6 0.1 collective-permute-start.15
  59.7 1.0 %from_blocks.3 = f32[64,1024]{1,0:T(8,128)} custom-call(f32[8,16,256]{2,1,0:T(8,128)S(1)} %get-tuple-element.41.low_ref, f32[8,16,256]{2,1,0:T(8,128)S(1)} %get-tuple-element.39.high_ref), custom_call_target="tpu_custom_call" | custom-call | tf_op jit(solution)/shard_map/from_blocks/pallas_call | solution.py:96
  60.7 0.0 collective-permute-done.12
  60.7 0.3 collective-permute-done.15
  61.0 0.2 minimum_subtract_fusion
  61.2 1.0 %from_blocks.2 = f32[64,1024]{1,0:T(8,128)} custom-call(f32[8,16,256]{2,1,0:T(8,128)S(1)} %get-tuple-element.43.low_ref, f32[8,16,256]{2,1,0:T(8,128)S(1)} %get-tuple-element.42.high_ref), custom_call_target="tpu_custom_call" | custom-call | tf_op jit(solution)/shard_map/from_blocks/pallas_call | solution.py:96
  (11 shorter events, 0.2 us)
Async XLA Ops:
  2.1 8.1 %collective-permute-start = (bf16[8,16,256]{2,1,0:T(8,128)(2,1)S(1)}, bf16[8,16,256]{2,1,0:T(8,128)(2,1)S(1)}, u32[]{:S(2)}, u32[]{:S(2)}) collective-permute-start(bf16[8,16,256]{2,1,0:T(8,128)(2,1)S(1)} %convert_element_type.73.own_ref), channel_id=1, source_target_pairs={{0,8},{8,16},{16,24},{24,0},{1,9},{9,17},{17,25},{25,1},{2,10},{10... | collective-permute-start | bytes 196616 | tf_op jit(solution)/shard_map/ppermute | solution.py:352
  12.6 4.6 %collective-permute-start.1 = (bf16[8,16,256]{2,1,0:T(8,128)(2,1)S(1)}, bf16[8,16,256]{2,1,0:T(8,128)(2,1)S(1)}, u32[]{:S(2)}, u32[]{:S(2)}) collective-permute-start(bf16[8,16,256]{2,1,0:T(8,128)(2,1)S(1)} %synthesize.4), channel_id=1, source_target_pairs={{0,4},{4,0},{1,5},{5,1},{2,6},{6,2},{3,7},{7,3},{8,12},{12,8},{9,1... | collective-permute-start | bytes 196616 | tf_op jit(solution)/shard_map/ppermute | solution.py:356
  16.6 5.3 %collective-permute-start.2 = (bf16[8,16,256]{2,1,0:T(8,128)(2,1)S(1)}, bf16[8,16,256]{2,1,0:T(8,128)(2,1)S(1)}, u32[]{:S(2)}, u32[]{:S(2)}) collective-permute-start(bf16[8,16,256]{2,1,0:T(8,128)(2,1)S(1)} %synthesize.5), channel_id=1, source_target_pairs={{0,4},{4,0},{1,5},{5,1},{2,6},{6,2},{3,7},{7,3},{8,12},{12,8},{9,1... | collective-permute-start | bytes 196616 | tf_op jit(solution)/shard_map/ppermute | solution.py:356
  17.2 4.7 %collective-permute-start.3 = (bf16[8,16,256]{2,1,0:T(8,128)(2,1)S(1)}, bf16[8,16,256]{2,1,0:T(8,128)(2,1)S(1)}, u32[]{:S(2)}, u32[]{:S(2)}) collective-permute-start(bf16[8,16,256]{2,1,0:T(8,128)(2,1)S(1)} %subtract_convert_fusion.1.own_ref), channel_id=1, source_target_pairs={{0,24},{8,0},{16,8},{24,16},{1,25},{9,1},{17,9},{25,17},{2,26},{10... | collective-permute-start | bytes 196616 | tf_op jit(solution)/shard_map/ppermute | solution.py:352
  24.3 4.3 %collective-permute-start.5 = (bf16[8,16,256]{2,1,0:T(8,128)(2,1)S(1)}, bf16[8,16,256]{2,1,0:T(8,128)(2,1)S(1)}, u32[]{:S(2)}, u32[]{:S(2)}) collective-permute-start(bf16[8,16,256]{2,1,0:T(8,128)(2,1)S(1)} %correlate.4), channel_id=1, source_target_pairs={{0,2},{1,3},{2,0},{3,1},{4,6},{5,7},{6,4},{7,5},{8,10},{9,11},{10,... | collective-permute-start | bytes 196616 | tf_op jit(solution)/shard_map/ppermute | solution.py:356
  28.7 1.9 %collective-permute-start.6 = (f32[8,16,256]{2,1,0:T(8,128)S(1)}, f32[8,16,256]{2,1,0:T(8,128)S(1)}, u32[]{:S(2)}, u32[]{:S(2)}) collective-permute-start(f32[8,16,256]{2,1,0:T(8,128)S(1)} %convert_add_fusion.3), channel_id=1, source_target_pairs={{0,1},{1,0},{2,3},{3,2},{4,5},{5,4},{6,7},{7,6},{8,9},{9,8},{10,11... | collective-permute-start | bytes 393224 | tf_op jit(solution)/shard_map/ppermute | solution.py:356
  28.8 4.5 %collective-permute-start.4 = (bf16[8,16,256]{2,1,0:T(8,128)(2,1)S(1)}, bf16[8,16,256]{2,1,0:T(8,128)(2,1)S(1)}, u32[]{:S(2)}, u32[]{:S(2)}) collective-permute-start(bf16[8,16,256]{2,1,0:T(8,128)(2,1)S(1)} %correlate.5), channel_id=1, source_target_pairs={{0,2},{1,3},{2,0},{3,1},{4,6},{5,7},{6,4},{7,5},{8,10},{9,11},{10,... | collective-permute-start | bytes 196616 | tf_op jit(solution)/shard_map/ppermute | solution.py:356
  30.6 6.3 %collective-permute-start.7 = (bf16[8,16,256]{2,1,0:T(8,128)(2,1)S(1)}, bf16[8,16,256]{2,1,0:T(8,128)(2,1)S(1)}, u32[]{:S(2)}, u32[]{:S(2)}) collective-permute-start(bf16[8,16,256]{2,1,0:T(8,128)(2,1)S(1)} %fusion.own_ref), channel_id=1, source_target_pairs={{0,8},{8,16},{16,24},{24,0},{1,9},{9,17},{17,25},{25,1},{2,10},{10... | collective-permute-start | bytes 196616 | tf_op jit(solution)/shard_map/ppermute | solution.py:352
  37.0 1.4 %collective-permute-start.8 = (f32[8,16,256]{2,1,0:T(8,128)S(1)}, f32[8,16,256]{2,1,0:T(8,128)S(1)}, u32[]{:S(2)}, u32[]{:S(2)}) collective-permute-start(f32[8,16,256]{2,1,0:T(8,128)S(1)} %convert_add_fusion.2), channel_id=1, source_target_pairs={{0,1},{1,0},{2,3},{3,2},{4,5},{5,4},{6,7},{7,6},{8,9},{9,8},{10,11... | collective-permute-start | bytes 393224 | tf_op jit(solution)/shard_map/ppermute | solution.py:356
  40.9 4.6 %collective-permute-start.9 = (bf16[8,16,256]{2,1,0:T(8,128)(2,1)S(1)}, bf16[8,16,256]{2,1,0:T(8,128)(2,1)S(1)}, u32[]{:S(2)}, u32[]{:S(2)}) collective-permute-start(bf16[8,16,256]{2,1,0:T(8,128)(2,1)S(1)} %synthesize.6), channel_id=1, source_target_pairs={{0,4},{4,0},{1,5},{5,1},{2,6},{6,2},{3,7},{7,3},{8,12},{12,8},{9,1... | collective-permute-start | bytes 196616 | tf_op jit(solution)/shard_map/ppermute | solution.py:356
  44.8 4.3 %collective-permute-start.10 = (bf16[8,16,256]{2,1,0:T(8,128)(2,1)S(1)}, bf16[8,16,256]{2,1,0:T(8,128)(2,1)S(1)}, u32[]{:S(2)}, u32[]{:S(2)}) collective-permute-start(bf16[8,16,256]{2,1,0:T(8,128)(2,1)S(1)} %synthesize.7), channel_id=1, source_target_pairs={{0,4},{4,0},{1,5},{5,1},{2,6},{6,2},{3,7},{7,3},{8,12},{12,8},{9,1... | collective-permute-start | bytes 196616 | tf_op jit(solution)/shard_map/ppermute | solution.py:356
  45.4 7.5 %collective-permute-start.13 = (bf16[8,16,256]{2,1,0:T(8,128)(2,1)S(1)}, bf16[8,16,256]{2,1,0:T(8,128)(2,1)S(1)}, u32[]{:S(2)}, u32[]{:S(2)}) collective-permute-start(bf16[8,16,256]{2,1,0:T(8,128)(2,1)S(1)} %get-tuple-element.40.own_ref), channel_id=1, source_target_pairs={{0,24},{8,0},{16,8},{24,16},{1,25},{9,1},{17,9},{25,17},{2,26},{10... | collective-permute-start | bytes 196616 | tf_op jit(solution)/shard_map/ppermute | solution.py:352
  51.6 4.6 %collective-permute-start.11 = (bf16[8,16,256]{2,1,0:T(8,128)(2,1)S(1)}, bf16[8,16,256]{2,1,0:T(8,128)(2,1)S(1)}, u32[]{:S(2)}, u32[]{:S(2)}) collective-permute-start(bf16[8,16,256]{2,1,0:T(8,128)(2,1)S(1)} %correlate.6), channel_id=1, source_target_pairs={{0,2},{1,3},{2,0},{3,1},{4,6},{5,7},{6,4},{7,5},{8,10},{9,11},{10,... | collective-permute-start | bytes 196616 | tf_op jit(solution)/shard_map/ppermute | solution.py:356
  55.3 4.3 %collective-permute-start.14 = (bf16[8,16,256]{2,1,0:T(8,128)(2,1)S(1)}, bf16[8,16,256]{2,1,0:T(8,128)(2,1)S(1)}, u32[]{:S(2)}, u32[]{:S(2)}) collective-permute-start(bf16[8,16,256]{2,1,0:T(8,128)(2,1)S(1)} %correlate.7), channel_id=1, source_target_pairs={{0,2},{1,3},{2,0},{3,1},{4,6},{5,7},{6,4},{7,5},{8,10},{9,11},{10,... | collective-permute-start | bytes 196616 | tf_op jit(solution)/shard_map/ppermute | solution.py:356
  56.1 4.6 %collective-permute-start.12 = (f32[8,16,256]{2,1,0:T(8,128)S(1)}, f32[8,16,256]{2,1,0:T(8,128)S(1)}, u32[]{:S(2)}, u32[]{:S(2)}) collective-permute-start(f32[8,16,256]{2,1,0:T(8,128)S(1)} %convert_add_fusion.1), channel_id=1, source_target_pairs={{0,1},{1,0},{2,3},{3,2},{4,5},{5,4},{6,7},{7,6},{8,9},{9,8},{10,11... | collective-permute-start | bytes 393224 | tf_op jit(solution)/shard_map/ppermute | solution.py:356
  59.6 1.4 %collective-permute-start.15 = (f32[8,16,256]{2,1,0:T(8,128)S(1)}, f32[8,16,256]{2,1,0:T(8,128)S(1)}, u32[]{:S(2)}, u32[]{:S(2)}) collective-permute-start(f32[8,16,256]{2,1,0:T(8,128)S(1)} %convert_add_fusion), channel_id=1, source_target_pairs={{0,1},{1,0},{2,3},{3,2},{4,5},{5,4},{6,7},{7,6},{8,9},{9,8},{10,11... | collective-permute-start | bytes 393224 | tf_op jit(solution)/shard_map/ppermute | solution.py:356
